TPU v7x, 32 devices: a whole 2x2x4 slice. The times are simulated.
32 devices in a mesh: grp: 4 (over z), enc: 8 (over y, x, core).
Axes of the slice: x: 2, y: 2, z: 4, core: 2. Of those that a mesh axis runs over, the one named last changes fastest.
Arguments:
- history: bfloat16 [384, 128, 1024], P(('grp', 'enc')), may hold values from -6 to 6
- hist_len: int32 [384], P(('grp', 'enc')), may hold values from 0 to 2, as said below
- cand: bfloat16 [16384, 1024], P(('grp', 'enc')), may hold values from -6 to 6
- cand_owner: int32 [16384, 1], P(('grp', 'enc')), may hold values from 0 to 31; in each aligned block of 512 rows (0 to 511, 512 to 1023, ...) at most 24 rows name the same one
- cand_user: int32 [16384], P(('grp', 'enc')), may hold values from 0 to 11
- norm_gain: float32 [1024], replicated, may hold values from 0.1 to 1.9
- w_proj: bfloat16 [1024, 2048], replicated, may hold values from -0.1875 to 0.1875
Outputs:
- kv_cache: bfloat16 [384, 128, 1024], P(('grp', 'enc'))
- cand_out: bfloat16 [16384, 512], P(('grp', 'enc'))
Inputs may be any that keep to these rules, and one draw needn't show every extreme that they name: `hist_len`: blocks of history of each missed user; the first user slot of every device has 2. `cand_owner`: among the 512 candidates of one device no owner device is named more than 24 times.
All inputs are finite; a program needn't handle non-finite values.
Results may differ from a plain program's by a relative error of at most 0.013.
Values may be sent and summed in bfloat16 or wider, within the bound.
No kernel may reach another device: no remote copies, remote signals or barrier semaphores. Data moves between devices by JAX's collectives and lax.ppermute only.
A program may use at most 64 MiB of HBM per device.

v0:
```python
import jax
import jax.numpy as jnp
from jax import lax
from jax.sharding import PartitionSpec as P

HDIM = 128
PIECE = 64


def norm_rows(values):
    center = values - jnp.mean(values, axis=-1, keepdims=True)
    spread = jnp.mean(center * center, axis=-1, keepdims=True)
    return center * lax.rsqrt(spread + 1e-05)


def attend(query, own_k, own_v, uid, keys_leading_layout, values_leading_layout, col_user):
    count = query.shape[0]
    width = query.shape[1]
    heads = width // HDIM
    score_scale = HDIM ** (-0.5)
    query_per_head = query.reshape(count, heads, HDIM)
    scores = (
        jnp.einsum(
            "ofk,fgk->fog", query_per_head, keys_leading_layout, preferred_element_type=jnp.float32
        )
        * score_scale
    )
    belongs = col_user[None, None, :] == uid[None, :, None]
    attention_weight = jnp.where(belongs, jax.nn.silu(scores), 0.0).astype(jnp.bfloat16)
    self_score = jnp.sum(
        query_per_head.astype(jnp.float32) * own_k.reshape(count, heads, HDIM).astype(jnp.float32),
        axis=-1,
    )
    self_weight = jax.nn.silu(self_score * score_scale).astype(jnp.bfloat16)
    reduced_total = jnp.einsum(
        "tlc,tcf->ltf", attention_weight, values_leading_layout, preferred_element_type=jnp.float32
    )
    reduced_total = reduced_total + self_weight.astype(jnp.float32)[:, :, None] * own_v.reshape(
        count, heads, HDIM
    ).astype(jnp.float32)
    return norm_rows(reduced_total.reshape(count, width)).astype(jnp.bfloat16)


def project_rows(rows_in, norm_gain, w_proj):
    normed = (norm_rows(rows_in.astype(jnp.float32)) * norm_gain).astype(jnp.bfloat16)
    return jax.nn.silu(jnp.dot(normed, w_proj, preferred_element_type=jnp.float32)).astype(
        jnp.bfloat16
    )


def body(history, hist_len, cand, cand_owner, cand_user, norm_gain, w_proj):
    rows = history.shape[1]
    width = w_proj.shape[1] // 4
    heads = width // HDIM
    n_enc = lax.axis_size("enc")
    n_grp = lax.axis_size("grp")
    n_dev = n_grp * n_enc
    w_kv = jnp.concatenate([w_proj[:, 3 * width :], w_proj[:, width : 2 * width]], axis=1)
    normed_hist = (norm_rows(history.astype(jnp.float32)) * norm_gain).astype(jnp.bfloat16)
    mixed = jnp.einsum("urd,de->ure", normed_hist, w_kv, preferred_element_type=jnp.float32)
    keyval = jax.nn.silu(mixed).astype(jnp.bfloat16)
    row_ids = jnp.arange(rows, dtype=jnp.int32)
    live_rows = row_ids[None, :] < (hist_len * PIECE)[:, None]
    kv_cache = jnp.where(live_rows[:, :, None], keyval, jnp.zeros((), keyval.dtype))
    user_slots = kv_cache.shape[0]
    flat_kv = kv_cache.reshape(user_slots * rows, 2 * width)
    keys_leading_layout = (
        flat_kv[:, :width].reshape(user_slots * rows, heads, HDIM).transpose(1, 0, 2)
    )
    values_leading_layout = (
        flat_kv[:, width:].reshape(user_slots * rows, heads, HDIM).transpose(1, 0, 2)
    )
    col_user = jnp.arange(user_slots * rows, dtype=jnp.int32) // rows
    count = cand.shape[0]
    cap_cand = max(2, 3 * count // (2 * n_dev))
    owners = cand_owner[:, 0]
    cand_ids = jnp.arange(count, dtype=jnp.int32)
    same_owner = owners[:, None] == owners[None, :]
    cand_rank = jnp.sum(same_owner & (cand_ids[None, :] < cand_ids[:, None]), axis=1)
    dev_ids = jnp.arange(n_dev, dtype=jnp.int32)
    cslot_ids = jnp.arange(cap_cand, dtype=jnp.int32)
    ctable = (owners[None, None, :] == dev_ids[:, None, None]) & (
        cand_rank[None, None, :] == cslot_ids[None, :, None]
    )
    slot_cand = jnp.sum(jnp.where(ctable, cand_ids[None, None, :], 0), axis=2)
    candidate_slot_active = jnp.any(ctable, axis=2)
    slot_uid = jnp.where(candidate_slot_active, cand_user[slot_cand], 0)
    slot_uid = slot_uid.reshape(n_grp, n_enc, cap_cand)
    dest_grp = owners // n_enc
    dest_enc = owners % n_enc
    total_slots = n_dev * cap_cand
    block = 128
    cand_buf = jnp.where(
        candidate_slot_active[:, :, None], cand[slot_cand], jnp.zeros((), cand.dtype)
    )
    cand_buf = cand_buf.reshape(n_grp, n_enc, cap_cand, cand.shape[1])
    arrived, arrived_uid = (
        lax.all_to_all(
            lax.all_to_all(cand_buf, "grp", split_axis=0, concat_axis=0, tiled=True),
            "enc",
            split_axis=1,
            concat_axis=1,
            tiled=True,
        ),
        lax.all_to_all(
            lax.all_to_all(slot_uid, "grp", split_axis=0, concat_axis=0, tiled=True),
            "enc",
            split_axis=1,
            concat_axis=1,
            tiled=True,
        ),
    )

    def per_block(item):
        rows_in, uid = item
        projected = project_rows(rows_in, norm_gain, w_proj)
        normed_attn = attend(
            projected[:, 2 * width : 3 * width],
            projected[:, 3 * width :],
            projected[:, width : 2 * width],
            uid,
            keys_leading_layout,
            values_leading_layout,
            col_user,
        )
        return (normed_attn.astype(jnp.float32) * projected[:, :width].astype(jnp.float32)).astype(
            jnp.bfloat16
        )

    flat_in = arrived.reshape(total_slots // block, block, cand.shape[1])
    flat_uid = arrived_uid.reshape(total_slots // block, block)
    result = lax.map(per_block, (flat_in, flat_uid)).reshape(n_grp, n_enc, cap_cand, width)
    answered = lax.all_to_all(
        lax.all_to_all(result, "grp", split_axis=0, concat_axis=0, tiled=True),
        "enc",
        split_axis=1,
        concat_axis=1,
        tiled=True,
    )
    cand_out = answered[dest_grp, dest_enc, cand_rank]
    return (kv_cache, cand_out)


def solution(mesh):
    placed = (
        P(("grp", "enc"), None, None),
        P(("grp", "enc")),
        P(("grp", "enc"), None),
        P(("grp", "enc"), None),
        P(("grp", "enc")),
        P(),
        P(),
    )
    return jax.shard_map(
        body,
        mesh=mesh,
        in_specs=placed,
        out_specs=(P(("grp", "enc"), None, None), P(("grp", "enc"), None)),
        check_vma=False,
    )
```

profile of v0, /device:TPU:0, one launch (start us, length us, event | category | flops | bytes accessed | tf_op | source)
XLA Modules:
  0.0 201.5 jit_solution(14211140273909198550)
XLA Ops:
  3.8 5.0 %gather_fusion = s32[768]{0:T(1024)S(1)} fusion(s32[512]{0:T(512)S(1)} %copy-done.1, s32[1024]{0:T(1024)S(1)} %pad_clamp_fusion), kind=kCustom, calls=%fused_computation | custom fusion | bytes 9216 | tf_op jit(solution)/shard_map/gather | solution.py:87
  9.6 6.3 %all-to-all-start = ((s32[4,1,192]{2,1,0:T(1,128)}), s32[4,1,192]{2,1,0:T(1,128)S(1)}, u32[]{:S(2)}, u32[]{:S(2)}) async-start(s32[4,1,192]{2,1,0:T(1,128)} %reshape.267), calls=%async_computation | async-start | bytes 8192 | tf_op jit(solution)/shard_map/all_to_all | solution.py:106
  15.9 2.8 %gather_fusion.1 = bf16[768,1024]{1,0:T(8,128)(2,1)S(1)} fusion(bf16[512,1024]{1,0:T(8,128)(2,1)S(1)} %copy-done, s32[1024]{0:T(1024)S(1)} %pad_clamp_fusion), kind=kCustom, calls=%fused_computation.1 | custom fusion | bytes 3148800 | tf_op jit(solution)/shard_map/gather | solution.py:94
  21.5 3.7 %all-to-all-start.2 = ((bf16[4,8,24,1024]{3,2,1,0:T(8,128)(2,1)}), bf16[4,8,24,1024]{3,2,1,0:T(8,128)(2,1)S(1)}, u32[]{:S(2)}, u32[]{:S(2)}) async-start(bf16[4,8,24,1024]{3,2,1,0:T(8,128)(2,1)} %broadcast_select_fusion), calls=%async_computation.2 | async-start | bytes 3145728 | tf_op jit(solution)/shard_map/all_to_all | solution.py:99
  25.2 2.5 %convert_reduce_fusion.1 = f32[12,128]{1,0:T(8,128)S(1)} fusion(bf16[12,128,1024]{2,1,0:T(8,128)(2,1)} %param.9), kind=kLoop, calls=%fused_computation.56 | loop fusion | flops 3144192 | bytes 3151872 | tf_op jit(solution)/shard_map/reduce_sum | solution.py:11
  29.0 3.0 %fusion.65 = (bf16[1024,512]{1,0:T(8,128)(2,1)}, bf16[1024,512]{1,0:T(8,128)(2,1)}) fusion(bf16[1024,2048]{1,0:T(8,128)(2,1)} %param.15), kind=kLoop, calls=%fused_computation.106 | loop fusion | bytes 4194304 | tf_op jit(solution)/shard_map/slice | solution.py:58
  33.9 27.7 %all-to-all-done.2 = bf16[4,8,24,1024]{3,2,1,0:T(8,128)(2,1)S(1)} async-done(((bf16[4,8,24,1024]{3,2,1,0:T(8,128)(2,1)}), bf16[4,8,24,1024]{3,2,1,0:T(8,128)(2,1)S(1)}, u32[]{:S(2)}, u32[]{:S(2)}) %all-to-all-start.2) | async-done | bytes 1572896 | tf_op jit(solution)/shard_map/all_to_all | solution.py:99
  61.6 3.7 %all-to-all-start.1 = ((s32[4,8,24]{2,0,1:T(4,128)}), s32[4,8,24]{2,0,1:T(4,128)S(1)}, u32[]{:S(2)}, u32[]{:S(2)}) async-start(s32[4,8,24]{2,0,1:T(4,128)} %copy.72), calls=%async_computation.1 | async-start | bytes 32768 | tf_op jit(solution)/shard_map/all_to_all | solution.py:105
  66.7 3.4 %all-to-all-done.1 = s32[4,8,24]{2,0,1:T(4,128)S(1)} async-done(((s32[4,8,24]{2,0,1:T(4,128)}), s32[4,8,24]{2,0,1:T(4,128)S(1)}, u32[]{:S(2)}, u32[]{:S(2)}) %all-to-all-start.1) | async-done | bytes 3104 | tf_op jit(solution)/shard_map/all_to_all | solution.py:105
  70.0 3.8 %all-to-all-start.3 = ((bf16[4,8,24,1024]{3,2,0,1:T(8,128)(2,1)}), bf16[4,8,24,1024]{3,2,0,1:T(8,128)(2,1)S(1)}, u32[]{:S(2)}, u32[]{:S(2)}) async-start(bf16[4,8,24,1024]{3,2,0,1:T(8,128)(2,1)} %copy.74), calls=%async_computation.3 | async-start | bytes 3145728 | tf_op jit(solution)/shard_map/all_to_all | solution.py:98
  73.8 6.6 %fusion.45 = bf16[12,128,1024]{2,1,0:T(8,128)(2,1)S(1)} fusion(pred[12,128]{1,0:T(8,128)(4,1)S(1)} %iota_compare_fusion.3, bf16[12,128,1024]{2,1,0:T(8,128)(2,1)} %param.9, f32[1024]{0:T(1024)S(1)} %copy-done.5, f32[12,128]{1,0:T(8,128)S(1)} %add_rsqrt_fusion.2, f32[12,128]{1,0:T(8,128)S(1)} %broadcast_multiply_fusion.2, ...), kind=kOutput, calls=%fused_computation.67 | convolution fusion | flops 3242721280 | bytes 8406528 | tf_op jit(solution)/shard_map/urd,de->ure/dot_general | solution.py:60
  83.1 2.6 %copy.83 = bf16[1536,512]{0,1:T(8,128)(2,1)} copy(bf16[1536,512]{1,0:T(8,128)(2,1)} %get-tuple-element.141) | data formatting | bytes 3145728
  85.7 2.6 %copy.78 = bf16[4,1536,128]{2,1,0:T(8,128)(2,1)} copy(bf16[4,1536,128]{1,2,0:T(8,128)(2,1)} %bitcast.85) | data formatting | bytes 3145728
  88.3 2.6 %copy.77 = bf16[1536,512]{0,1:T(8,128)(2,1)} copy(bf16[1536,512]{1,0:T(8,128)(2,1)} %get-tuple-element.140) | data formatting | bytes 3145728 | tf_op jit(solution)/shard_map/slice | solution.py:71
  91.0 3.6 %all-to-all-done.3 = bf16[4,8,24,1024]{3,2,0,1:T(8,128)(2,1)S(1)} async-done(((bf16[4,8,24,1024]{3,2,0,1:T(8,128)(2,1)}), bf16[4,8,24,1024]{3,2,0,1:T(8,128)(2,1)S(1)}, u32[]{:S(2)}, u32[]{:S(2)}) %all-to-all-start.3) | async-done | bytes 1572896 | tf_op jit(solution)/shard_map/all_to_all | solution.py:98
  95.9 61.3 %while.11 = (s32[]{:T(128)}, bf16[6,128,512]{2,1,0:T(8,128)(2,1)S(1)}, s32[6,128]{1,0:T(8,128)S(1)}, bf16[6,128,1024]{2,1,0:T(8,128)(2,1)}, f32[1024]{0:T(1024)S...) while((s32[]{:T(128)}, ...), condition=%wide.region_11.12_spmd.clone, body=%wide.region_5.11_spmd.clone.sunk | while | flops 949173504 | bytes 13933677 | solution.py:132
  98.1 3.2 %multiply_convert_fusion.5 = bf16[128,2048]{1,0:T(8,128)(2,1)S(1)} fusion(bf16[1024,2048]{1,0:T(8,128)(2,1)} %get-tuple-element.226, f32[1024]{0:T(1024)S(1)} %get-tuple-element.225, f32[128]{0:T(128)S(1)} %add_rsqrt_fusion.5, f32[128]{0:T(128)S(1)} %broadcast_multiply_fusion.6, bf16[6,128,1024]{2,1,0:T(8,128)(2,1)} %get-tuple-element.224, ...), kind=kOutput, calls=%fused_computation.9.clone.1 | convolution fusion | flops 538836992 | bytes 4986368 | tf_op jit(solution)/shard_map/while/body/eval_jaxpr/dot_general | solution.py:46
  102.2 3.5 %fusion.90 = (f32[128]{0:T(128)S(1)}, f32[128,4,128]{0,2,1:T(8,128)S(1)}) fusion(f32[128,4,128]{0,2,1:T(8,128)S(1)} %bitcast.84, f32[128,4]{0,1:T(4,128)S(1)} %fusion.88, bf16[4,1536,128]{1,2,0:T(8,128)(2,1)} %get-tuple-element.228, bf16[4,1536,128]{2,1,0:T(8,128)(2,1)} %get-tuple-element.227, pred[128,1536]{1,0:T(8,128)(4,1)S(1)} %broadcast_compare_fusion.2, ...), kind=kOutput, calls=%fused_computation.105.clone.1 | convolution fusion | flops 408354688 | bytes 4000256 | tf_op jit(solution)/shard_map/while/body/eval_jaxpr/tlc,tcf->ltf/dot_general | solution.py:35
  108.4 3.1 %multiply_convert_fusion.5 = bf16[128,2048]{1,0:T(8,128)(2,1)S(1)} fusion(bf16[1024,2048]{1,0:T(8,128)(2,1)} %get-tuple-element.226, f32[1024]{0:T(1024)S(1)} %get-tuple-element.225, f32[128]{0:T(128)S(1)} %add_rsqrt_fusion.5, f32[128]{0:T(128)S(1)} %broadcast_multiply_fusion.6, bf16[6,128,1024]{2,1,0:T(8,128)(2,1)} %get-tuple-element.224, ...), kind=kOutput, calls=%fused_computation.9.clone.1 | convolution fusion | flops 538836992 | bytes 4986368 | tf_op jit(solution)/shard_map/while/body/eval_jaxpr/dot_general | solution.py:46
  112.4 3.5 %fusion.90 = (f32[128]{0:T(128)S(1)}, f32[128,4,128]{0,2,1:T(8,128)S(1)}) fusion(f32[128,4,128]{0,2,1:T(8,128)S(1)} %bitcast.84, f32[128,4]{0,1:T(4,128)S(1)} %fusion.88, bf16[4,1536,128]{1,2,0:T(8,128)(2,1)} %get-tuple-element.228, bf16[4,1536,128]{2,1,0:T(8,128)(2,1)} %get-tuple-element.227, pred[128,1536]{1,0:T(8,128)(4,1)S(1)} %broadcast_compare_fusion.2, ...), kind=kOutput, calls=%fused_computation.105.clone.1 | convolution fusion | flops 408354688 | bytes 4000256 | tf_op jit(solution)/shard_map/while/body/eval_jaxpr/tlc,tcf->ltf/dot_general | solution.py:35
  118.6 3.1 %multiply_convert_fusion.5 = bf16[128,2048]{1,0:T(8,128)(2,1)S(1)} fusion(bf16[1024,2048]{1,0:T(8,128)(2,1)} %get-tuple-element.226, f32[1024]{0:T(1024)S(1)} %get-tuple-element.225, f32[128]{0:T(128)S(1)} %add_rsqrt_fusion.5, f32[128]{0:T(128)S(1)} %broadcast_multiply_fusion.6, bf16[6,128,1024]{2,1,0:T(8,128)(2,1)} %get-tuple-element.224, ...), kind=kOutput, calls=%fused_computation.9.clone.1 | convolution fusion | flops 538836992 | bytes 4986368 | tf_op jit(solution)/shard_map/while/body/eval_jaxpr/dot_general | solution.py:46
  122.6 3.5 %fusion.90 = (f32[128]{0:T(128)S(1)}, f32[128,4,128]{0,2,1:T(8,128)S(1)}) fusion(f32[128,4,128]{0,2,1:T(8,128)S(1)} %bitcast.84, f32[128,4]{0,1:T(4,128)S(1)} %fusion.88, bf16[4,1536,128]{1,2,0:T(8,128)(2,1)} %get-tuple-element.228, bf16[4,1536,128]{2,1,0:T(8,128)(2,1)} %get-tuple-element.227, pred[128,1536]{1,0:T(8,128)(4,1)S(1)} %broadcast_compare_fusion.2, ...), kind=kOutput, calls=%fused_computation.105.clone.1 | convolution fusion | flops 408354688 | bytes 4000256 | tf_op jit(solution)/shard_map/while/body/eval_jaxpr/tlc,tcf->ltf/dot_general | solution.py:35
  128.8 3.1 %multiply_convert_fusion.5 = bf16[128,2048]{1,0:T(8,128)(2,1)S(1)} fusion(bf16[1024,2048]{1,0:T(8,128)(2,1)} %get-tuple-element.226, f32[1024]{0:T(1024)S(1)} %get-tuple-element.225, f32[128]{0:T(128)S(1)} %add_rsqrt_fusion.5, f32[128]{0:T(128)S(1)} %broadcast_multiply_fusion.6, bf16[6,128,1024]{2,1,0:T(8,128)(2,1)} %get-tuple-element.224, ...), kind=kOutput, calls=%fused_computation.9.clone.1 | convolution fusion | flops 538836992 | bytes 4986368 | tf_op jit(solution)/shard_map/while/body/eval_jaxpr/dot_general | solution.py:46
  132.8 3.5 %fusion.90 = (f32[128]{0:T(128)S(1)}, f32[128,4,128]{0,2,1:T(8,128)S(1)}) fusion(f32[128,4,128]{0,2,1:T(8,128)S(1)} %bitcast.84, f32[128,4]{0,1:T(4,128)S(1)} %fusion.88, bf16[4,1536,128]{1,2,0:T(8,128)(2,1)} %get-tuple-element.228, bf16[4,1536,128]{2,1,0:T(8,128)(2,1)} %get-tuple-element.227, pred[128,1536]{1,0:T(8,128)(4,1)S(1)} %broadcast_compare_fusion.2, ...), kind=kOutput, calls=%fused_computation.105.clone.1 | convolution fusion | flops 408354688 | bytes 4000256 | tf_op jit(solution)/shard_map/while/body/eval_jaxpr/tlc,tcf->ltf/dot_general | solution.py:35
  139.0 3.1 %multiply_convert_fusion.5 = bf16[128,2048]{1,0:T(8,128)(2,1)S(1)} fusion(bf16[1024,2048]{1,0:T(8,128)(2,1)} %get-tuple-element.226, f32[1024]{0:T(1024)S(1)} %get-tuple-element.225, f32[128]{0:T(128)S(1)} %add_rsqrt_fusion.5, f32[128]{0:T(128)S(1)} %broadcast_multiply_fusion.6, bf16[6,128,1024]{2,1,0:T(8,128)(2,1)} %get-tuple-element.224, ...), kind=kOutput, calls=%fused_computation.9.clone.1 | convolution fusion | flops 538836992 | bytes 4986368 | tf_op jit(solution)/shard_map/while/body/eval_jaxpr/dot_general | solution.py:46
  143.1 3.5 %fusion.90 = (f32[128]{0:T(128)S(1)}, f32[128,4,128]{0,2,1:T(8,128)S(1)}) fusion(f32[128,4,128]{0,2,1:T(8,128)S(1)} %bitcast.84, f32[128,4]{0,1:T(4,128)S(1)} %fusion.88, bf16[4,1536,128]{1,2,0:T(8,128)(2,1)} %get-tuple-element.228, bf16[4,1536,128]{2,1,0:T(8,128)(2,1)} %get-tuple-element.227, pred[128,1536]{1,0:T(8,128)(4,1)S(1)} %broadcast_compare_fusion.2, ...), kind=kOutput, calls=%fused_computation.105.clone.1 | convolution fusion | flops 408354688 | bytes 4000256 | tf_op jit(solution)/shard_map/while/body/eval_jaxpr/tlc,tcf->ltf/dot_general | solution.py:35
  149.3 3.1 %multiply_convert_fusion.5 = bf16[128,2048]{1,0:T(8,128)(2,1)S(1)} fusion(bf16[1024,2048]{1,0:T(8,128)(2,1)} %get-tuple-element.226, f32[1024]{0:T(1024)S(1)} %get-tuple-element.225, f32[128]{0:T(128)S(1)} %add_rsqrt_fusion.5, f32[128]{0:T(128)S(1)} %broadcast_multiply_fusion.6, bf16[6,128,1024]{2,1,0:T(8,128)(2,1)} %get-tuple-element.224, ...), kind=kOutput, calls=%fused_computation.9.clone.1 | convolution fusion | flops 538836992 | bytes 4986368 | tf_op jit(solution)/shard_map/while/body/eval_jaxpr/dot_general | solution.py:46
  153.3 3.5 %fusion.90 = (f32[128]{0:T(128)S(1)}, f32[128,4,128]{0,2,1:T(8,128)S(1)}) fusion(f32[128,4,128]{0,2,1:T(8,128)S(1)} %bitcast.84, f32[128,4]{0,1:T(4,128)S(1)} %fusion.88, bf16[4,1536,128]{1,2,0:T(8,128)(2,1)} %get-tuple-element.228, bf16[4,1536,128]{2,1,0:T(8,128)(2,1)} %get-tuple-element.227, pred[128,1536]{1,0:T(8,128)(4,1)S(1)} %broadcast_compare_fusion.2, ...), kind=kOutput, calls=%fused_computation.105.clone.1 | convolution fusion | flops 408354688 | bytes 4000256 | tf_op jit(solution)/shard_map/while/body/eval_jaxpr/tlc,tcf->ltf/dot_general | solution.py:35
  157.2 19.8 %all_to_all.30 = bf16[4,8,24,512]{3,2,1,0:T(8,128)(2,1)S(1)} all-to-all(bf16[4,8,24,512]{3,2,1,0:T(8,128)(2,1)S(1)} %bitcast.89), channel_id=1, replica_groups=mesh['grp'=4,'enc'=8] {'grp'}, dimensions={0} | all-to-all | bytes 1572864 | tf_op jit(solution)/shard_map/all_to_all | solution.py:134
  178.0 5.0 %all-to-all-start.5 = ((bf16[4,8,24,512]{3,2,0,1:T(8,128)(2,1)}), bf16[4,8,24,512]{3,2,0,1:T(8,128)(2,1)S(1)}, u32[]{:S(2)}, u32[]{:S(2)}) async-start(bf16[4,8,24,512]{3,2,0,1:T(8,128)(2,1)} %copy.79), calls=%async_computation.5 | async-start | bytes 1572864 | tf_op jit(solution)/shard_map/all_to_all | solution.py:133
  183.0 12.6 %all-to-all-done.5 = bf16[4,8,24,512]{3,2,0,1:T(8,128)(2,1)S(1)} async-done(((bf16[4,8,24,512]{3,2,0,1:T(8,128)(2,1)}), bf16[4,8,24,512]{3,2,0,1:T(8,128)(2,1)S(1)}, u32[]{:S(2)}, u32[]{:S(2)}) %all-to-all-start.5) | async-done | bytes 786464 | tf_op jit(solution)/shard_map/all_to_all | solution.py:133
  195.7 5.8 %gather_fusion.2 = bf16[512,512]{1,0:T(8,128)(2,1)} fusion(bf16[4,8,24,512]{3,2,1,0:T(8,128)(2,1)S(1)} %copy.80, s32[512]{0:T(512)S(1)} %bitcast.82), kind=kCustom, calls=%fused_computation.2 | custom fusion | bytes 1054720 | tf_op jit(solution)/shard_map/gather | solution.py:140
  (159 shorter events, 36.8 us)
Async XLA Ops:
  0.6 15.3 %copy-start = (bf16[512,1024]{1,0:T(8,128)(2,1)S(1)}, bf16[512,1024]{1,0:T(8,128)(2,1)}, u32[]{:S(2)}) copy-start(bf16[512,1024]{1,0:T(8,128)(2,1)} %param.11) | copy-start | bytes 3145732
  0.6 3.2 %copy-start.1 = (s32[512]{0:T(512)S(1)}, s32[512]{0:T(512)}, u32[]{:S(2)}) copy-start(s32[512]{0:T(512)} %param.13) | copy-start | bytes 6148
  9.6 11.9 %all-to-all-start = ((s32[4,1,192]{2,1,0:T(1,128)}), s32[4,1,192]{2,1,0:T(1,128)S(1)}, u32[]{:S(2)}, u32[]{:S(2)}) async-start(s32[4,1,192]{2,1,0:T(1,128)} %reshape.267), calls=%async_computation | async-start | bytes 8192 | tf_op jit(solution)/shard_map/all_to_all | solution.py:106
  18.7 6.4 %copy-start.6 = (s32[12]{0:T(128)S(1)}, s32[12]{0:T(128)}, u32[]{:S(2)}) copy-start(s32[12]{0:T(128)} %param.10) | copy-start | bytes 148
  21.5 40.1 %all-to-all-start.2 = ((bf16[4,8,24,1024]{3,2,1,0:T(8,128)(2,1)}), bf16[4,8,24,1024]{3,2,1,0:T(8,128)(2,1)S(1)}, u32[]{:S(2)}, u32[]{:S(2)}) async-start(bf16[4,8,24,1024]{3,2,1,0:T(8,128)(2,1)} %broadcast_select_fusion), calls=%async_computation.2 | async-start | bytes 3145728 | tf_op jit(solution)/shard_map/all_to_all | solution.py:99
  25.2 2.8 %copy-start.2 = (bf16[12,128,1024]{2,1,0:T(8,128)(2,1)S(1)}, bf16[12,128,1024]{2,1,0:T(8,128)(2,1)}, u32[]{:S(2)}) copy-start(bf16[12,128,1024]{2,1,0:T(8,128)(2,1)} %param.9) | copy-start | bytes 9437188
  61.6 8.5 %all-to-all-start.1 = ((s32[4,8,24]{2,0,1:T(4,128)}), s32[4,8,24]{2,0,1:T(4,128)S(1)}, u32[]{:S(2)}, u32[]{:S(2)}) async-start(s32[4,8,24]{2,0,1:T(4,128)} %copy.72), calls=%async_computation.1 | async-start | bytes 32768 | tf_op jit(solution)/shard_map/all_to_all | solution.py:105
  65.4 8.5 %copy-start.5 = (f32[1024]{0:T(1024)S(1)}, f32[1024]{0:T(1024)}, u32[]{:S(2)}) copy-start(f32[1024]{0:T(1024)} %param.14) | copy-start | bytes 12292
  70.0 24.5 %all-to-all-start.3 = ((bf16[4,8,24,1024]{3,2,0,1:T(8,128)(2,1)}), bf16[4,8,24,1024]{3,2,0,1:T(8,128)(2,1)S(1)}, u32[]{:S(2)}, u32[]{:S(2)}) async-start(bf16[4,8,24,1024]{3,2,0,1:T(8,128)(2,1)} %copy.74), calls=%async_computation.3 | async-start | bytes 3145728 | tf_op jit(solution)/shard_map/all_to_all | solution.py:98
  80.5 2.7 %copy-start.3 = (bf16[12,128,1024]{2,1,0:T(8,128)(2,1)}, bf16[12,128,1024]{2,1,0:T(8,128)(2,1)S(1)}, u32[]{:S(2)}) copy-start(bf16[12,128,1024]{2,1,0:T(8,128)(2,1)S(1)} %fusion.45) | copy-start | bytes 9437188
  157.2 25.8 %copy-start.4 = (s32[512,1]{0,1:T(1,128)S(1)}, s32[512,1]{0,1:T(1,128)}, u32[]{:S(2)}) copy-start(s32[512,1]{0,1:T(1,128)} %param.12) | copy-start | bytes 6148
  178.0 17.6 %all-to-all-start.5 = ((bf16[4,8,24,512]{3,2,0,1:T(8,128)(2,1)}), bf16[4,8,24,512]{3,2,0,1:T(8,128)(2,1)S(1)}, u32[]{:S(2)}, u32[]{:S(2)}) async-start(bf16[4,8,24,512]{3,2,0,1:T(8,128)(2,1)} %copy.79), calls=%async_computation.5 | async-start | bytes 1572864 | tf_op jit(solution)/shard_map/all_to_all | solution.py:133
where the time goes:
time: 203 us; the launch traced here: 201 us
  waiting for transfers between devices  48.6 us (24%)
  matrix products  46.8 us (23%)
  local copies, waits for them, and re-layouts  36 us (18%)
  other arithmetic  26.3 us (13%)
  starting transfers between devices  22.4 us (11%)
  blocking collectives  19.8 us (10%)
    all_to_all x1, waiting for transfers between devices, body(): lax.all_to_all(cand_buf, 'grp', split_axis=0, concat_axis=0, tiled=True)  27.7 us
    dot_general x6, matrix products, attend(): jnp.einsum('tlc,tcf->ltf', attention_weight, values_leading_layout, prefe...  21.3 us
    all_to_all x1, blocking collectives, body(): lax.all_to_all(result, 'grp', split_axis=0, concat_axis=0, tiled=True)  19.8 us
    dot_general x6, matrix products, project_rows(): jnp.dot(normed, w_proj, preferred_element_type=jnp.float32)  18.9 us
    all_to_all x1, waiting for transfers between devices, body(): lax.all_to_all(lax.all_to_all(result, 'grp', split_axis=0, concat_axis=0,...  12.6 us
    reduce_sum x7, other arithmetic, norm_rows(): center = values - jnp.mean(values, axis=-1, keepdims=True)  8.93 us
    reduce_sum x13, other arithmetic, norm_rows(): spread = jnp.mean(center * center, axis=-1, keepdims=True)  8.5 us
    unnamed x18, local copies, waits for them, and re-layouts  6.85 us
  transfers between devices with their start and end apart: 5, of which 5 were waited for; matrix products, arithmetic and copies ran while one was open for 15% of the time, Pallas kernels for 0%

commit v1 on v0

v1 whole, which is shorter than its diff:
```python
import functools

import jax
import jax.numpy as jnp
from jax import lax
from jax.experimental import pallas as pl
from jax.experimental.pallas import tpu as pltpu
from jax.sharding import PartitionSpec as P

HDIM = 128
PIECE = 64
CODE = 64
F32 = jnp.float32
BF16 = jnp.bfloat16
AXES = ("grp", "enc")
NT = (((1,), (1,)), ((), ()))


def silu(x):
    half = 0.5 * x
    return half + half * jnp.tanh(half)


def norm_rows(values):
    center = values - jnp.mean(values, axis=-1, keepdims=True)
    spread = jnp.mean(center * center, axis=-1, keepdims=True)
    return center * lax.rsqrt(spread + 1e-05)


def mm(a, b):
    return jnp.dot(a, b, preferred_element_type=F32)


def one_hot(hit):
    return jnp.where(hit, 1.0, 0.0).astype(BF16)


def iota(shape, dim):
    return lax.broadcasted_iota(jnp.int32, shape, dim)


def strict_upper(n):
    return one_hot(iota((n, n), 0) < iota((n, n), 1))


def dispatch_kernel(n_dev, cap, cand_ref, gain_ref, wq_ref, owner_ref, normed_ref, q_ref, slot_ref, out_ref):
    count = cand_ref.shape[0]
    step = 128
    gain = gain_ref[...]
    for r in range(0, count, step):
        rows = slice(r, r + step)
        normed = (norm_rows(cand_ref[rows, :].astype(F32)) * gain).astype(BF16)
        normed_ref[rows, :] = normed
        q_ref[rows, :] = silu(mm(normed, wq_ref[...])).astype(BF16)
    owner = owner_ref[...]
    named = iota((n_dev, count), 0) == owner
    before = mm(one_hot(named), strict_upper(count))
    rank = jnp.sum(jnp.where(named, before, 0.0), axis=0, keepdims=True)
    slot = owner * cap + rank.astype(jnp.int32)
    slot_ref[...] = slot
    total = n_dev * cap
    pick = one_hot(iota((total, count), 0) == slot)
    out_ref[...] = mm(pick, q_ref[...]).astype(BF16)


def encode_kernel(len_ref, hist_ref, gain_ref, wv_ref, wk_ref, out_ref):
    users, rows, dim = hist_ref.shape
    width = wk_ref.shape[1]
    first = pl.program_id(0) * users
    x = hist_ref[...].reshape(users * rows, dim).astype(F32)
    normed = (norm_rows(x) * gain_ref[...]).astype(BF16)
    keys = silu(mm(normed, wk_ref[...]))
    values = silu(mm(normed, wv_ref[...]))
    row_ids = iota((rows, width), 0)
    for u in range(users):
        live = row_ids < len_ref[first + u] * PIECE
        part = slice(u * rows, (u + 1) * rows)
        out_ref[u, :, :width] = jnp.where(live, keys[part], 0.0).astype(BF16)
        out_ref[u, :, width:] = jnp.where(live, values[part], 0.0).astype(BF16)


def own_kernel(normed_ref, q_ref, slot_ref, wu_ref, wv_ref, wk_ref, u_ref, self_ref, column_ref):
    count, width = q_ref.shape
    step = 128
    for r in range(0, count, step):
        rows = slice(r, r + step)
        normed = normed_ref[rows, :]
        u_ref[rows, :] = silu(mm(normed, wu_ref[...])).astype(BF16)
        own_v = silu(mm(normed, wv_ref[...])).astype(BF16).astype(F32)
        own_k = silu(mm(normed, wk_ref[...])).astype(BF16).astype(F32)
        prod = q_ref[rows, :].astype(F32) * own_k
        for h in range(width // HDIM):
            cols = slice(h * HDIM, (h + 1) * HDIM)
            score = jnp.sum(prod[:, cols], axis=-1, keepdims=True) * HDIM ** (-0.5)
            weight = silu(score).astype(BF16).astype(F32)
            self_ref[rows, cols] = weight * own_v[:, cols]
    spread = jnp.broadcast_to(slot_ref[...].astype(F32), (128, count))
    column_ref[...] = spread.T.astype(jnp.int32)


def users_kernel(cap, me_ref, code_ref, out_ref):
    n_dev, count = code_ref.shape
    total = n_dev * cap
    user = code_ref[...] - me_ref[0] * CODE
    mine = (user >= 0) & (user < CODE)
    rank = mm(one_hot(mine), strict_upper(count)).astype(jnp.int32)
    rank = jnp.where(mine, rank, -1)
    user = user.astype(F32)
    lane = iota((n_dev, 128), 1)
    table = jnp.zeros((n_dev, 128), F32)
    for k in range(cap):
        found = jnp.sum(jnp.where(rank == k, user, 0.0), axis=1, keepdims=True)
        table = jnp.where(lane == k, found, table)
    source = iota((total, n_dev), 0) - iota((total, n_dev), 1) * cap
    spread = mm(one_hot((source >= 0) & (source < cap)), table.astype(BF16))
    place = lax.rem(iota((total, 128), 0), cap)
    own = jnp.where(place == iota((total, 128), 1), spread, 0.0)
    out_ref[...] = jnp.broadcast_to(jnp.sum(own, axis=1, keepdims=True), (total, 128))


def attend_kernel(uid_ref, q_ref, k_ref, v_ref, out_ref, mask_ref, odd_ref):
    rows = k_ref.shape[0]
    pairs = rows // 256

    @pl.when(pl.program_id(0) == 0)
    def _():
        uid = uid_ref[...]
        odd = jnp.zeros_like(uid)
        for p in range(pairs):
            low, high = uid == 2.0 * p, uid == 2.0 * p + 1.0
            mask_ref[:, p * 128:(p + 1) * 128] = one_hot(low | high)
            odd = jnp.where(high, 1.0, odd)
        odd_ref[...] = odd

    odd = odd_ref[...] > 0.5

    def spread(x):
        return jnp.concatenate([x * mask_ref[:, p * 128:(p + 1) * 128] for p in range(pairs)], axis=1)

    def chosen(x):
        return jnp.where(odd, x[:, 128:], x[:, :128])

    keys = jnp.concatenate([k_ref[p * 256:(p + 1) * 256, :] for p in range(pairs)], axis=1)
    scores = chosen(lax.dot_general(spread(q_ref[...]), keys, NT, preferred_element_type=F32))
    weight = silu(scores * HDIM ** (-0.5)).astype(BF16)
    values = jnp.concatenate(
        [
            jnp.concatenate([v_ref[p * 256:p * 256 + 128, :], v_ref[p * 256 + 128:(p + 1) * 256, :]], axis=1)
            for p in range(pairs)
        ],
        axis=0,
    )
    out_ref[...] = chosen(mm(spread(weight), values)).astype(BF16)


def answer_kernel(back_ref, column_ref, self_ref, u_ref, out_ref):
    total = back_ref.shape[0]
    count = u_ref.shape[0]
    step = 128
    for r in range(0, count, step):
        rows = slice(r, r + step)
        slot = column_ref[rows, 0:1]
        pick = one_hot(iota((step, total), 1) == slot)
        attended = mm(pick, back_ref[...]) + self_ref[rows, :]
        normed = norm_rows(attended).astype(BF16).astype(F32)
        out_ref[rows, :] = (normed * u_ref[rows, :].astype(F32)).astype(BF16)


def params(**more):
    return pltpu.CompilerParams(vmem_limit_bytes=40 * 1024 * 1024, **more)


def whole(shape):
    return pl.BlockSpec(shape, lambda *_: (0,) * len(shape))


def column(shape, index):
    return pl.BlockSpec(shape, lambda *_: (0, index))


def cost(flops, size):
    return pl.CostEstimate(flops=flops, bytes_accessed=size, transcendentals=0)


def body(history, hist_len, cand, cand_owner, cand_user, norm_gain, w_proj):
    users, rows, dim = history.shape
    width = w_proj.shape[1] // 4
    heads = width // HDIM
    count = cand.shape[0]
    n_enc = lax.axis_size("enc")
    n_dev = lax.axis_size("grp") * n_enc
    cap = max(2, 3 * count // (2 * n_dev))
    total = n_dev * cap
    gain = norm_gain.reshape(1, dim)
    owner = cand_owner.reshape(1, count)
    me = (lax.axis_index("grp") * n_enc + lax.axis_index("enc")).astype(jnp.int32).reshape(1)
    shape = jax.ShapeDtypeStruct

    codes = lax.all_gather(cand_owner[:, 0] * CODE + cand_user, AXES, axis=0, tiled=False)

    normed, q, slot, outgoing = pl.pallas_call(
        functools.partial(dispatch_kernel, n_dev, cap),
        grid=(1,),
        in_specs=[whole((count, dim)), whole((1, dim)), column((dim, width), 2), whole((1, count))],
        out_specs=[whole((count, dim)), whole((count, width)), whole((1, count)), whole((total, width))],
        out_shape=[
            shape((count, dim), BF16),
            shape((count, width), BF16),
            shape((1, count), jnp.int32),
            shape((total, width), BF16),
        ],
        compiler_params=params(),
        cost_estimate=cost(2 * count * width * (dim + total), 4 << 20),
        name="dispatch",
    )(cand, gain, w_proj, owner)

    arrived = lax.all_to_all(
        outgoing.reshape(n_dev, cap, width), AXES, split_axis=0, concat_axis=0, tiled=True
    ).reshape(total, width)

    step = 3
    kv_cache = pl.pallas_call(
        encode_kernel,
        grid=(users // step,),
        in_specs=[
            pl.BlockSpec(memory_space=pltpu.SMEM),
            pl.BlockSpec((step, rows, dim), lambda i: (i, 0, 0)),
            whole((1, dim)),
            column((dim, width), 1),
            column((dim, width), 3),
        ],
        out_specs=pl.BlockSpec((step, rows, 2 * width), lambda i: (i, 0, 0)),
        out_shape=shape((users, rows, 2 * width), BF16),
        compiler_params=params(),
        cost_estimate=cost(2 * users * rows * dim * 2 * width, 8 << 20),
        name="encode",
    )(hist_len, history, gain, w_proj, w_proj)

    gate, own, slots = pl.pallas_call(
        own_kernel,
        grid=(1,),
        in_specs=[
            whole((count, dim)),
            whole((count, width)),
            whole((1, count)),
            column((dim, width), 0),
            column((dim, width), 1),
            column((dim, width), 3),
        ],
        out_specs=[whole((count, width)), whole((count, width)), whole((count, 128))],
        out_shape=[shape((count, width), BF16), shape((count, width), F32), shape((count, 128), jnp.int32)],
        compiler_params=params(),
        cost_estimate=cost(6 * count * dim * width, 6 << 20),
        name="own",
    )(normed, q, slot, w_proj, w_proj, w_proj)

    uid = pl.pallas_call(
        functools.partial(users_kernel, cap),
        grid=(1,),
        in_specs=[pl.BlockSpec(memory_space=pltpu.SMEM), whole((n_dev, count))],
        out_specs=whole((total, 128)),
        out_shape=shape((total, 128), F32),
        compiler_params=params(),
        cost_estimate=cost(1 << 28, 1 << 19),
        name="users",
    )(me, codes)

    flat = kv_cache.reshape(users * rows, 2 * width)
    attended = pl.pallas_call(
        attend_kernel,
        grid=(heads,),
        in_specs=[
            whole((total, 128)),
            pl.BlockSpec((total, HDIM), lambda h: (0, h)),
            pl.BlockSpec((users * rows, HDIM), lambda h: (0, h)),
            pl.BlockSpec((users * rows, HDIM), lambda h: (0, heads + h)),
        ],
        out_specs=pl.BlockSpec((total, HDIM), lambda h: (0, h)),
        out_shape=shape((total, width), BF16),
        scratch_shapes=[pltpu.VMEM((total, users * 64), BF16), pltpu.VMEM((total, 128), F32)],
        compiler_params=params(),
        cost_estimate=cost(2 * total * rows * users * width * 2, 6 << 20),
        name="attend",
    )(uid, arrived, flat, flat)

    back = lax.all_to_all(
        attended.reshape(n_dev, cap, width), AXES, split_axis=0, concat_axis=0, tiled=True
    ).reshape(total, width)

    cand_out = pl.pallas_call(
        answer_kernel,
        grid=(1,),
        in_specs=[
            whole((total, width)),
            whole((count, 128)),
            whole((count, width)),
            whole((count, width)),
        ],
        out_specs=whole((count, width)),
        out_shape=shape((count, width), BF16),
        compiler_params=params(),
        cost_estimate=cost(2 * count * total * width, 4 << 20),
        name="answer",
    )(back, slots, own, gate)
    return (kv_cache, cand_out)


def solution(mesh):
    placed = (
        P(AXES, None, None),
        P(AXES),
        P(AXES, None),
        P(AXES, None),
        P(AXES),
        P(),
        P(),
    )
    return jax.shard_map(
        body,
        mesh=mesh,
        in_specs=placed,
        out_specs=(P(AXES, None, None), P(AXES, None)),
        check_vma=False,
    )
```

time: 203 us -> 114 us (0.56)
  the two profiles are of different devices: /device:TPU:0 before, /device:TPU:1 now
where the time goes in v1:
time: 114 us; the launch traced here: 113 us
  blocking collectives  48.2 us (42%)
  Pallas kernels  22 us (19%)
  local copies, waits for them, and re-layouts  18.4 us (16%)
  waiting for transfers between devices  14 us (12%)
  starting transfers between devices  9.54 us (8%)
    all_gather x1, blocking collectives, body(): lax.all_gather(cand_owner[:, 0] * CODE + cand_user, AXES, axis=0, tiled=F...  48.2 us
    unnamed x43, local copies, waits for them, and re-layouts  18.4 us
    all_to_all x1, waiting for transfers between devices, body(): lax.all_to_all(attended.reshape(n_dev, cap, width), AXES, split_axis=0, c...  14 us
    pallas_call x1, Pallas kernels, body(): pl.pallas_call(attend_kernel, grid=(heads,), in_specs=[whole((total, 128)...  8.11 us
    pallas_call x1, Pallas kernels, body(): pl.pallas_call(encode_kernel, grid=(users // step,), in_specs=[pl.BlockSp...  7.39 us
    all_to_all x1, starting transfers between devices, body(): lax.all_to_all(outgoing.reshape(n_dev, cap, width), AXES, split_axis=0, c...  7.14 us
    all_to_all x1, starting transfers between devices, body(): lax.all_to_all(attended.reshape(n_dev, cap, width), AXES, split_axis=0, c...  2.4 us
  transfers between devices with their start and end apart: 2, of which 1 were waited for; matrix products, arithmetic and copies ran while one was open for 0% of the time, Pallas kernels for 9%

profile of v1, /device:TPU:1, one launch (start us, length us, event | category | flops | bytes accessed | tf_op | source)
XLA Modules:
  0.0 112.9 jit_solution(8910299710244961219)
XLA Ops:
  0.6 0.0 copy-start
  0.6 2.2 %copy-done = bf16[1024,2048]{1,0:T(8,128)(2,1)S(1)} copy-done((bf16[1024,2048]{1,0:T(8,128)(2,1)S(1)}, bf16[1024,2048]{1,0:T(8,128)(2,1)}, u32[]{:S(2)}) %copy-start) | copy-done | bytes 4194328
  2.8 1.2 %copy-done.5 = bf16[512,1024]{1,0:T(8,128)(2,1)S(1)} copy-done((bf16[512,1024]{1,0:T(8,128)(2,1)S(1)}, bf16[512,1024]{1,0:T(8,128)(2,1)}, u32[]{:S(2)}) %copy-start.5) | copy-done | bytes 1048600
  4.0 0.7 copy-done.13
  4.7 0.7 copy-done.15
  5.4 1.9 %dispatch.1 = (bf16[512,1024]{1,0:T(8,128)(2,1)S(1)}, bf16[512,512]{1,0:T(8,128)(2,1)S(1)}, s32[1,512]{1,0:T(1,128)S(1)}, bf16[768,512]{1,0:T(8,128)(2,1)S(1)}) custom-call(bf16[512,1024]{1,0:T(8,128)(2,1)S(1)} %copy-done.5, f32[1,1024]{1,0:T(1,128)S(1)} %bitcast.18, bf16[1024,2048]{1,0:T(8,128)(2,1)S(1)} %copy-done, s32[1,512]{1,0:T(1,128)S(1)} %bitcast.20), custom_call_target="tpu_custom_call" | custom-call | flops 939524096 | bytes 4194304 | tf_op jit(solution)/shard_map/dispatch/pallas_call | solution.py:201
  7.3 1.0 copy-done.6
  8.3 0.9 copy-done.8
  9.2 0.8 copy-done.11
  10.0 7.1 %all-to-all-start = ((bf16[32,24,512]{2,1,0:T(8,128)(2,1)}), bf16[32,24,512]{2,1,0:T(8,128)(2,1)}, u32[]{:S(2)}, u32[]{:S(2)}) async-start(bf16[32,24,512]{2,1,0:T(8,128)(2,1)} %bitcast.16), calls=%async_computation | async-start | bytes 1572864 | tf_op jit(solution)/shard_map/all_to_all | solution.py:217
  17.2 48.2 %all-gather.1 = s32[32,1,512]{2,1,0:T(1,128)S(1)} all-gather(s32[1,1,512]{2,1,0:T(1,128)S(1)} %bitcast.21), channel_id=2, replica_groups=mesh['grp'=4,'enc'=8] {'grp','enc'}, dimensions={0}, use_global_device_ids=true | all-gather | bytes 67584 | tf_op jit(solution)/shard_map/all_gather | solution.py:199
  65.4 0.7 users.1.uid_ref
  66.1 0.0 copy-start.18
  66.1 0.8 copy-done.18
  66.9 0.0 copy-done.3
  66.9 0.0 copy-done.17
  66.9 2.2 %copy-done.1 = bf16[1024,2048]{1,0:T(8,128)(2,1)S(1)} copy-done((bf16[1024,2048]{1,0:T(8,128)(2,1)S(1)}, bf16[1024,2048]{1,0:T(8,128)(2,1)}, u32[]{:S(2)}) %copy-start.1) | copy-done | bytes 4194328
  69.1 7.4 %encode.1 = bf16[12,128,1024]{2,1,0:T(8,128)(2,1)} custom-call(s32[12]{0:T(128)S(1)} %copy-done.17, bf16[12,128,1024]{2,1,0:T(8,128)(2,1)S(1)} %copy-done.3, f32[1,1024]{1,0:T(1,128)S(1)} %bitcast.19, bf16[1024,2048]{1,0:T(8,128)(2,1)S(1)} %copy-done.1, bf16[1024,2048]{1,0:T(8,128)(2,1)S(1)} %copy-done.1), custom_call_target="tpu_custom_call" | custom-call | flops 3221225472 | bytes 8388608 | tf_op jit(solution)/shard_map/encode/pallas_call | solution.py:222
  76.5 0.0 all-to-all-done
  76.5 1.9 %copy-done.4 = bf16[12,128,1024]{2,1,0:T(8,128)(2,1)S(1)} copy-done((bf16[12,128,1024]{2,1,0:T(8,128)(2,1)S(1)}, bf16[12,128,1024]{2,1,0:T(8,128)(2,1)}, u32[]{:S(2)}) %copy-start.4) | copy-done | bytes 3145752
  78.4 1.0 copy-done.19
  79.4 8.1 %attend.1 = bf16[768,512]{1,0:T(8,128)(2,1)} custom-call(f32[768,128]{1,0:T(8,128)S(1)} %copy-done.19, bf16[768,512]{1,0:T(8,128)(2,1)} %bitcast.6.q_ref, bf16[1536,1024]{1,0:T(8,128)(2,1)S(1)} %bitcast.13, bf16[1536,1024]{1,0:T(8,128)(2,1)S(1)} %bitcast.14), custom_call_target="tpu_custom_call" | custom-call | flops 2415919104 | bytes 6291456 | tf_op jit(solution)/shard_map/attend/pallas_call | solution.py:269
  87.5 2.4 %all-to-all-start.1 = ((bf16[32,24,512]{2,1,0:T(8,128)(2,1)}), bf16[32,24,512]{2,1,0:T(8,128)(2,1)S(1)}, u32[]{:S(2)}, u32[]{:S(2)}) async-start(bf16[32,24,512]{2,1,0:T(8,128)(2,1)} %bitcast.8), calls=%async_computation.1 | async-start | bytes 1572864 | tf_op jit(solution)/shard_map/all_to_all | solution.py:286
  89.9 0.0 copy-start.2
  89.9 2.2 %copy-done.2 = bf16[1024,2048]{1,0:T(8,128)(2,1)S(1)} copy-done((bf16[1024,2048]{1,0:T(8,128)(2,1)S(1)}, bf16[1024,2048]{1,0:T(8,128)(2,1)}, u32[]{:S(2)}) %copy-start.2) | copy-done | bytes 4194328
  92.1 1.0 copy-done.12
  93.1 2.2 %own.1 = (bf16[512,512]{1,0:T(8,128)(2,1)S(1)}, f32[512,512]{1,0:T(8,128)S(1)}, s32[512,128]{1,0:T(8,128)S(1)}) custom-call(bf16[512,1024]{1,0:T(8,128)(2,1)S(1)} %copy-done.7, bf16[512,512]{1,0:T(8,128)(2,1)S(1)} %copy-done.12, s32[1,512]{1,0:T(1,128)S(1)} %get-tuple-element.12.slot_ref, bf16[1024,2048]{1,0:T(8,128)(2,1)S(1)} %copy-done.2, ...), custom_call_target="tpu_custom_call" | custom-call | flops 1610612736 | bytes 6291456 | tf_op jit(solution)/shard_map/own/pallas_call | solution.py:239
  95.3 0.0 copy-start.9
  95.4 0.8 copy-done.9
  96.1 14.0 %all-to-all-done.1 = bf16[32,24,512]{2,1,0:T(8,128)(2,1)S(1)} async-done(((bf16[32,24,512]{2,1,0:T(8,128)(2,1)}), bf16[32,24,512]{2,1,0:T(8,128)(2,1)S(1)}, u32[]{:S(2)}, u32[]{:S(2)}) %all-to-all-start.1) | async-done | bytes 786464 | tf_op jit(solution)/shard_map/all_to_all | solution.py:286
  110.2 1.0 copy-done.10
  111.2 1.7 %answer.1 = bf16[512,512]{1,0:T(8,128)(2,1)} custom-call(bf16[768,512]{1,0:T(8,128)(2,1)S(1)} %bitcast.15, s32[512,128]{1,0:T(8,128)S(1)} %get-tuple-element.13.column_ref, f32[512,512]{1,0:T(8,128)S(1)} %get-tuple-element.14.self_ref, bf16[512,512]{1,0:T(8,128)(2,1)S(1)} %copy-done.10), custom_call_target="tpu_custom_call" | custom-call | flops 402653184 | bytes 4194304 | tf_op jit(solution)/shard_map/answer/pallas_call | solution.py:290
  (24 shorter events, 0.1 us)
Async XLA Ops:
  0.6 2.2 %copy-start = (bf16[1024,2048]{1,0:T(8,128)(2,1)S(1)}, bf16[1024,2048]{1,0:T(8,128)(2,1)}, u32[]{:S(2)}) copy-start(bf16[1024,2048]{1,0:T(8,128)(2,1)} %wk_ref.3) | copy-start | bytes 12582916
  2.8 1.2 %copy-start.5 = (bf16[512,1024]{1,0:T(8,128)(2,1)S(1)}, bf16[512,1024]{1,0:T(8,128)(2,1)}, u32[]{:S(2)}) copy-start(bf16[512,1024]{1,0:T(8,128)(2,1)} %cand_ref.1) | copy-start | bytes 3145732
  4.0 0.7 copy-start.13
  4.7 0.7 copy-start.15
  5.4 11.8 %copy-start.16 = (s32[512,1]{0,1:T(1,128)S(1)}, s32[512,1]{0,1:T(1,128)}, u32[]{:S(2)}) copy-start(s32[512,1]{0,1:T(1,128)} %param.10) | copy-start | bytes 6148
  5.4 11.8 %copy-start.20 = (s32[512]{0:T(512)S(1)}, s32[512]{0:T(512)}, u32[]{:S(2)}) copy-start(s32[512]{0:T(512)} %param.11) | copy-start | bytes 6148
  5.4 61.5 %copy-start.3 = (bf16[12,128,1024]{2,1,0:T(8,128)(2,1)S(1)}, bf16[12,128,1024]{2,1,0:T(8,128)(2,1)}, u32[]{:S(2)}) copy-start(bf16[12,128,1024]{2,1,0:T(8,128)(2,1)} %hist_ref.1) | copy-start | bytes 9437188
  5.4 61.5 %copy-start.14 = (f32[1024]{0:T(1024)S(1)}, f32[1024]{0:T(1024)}, u32[]{:S(2)}) copy-start(f32[1024]{0:T(1024)} %param.12) | copy-start | bytes 12292
  5.4 61.5 %copy-start.17 = (s32[12]{0:T(128)S(1)}, s32[12]{0:T(128)}, u32[]{:S(2)}) copy-start(s32[12]{0:T(128)} %len_ref.1) | copy-start | bytes 148
  7.3 1.0 copy-start.6
  8.3 0.9 copy-start.8
  9.2 0.8 copy-start.11
  10.0 66.5 %all-to-all-start = ((bf16[32,24,512]{2,1,0:T(8,128)(2,1)}), bf16[32,24,512]{2,1,0:T(8,128)(2,1)}, u32[]{:S(2)}, u32[]{:S(2)}) async-start(bf16[32,24,512]{2,1,0:T(8,128)(2,1)} %bitcast.16), calls=%async_computation | async-start | bytes 1572864 | tf_op jit(solution)/shard_map/all_to_all | solution.py:217
  66.1 0.8 copy-start.18
  66.9 2.2 %copy-start.1 = (bf16[1024,2048]{1,0:T(8,128)(2,1)S(1)}, bf16[1024,2048]{1,0:T(8,128)(2,1)}, u32[]{:S(2)}) copy-start(bf16[1024,2048]{1,0:T(8,128)(2,1)} %wk_ref.3) | copy-start | bytes 12582916
  76.5 1.9 %copy-start.4 = (bf16[12,128,1024]{2,1,0:T(8,128)(2,1)S(1)}, bf16[12,128,1024]{2,1,0:T(8,128)(2,1)}, u32[]{:S(2)}) copy-start(bf16[12,128,1024]{2,1,0:T(8,128)(2,1)} %encode.1) | copy-start | bytes 9437188
  78.4 1.0 copy-start.19
  79.4 10.5 %copy-start.7 = (bf16[512,1024]{1,0:T(8,128)(2,1)S(1)}, bf16[512,1024]{1,0:T(8,128)(2,1)}, u32[]{:S(2)}) copy-start(bf16[512,1024]{1,0:T(8,128)(2,1)} %copy-done.6) | copy-start | bytes 3145732
  87.5 22.7 %all-to-all-start.1 = ((bf16[32,24,512]{2,1,0:T(8,128)(2,1)}), bf16[32,24,512]{2,1,0:T(8,128)(2,1)S(1)}, u32[]{:S(2)}, u32[]{:S(2)}) async-start(bf16[32,24,512]{2,1,0:T(8,128)(2,1)} %bitcast.8), calls=%async_computation.1 | async-start | bytes 1572864 | tf_op jit(solution)/shard_map/all_to_all | solution.py:286
  89.9 2.2 %copy-start.2 = (bf16[1024,2048]{1,0:T(8,128)(2,1)S(1)}, bf16[1024,2048]{1,0:T(8,128)(2,1)}, u32[]{:S(2)}) copy-start(bf16[1024,2048]{1,0:T(8,128)(2,1)} %wk_ref.3) | copy-start | bytes 12582916
  92.1 1.0 copy-start.12
  95.3 0.8 copy-start.9
  110.2 1.0 copy-start.10

commit v2 on v1

v2 whole, which is shorter than its diff:
```python
import functools

import jax
import jax.numpy as jnp
from jax import lax
from jax.experimental import pallas as pl
from jax.experimental.pallas import tpu as pltpu
from jax.sharding import PartitionSpec as P

HDIM = 128
PIECE = 64
F32 = jnp.float32
BF16 = jnp.bfloat16
AXES = ("grp", "enc")
NT = (((1,), (1,)), ((), ()))


def silu(x):
    half = 0.5 * x
    return half + half * jnp.tanh(half)


def norm_rows(values):
    center = values - jnp.mean(values, axis=-1, keepdims=True)
    spread = jnp.mean(center * center, axis=-1, keepdims=True)
    return center * lax.rsqrt(spread + 1e-05)


def mm(a, b):
    return jnp.dot(a, b, preferred_element_type=F32)


def one_hot(hit):
    return jnp.where(hit, 1.0, 0.0).astype(BF16)


def iota(shape, dim):
    return lax.broadcasted_iota(jnp.int32, shape, dim)


def ranks(owner, n_dev):
    count = owner.shape[1]
    named = iota((n_dev, count), 0) == owner
    before = mm(one_hot(named), one_hot(iota((count, count), 0) < iota((count, count), 1)))
    return named, jnp.sum(jnp.where(named, before, 0.0), axis=0, keepdims=True).astype(jnp.int32)


def dispatch_kernel(cap, cand_ref, gain_ref, wq_ref, owner_ref, user_ref, out_ref, q_ref, pick_ref):
    n_dev = out_ref.shape[0]
    step, width = cand_ref.shape[0], wq_ref.shape[1]
    count = owner_ref.shape[1]
    heads = width // HDIM
    i = pl.program_id(0)

    @pl.when(i == 0)
    def _():
        owner = owner_ref[...]
        named, rank = ranks(owner, n_dev)
        pick_ref[...] = one_hot(iota((n_dev * cap, count), 0) == owner * cap + rank)
        users = jnp.where(named, user_ref[...].astype(F32), 0.0).astype(BF16)
        place = one_hot(iota((128, count), 0) == rank)
        table = lax.dot_general(users, place, NT, preferred_element_type=F32)
        out_ref[:, heads * cap :, :] = jnp.broadcast_to(table[:, None, :], (n_dev, 8, 128)).astype(BF16)

    normed = (norm_rows(cand_ref[...].astype(F32)) * gain_ref[...]).astype(BF16)
    q_ref[pl.ds(pl.multiple_of(i * step, step), step), :] = silu(mm(normed, wq_ref[...])).astype(BF16)

    @pl.when(i == pl.num_programs(0) - 1)
    def _():
        sent = mm(pick_ref[...], q_ref[...])
        for h in range(heads):
            part = sent[:, h * HDIM : (h + 1) * HDIM].reshape(n_dev, cap, HDIM)
            out_ref[:, h * cap : (h + 1) * cap, :] = part.astype(BF16)


def encode_kernel(len_ref, hist_ref, gain_ref, wv_ref, wk_ref, out_ref, key_ref, value_ref):
    users, rows, dim = hist_ref.shape
    width = wk_ref.shape[1]
    first = pl.program_id(0) * users
    x = hist_ref[...].reshape(users * rows, dim).astype(F32)
    normed = (norm_rows(x) * gain_ref[...]).astype(BF16)
    keys = silu(mm(normed, wk_ref[...]))
    values = silu(mm(normed, wv_ref[...]))
    row_ids = iota((rows, width), 0)
    for u in range(users):
        live = row_ids < len_ref[first + u] * PIECE
        part = slice(u * rows, (u + 1) * rows)
        side = slice((u % 2) * rows, (u % 2 + 1) * rows)
        pair = slice((u // 2) * HDIM, (u // 2 + 1) * HDIM)
        key = jnp.where(live, keys[part], 0.0)
        value = jnp.where(live, values[part], 0.0).astype(BF16)
        out_ref[u, :, :width] = key.astype(BF16)
        out_ref[u, :, width:] = value
        for h in range(width // HDIM):
            cols = slice(h * HDIM, (h + 1) * HDIM)
            key_ref[h, pair, side] = key[:, cols].T.astype(BF16)
            value_ref[h, pair, side] = value[:, cols]


def own_kernel(n_dev, cap, cand_ref, gain_ref, w_ref, owner_ref, u_ref, self_ref, column_ref):
    step, width = u_ref.shape
    i = pl.program_id(0)
    normed = (norm_rows(cand_ref[...].astype(F32)) * gain_ref[...]).astype(BF16)

    def projected(part):
        return silu(mm(normed, w_ref[:, part * width : (part + 1) * width])).astype(BF16)

    u_ref[...] = projected(0)
    own_v = projected(1).astype(F32)
    prod = projected(2).astype(F32) * projected(3).astype(F32)
    for h in range(width // HDIM):
        cols = slice(h * HDIM, (h + 1) * HDIM)
        score = jnp.sum(prod[:, cols], axis=-1, keepdims=True) * HDIM ** (-0.5)
        self_ref[:, cols] = silu(score).astype(BF16).astype(F32) * own_v[:, cols]

    @pl.when(i == 0)
    def _():
        owner = owner_ref[...]
        _, rank = ranks(owner, n_dev)
        slot = (owner * cap + rank).astype(F32)
        column_ref[...] = jnp.broadcast_to(slot, (128, slot.shape[1])).T.astype(jnp.int32)


def attend_kernel(cap, table_ref, q_ref, k_ref, v_ref, out_ref, mask_ref, odd_ref):
    n_dev = q_ref.shape[0]
    total = n_dev * cap
    pairs = k_ref.shape[1] // HDIM

    @pl.when(pl.program_id(0) == 0)
    def _():
        table = table_ref[:, 0:1, :].astype(F32)
        full = (n_dev, cap, 128)
        uid = jnp.where(iota(full, 1) == iota(full, 2), jnp.broadcast_to(table, full), 0.0)
        uid = jnp.broadcast_to(jnp.sum(uid, axis=2, keepdims=True), full).reshape(total, 128)
        pair = jnp.floor(uid * 0.5)
        odd_ref[...] = uid - 2.0 * pair
        for p in range(pairs):
            mask_ref[:, p * 128 : (p + 1) * 128] = one_hot(pair == 1.0 * p)

    odd = odd_ref[...] > 0.5

    def spread(x):
        return jnp.concatenate([x * mask_ref[:, p * 128 : (p + 1) * 128] for p in range(pairs)], axis=1)

    def chosen(x):
        return jnp.where(odd, x[:, 128:], x[:, :128])

    for h in range(k_ref.shape[0]):
        rows = slice(h * cap, (h + 1) * cap)
        query = q_ref[:, rows, :].astype(F32).reshape(total, HDIM).astype(BF16)
        scores = chosen(mm(spread(query), k_ref[h]))
        weight = silu(scores * HDIM ** (-0.5)).astype(BF16)
        attended = chosen(mm(spread(weight), v_ref[h]))
        out_ref[:, rows, :] = attended.reshape(n_dev, cap, HDIM).astype(BF16)


def answer_kernel(back_ref, column_ref, self_ref, u_ref, out_ref):
    step, width = u_ref.shape
    n_dev = back_ref.shape[0]
    heads = width // HDIM
    cap = back_ref.shape[1] // heads
    total = n_dev * cap
    pick = one_hot(iota((step, total), 1) == column_ref[:, 0:1])
    back = [
        back_ref[:, h * cap : (h + 1) * cap, :].astype(F32).reshape(total, HDIM).astype(BF16) for h in range(heads)
    ]
    attended = mm(pick, jnp.concatenate(back, axis=1)) + self_ref[...]
    normed = norm_rows(attended).astype(BF16).astype(F32)
    out_ref[...] = (normed * u_ref[...].astype(F32)).astype(BF16)


def params():
    return pltpu.CompilerParams(vmem_limit_bytes=58 * 1024 * 1024)


def whole(shape):
    return pl.BlockSpec(shape, lambda *_: (0,) * len(shape))


def column(shape, index):
    return pl.BlockSpec(shape, lambda *_: (0, index))


def cost(flops, size):
    return pl.CostEstimate(flops=flops, bytes_accessed=size, transcendentals=0)


def exchange(slots):
    return lax.all_to_all(slots, AXES, split_axis=0, concat_axis=0, tiled=True)


def body(history, hist_len, cand, cand_owner, cand_user, norm_gain, w_proj):
    users, rows, dim = history.shape
    width = w_proj.shape[1] // 4
    heads = width // HDIM
    count = cand.shape[0]
    n_dev = lax.axis_size("grp") * lax.axis_size("enc")
    cap = -(-max(2, 3 * count // (2 * n_dev)) // 8) * 8
    total = n_dev * cap
    gain = norm_gain.reshape(1, dim)
    owner = cand_owner.reshape(1, count)
    user = cand_user.reshape(1, count)
    shape = jax.ShapeDtypeStruct

    step = count // 2
    outgoing = pl.pallas_call(
        functools.partial(dispatch_kernel, cap),
        grid=(count // step,),
        in_specs=[
            pl.BlockSpec((step, dim), lambda i: (i, 0)),
            whole((1, dim)),
            column((dim, width), 2),
            whole((1, count)),
            whole((1, count)),
        ],
        out_specs=whole((n_dev, heads * cap + 8, HDIM)),
        out_shape=shape((n_dev, heads * cap + 8, HDIM), BF16),
        scratch_shapes=[pltpu.VMEM((count, width), BF16), pltpu.VMEM((total, count), BF16)],
        compiler_params=params(),
        cost_estimate=cost(2 * count * width * (dim + total), 4 << 20),
        name="dispatch",
    )(cand, gain, w_proj, owner, user)

    arrived = exchange(outgoing)

    span = 4
    kv_cache, keys, values = pl.pallas_call(
        encode_kernel,
        grid=(users // span,),
        in_specs=[
            pl.BlockSpec(memory_space=pltpu.SMEM),
            pl.BlockSpec((span, rows, dim), lambda i: (i, 0, 0)),
            whole((1, dim)),
            column((dim, width), 1),
            column((dim, width), 3),
        ],
        out_specs=[
            pl.BlockSpec((span, rows, 2 * width), lambda i: (i, 0, 0)),
            pl.BlockSpec((heads, span * HDIM // 2, 2 * rows), lambda i: (0, i, 0)),
            pl.BlockSpec((heads, span * rows // 2, 2 * HDIM), lambda i: (0, i, 0)),
        ],
        out_shape=[
            shape((users, rows, 2 * width), BF16),
            shape((heads, users * HDIM // 2, 2 * rows), BF16),
            shape((heads, users * rows // 2, 2 * HDIM), BF16),
        ],
        compiler_params=params(),
        cost_estimate=cost(2 * users * rows * dim * 2 * width, 12 << 20),
        name="encode",
    )(hist_len, history, gain, w_proj, w_proj)

    gate, own, slots = pl.pallas_call(
        functools.partial(own_kernel, n_dev, cap),
        grid=(count // step,),
        in_specs=[
            pl.BlockSpec((step, dim), lambda i: (i, 0)),
            whole((1, dim)),
            whole((dim, 4 * width)),
            whole((1, count)),
        ],
        out_specs=[
            pl.BlockSpec((step, width), lambda i: (i, 0)),
            pl.BlockSpec((step, width), lambda i: (i, 0)),
            whole((count, 128)),
        ],
        out_shape=[shape((count, width), BF16), shape((count, width), F32), shape((count, 128), jnp.int32)],
        compiler_params=params(),
        cost_estimate=cost(8 * count * dim * width, 6 << 20),
        name="own",
    )(cand, gain, w_proj, owner)

    each = 2
    attended = pl.pallas_call(
        functools.partial(attend_kernel, cap),
        grid=(heads // each,),
        in_specs=[
            pl.BlockSpec((n_dev, 8, HDIM), lambda h: (0, heads * cap // 8, 0)),
            pl.BlockSpec((n_dev, each * cap, HDIM), lambda h: (0, h, 0)),
            pl.BlockSpec((each, users * HDIM // 2, 2 * rows), lambda h: (h, 0, 0)),
            pl.BlockSpec((each, users * rows // 2, 2 * HDIM), lambda h: (h, 0, 0)),
        ],
        out_specs=pl.BlockSpec((n_dev, each * cap, HDIM), lambda h: (0, h, 0)),
        out_shape=shape((n_dev, heads * cap, HDIM), BF16),
        scratch_shapes=[pltpu.VMEM((total, users * 64), BF16), pltpu.VMEM((total, 128), F32)],
        compiler_params=params(),
        cost_estimate=cost(2 * total * rows * users * width * 2, 6 << 20),
        name="attend",
    )(arrived, arrived, keys, values)

    back = exchange(attended)

    cand_out = pl.pallas_call(
        answer_kernel,
        grid=(count // step,),
        in_specs=[
            whole((n_dev, heads * cap, HDIM)),
            pl.BlockSpec((step, 128), lambda i: (i, 0)),
            pl.BlockSpec((step, width), lambda i: (i, 0)),
            pl.BlockSpec((step, width), lambda i: (i, 0)),
        ],
        out_specs=pl.BlockSpec((step, width), lambda i: (i, 0)),
        out_shape=shape((count, width), BF16),
        compiler_params=params(),
        cost_estimate=cost(2 * count * total * width, 4 << 20),
        name="answer",
    )(back, slots, own, gate)
    return (kv_cache, cand_out)


def solution(mesh):
    placed = (
        P(AXES, None, None),
        P(AXES),
        P(AXES, None),
        P(AXES, None),
        P(AXES),
        P(),
        P(),
    )
    return jax.shard_map(
        body,
        mesh=mesh,
        in_specs=placed,
        out_specs=(P(AXES, None, None), P(AXES, None)),
        check_vma=False,
    )
```

time: 114 us -> 71.6 us (0.63)
  blocking collectives: 48.2 us -> 0 us
  local copies, waits for them, and re-layouts: 18.4 us -> 1.83 us
  waiting for transfers between devices: 14 us -> 24.6 us
  Pallas kernels: 22 us -> 32.1 us
  starting transfers between devices: 9.54 us -> 11.4 us
    all_gather x1 -> x0, blocking collectives: 48.2 us -> none  [body(): lax.all_gather(cand_owner[:, 0] * CODE + cand_user, AXES, axis=0, tiled=F...]
    unnamed x43 -> x4, local copies, waits for them, and re-layouts: 18.4 us -> 1.83 us
    all_to_all x2, waiting for transfers between devices: 14 us -> 24.6 us  [exchange(): return lax.all_to_all(slots, AXES, split_axis=0, concat_axis=0, tiled=True)]
    pallas_call x6 -> x5, Pallas kernels: 22 us -> 32.1 us  [the longest x1 9.31 us: body(): pl.pallas_call(encode_kernel, grid=(users // span,), in_specs=[pl.BlockSp...]
    all_to_all x2, starting transfers between devices: 9.54 us -> 11.4 us  [exchange(): return lax.all_to_all(slots, AXES, split_axis=0, concat_axis=0, tiled=True)]
  transfers between devices with their start and end apart: 2 -> 2, of which waited for: 1 -> 2; matrix products, arithmetic and copies ran while one was open for 0% -> 0% of each run, Pallas kernels for 9% -> 24%
where the time goes in v2:
time: 71.6 us; the launch traced here: 70.6 us
  Pallas kernels  32.1 us (45%)
  waiting for transfers between devices  24.6 us (34%)
  starting transfers between devices  11.4 us (16%)
  local copies, waits for them, and re-layouts  1.83 us (3%)
    all_to_all x2, waiting for transfers between devices, exchange(): return lax.all_to_all(slots, AXES, split_axis=0, concat_axis=0, tiled=True)  24.6 us
    all_to_all x2, starting transfers between devices, exchange(): return lax.all_to_all(slots, AXES, split_axis=0, concat_axis=0, tiled=True)  11.4 us
    pallas_call x1, Pallas kernels, body(): pl.pallas_call(encode_kernel, grid=(users // span,), in_specs=[pl.BlockSp...  9.31 us
    pallas_call x1, Pallas kernels, body(): pl.pallas_call(functools.partial(own_kernel, n_dev, cap), grid=(count //...  7.55 us
    pallas_call x1, Pallas kernels, body(): pl.pallas_call(functools.partial(attend_kernel, cap), grid=(heads // each...  6.53 us
    pallas_call x1, Pallas kernels, body(): pl.pallas_call(functools.partial(dispatch_kernel, cap), grid=(count // st...  5.08 us
    pallas_call x1, Pallas kernels, body(): pl.pallas_call(answer_kernel, grid=(count // step,), in_specs=[whole((n_d...  3.59 us
    unnamed x4, local copies, waits for them, and re-layouts  1.83 us
  transfers between devices with their start and end apart: 2, of which 2 were waited for; matrix products, arithmetic and copies ran while one was open for 0% of the time, Pallas kernels for 24%

profile of v2, /device:TPU:1, one launch (start us, length us, event | category | flops | bytes accessed | tf_op | source)
XLA Modules:
  0.0 70.6 jit_solution(14987654994604884249)
XLA Ops:
  0.6 5.1 %dispatch.1 = bf16[32,104,128]{2,1,0:T(8,128)(2,1)} custom-call(bf16[512,1024]{1,0:T(8,128)(2,1)} %cand_ref.3, f32[1,1024]{1,0:T(1,128)} %bitcast.3, bf16[1024,2048]{1,0:T(8,128)(2,1)} %w_ref.1, s32[1,512]{1,0:T(1,128)} %bitcast.7, s32[1,512]{1,0:T(1,128)} %bitcast.6), custom_call_target="tpu_custom_call" | custom-call | flops 939524096 | bytes 4194304 | tf_op jit(solution)/shard_map/dispatch/pallas_call | solution.py:206
  5.7 7.1 %all-to-all-start = ((bf16[32,104,128]{2,1,0:T(8,128)(2,1)}), bf16[32,104,128]{2,1,0:T(8,128)(2,1)S(1)}, u32[]{:S(2)}, u32[]{:S(2)}) async-start(bf16[32,104,128]{2,1,0:T(8,128)(2,1)} %dispatch.1), calls=%async_computation | async-start | bytes 1703936 | tf_op jit(solution)/shard_map/all_to_all | solution.py:189
  12.8 9.3 %encode.1 = (bf16[12,128,1024]{2,1,0:T(8,128)(2,1)}, bf16[4,768,256]{2,1,0:T(8,128)(2,1)}, bf16[4,768,256]{2,1,0:T(8,128)(2,1)}) custom-call(s32[12]{0:T(128)} %len_ref.1, bf16[12,128,1024]{2,1,0:T(8,128)(2,1)} %hist_ref.1, f32[1,1024]{1,0:T(1,128)} %bitcast.4, bf16[1024,2048]{1,0:T(8,128)(2,1)} %w_ref.1, bf16[1024,2048]{1,0:T(8,128)(2,1)} %w_ref.1), custom_call_target="tpu_custom_call" | custom-call | flops 3221225472 | bytes 12582912 | tf_op jit(solution)/shard_map/encode/pallas_call | solution.py:227
  22.1 12.0 %all-to-all-done.table_ref.q_ref = bf16[32,104,128]{2,1,0:T(8,128)(2,1)S(1)} async-done(((bf16[32,104,128]{2,1,0:T(8,128)(2,1)}), bf16[32,104,128]{2,1,0:T(8,128)(2,1)S(1)}, u32[]{:S(2)}, u32[]{:S(2)}) %all-to-all-start) | async-done | bytes 852000 | tf_op jit(solution)/shard_map/all_to_all | solution.py:189
  34.2 0.0 copy-start.1
  34.2 0.9 %copy-done.1 = bf16[32,104,128]{2,1,0:T(8,128)(2,1)} copy-done((bf16[32,104,128]{2,1,0:T(8,128)(2,1)}, bf16[32,104,128]{2,1,0:T(8,128)(2,1)S(1)}, u32[]{:S(2)}) %copy-start.1) | copy-done | bytes 851992
  35.1 6.5 %attend.1 = bf16[32,96,128]{2,1,0:T(8,128)(2,1)} custom-call(bf16[32,104,128]{2,1,0:T(8,128)(2,1)} %copy-done.1, bf16[32,104,128]{2,1,0:T(8,128)(2,1)} %copy-done.1, bf16[4,768,256]{2,1,0:T(8,128)(2,1)} %get-tuple-element.9.k_ref, bf16[4,768,256]{2,1,0:T(8,128)(2,1)} %get-tuple-element.10.v_ref), custom_call_target="tpu_custom_call" | custom-call | flops 2415919104 | bytes 6291456 | tf_op jit(solution)/shard_map/attend/pallas_call | solution.py:273
  41.6 4.3 %all-to-all-start.1 = ((bf16[32,96,128]{2,1,0:T(8,128)(2,1)}), bf16[32,96,128]{2,1,0:T(8,128)(2,1)S(1)}, u32[]{:S(2)}, u32[]{:S(2)}) async-start(bf16[32,96,128]{2,1,0:T(8,128)(2,1)} %attend.1), calls=%async_computation.1 | async-start | bytes 1572864 | tf_op jit(solution)/shard_map/all_to_all | solution.py:189
  45.9 7.5 %own.1 = (bf16[512,512]{1,0:T(8,128)(2,1)}, f32[512,512]{1,0:T(8,128)}, s32[512,128]{1,0:T(8,128)}) custom-call(bf16[512,1024]{1,0:T(8,128)(2,1)} %cand_ref.3, f32[1,1024]{1,0:T(1,128)} %bitcast.5, bf16[1024,2048]{1,0:T(8,128)(2,1)} %w_ref.1, s32[1,512]{1,0:T(1,128)} %bitcast.8), custom_call_target="tpu_custom_call" | custom-call | flops 2147483648 | bytes 6291456 | tf_op jit(solution)/shard_map/own/pallas_call | solution.py:252
  53.5 12.6 %all-to-all-done.1.back_ref = bf16[32,96,128]{2,1,0:T(8,128)(2,1)S(1)} async-done(((bf16[32,96,128]{2,1,0:T(8,128)(2,1)}), bf16[32,96,128]{2,1,0:T(8,128)(2,1)S(1)}, u32[]{:S(2)}, u32[]{:S(2)}) %all-to-all-start.1) | async-done | bytes 786464 | tf_op jit(solution)/shard_map/all_to_all | solution.py:189
  66.1 0.0 copy-start
  66.1 0.9 %copy-done = bf16[32,96,128]{2,1,0:T(8,128)(2,1)} copy-done((bf16[32,96,128]{2,1,0:T(8,128)(2,1)}, bf16[32,96,128]{2,1,0:T(8,128)(2,1)S(1)}, u32[]{:S(2)}) %copy-start) | copy-done | bytes 786456
  67.0 3.6 %answer.1 = bf16[512,512]{1,0:T(8,128)(2,1)} custom-call(bf16[32,96,128]{2,1,0:T(8,128)(2,1)} %copy-done, s32[512,128]{1,0:T(8,128)} %get-tuple-element.11.column_ref, f32[512,512]{1,0:T(8,128)} %get-tuple-element.12.self_ref, bf16[512,512]{1,0:T(8,128)(2,1)} %get-tuple-element.13.u_ref), custom_call_target="tpu_custom_call" | custom-call | flops 402653184 | bytes 4194304 | tf_op jit(solution)/shard_map/answer/pallas_call | solution.py:292
Async XLA Ops:
  5.7 28.4 %all-to-all-start = ((bf16[32,104,128]{2,1,0:T(8,128)(2,1)}), bf16[32,104,128]{2,1,0:T(8,128)(2,1)S(1)}, u32[]{:S(2)}, u32[]{:S(2)}) async-start(bf16[32,104,128]{2,1,0:T(8,128)(2,1)} %dispatch.1), calls=%async_computation | async-start | bytes 1703936 | tf_op jit(solution)/shard_map/all_to_all | solution.py:189
  34.2 0.9 %copy-start.1 = (bf16[32,104,128]{2,1,0:T(8,128)(2,1)}, bf16[32,104,128]{2,1,0:T(8,128)(2,1)S(1)}, u32[]{:S(2)}) copy-start(bf16[32,104,128]{2,1,0:T(8,128)(2,1)S(1)} %all-to-all-done.table_ref.q_ref) | copy-start | bytes 2555908
  41.6 24.5 %all-to-all-start.1 = ((bf16[32,96,128]{2,1,0:T(8,128)(2,1)}), bf16[32,96,128]{2,1,0:T(8,128)(2,1)S(1)}, u32[]{:S(2)}, u32[]{:S(2)}) async-start(bf16[32,96,128]{2,1,0:T(8,128)(2,1)} %attend.1), calls=%async_computation.1 | async-start | bytes 1572864 | tf_op jit(solution)/shard_map/all_to_all | solution.py:189
  66.1 0.9 %copy-start = (bf16[32,96,128]{2,1,0:T(8,128)(2,1)}, bf16[32,96,128]{2,1,0:T(8,128)(2,1)S(1)}, u32[]{:S(2)}) copy-start(bf16[32,96,128]{2,1,0:T(8,128)(2,1)S(1)} %all-to-all-done.1.back_ref) | copy-start | bytes 2359300

commit v3 on v2

v3 whole, which is shorter than its diff:
```python
import functools

import jax
import jax.numpy as jnp
from jax import lax
from jax.experimental import pallas as pl
from jax.experimental.pallas import tpu as pltpu
from jax.sharding import PartitionSpec as P

HDIM = 128
PIECE = 64
F32 = jnp.float32
BF16 = jnp.bfloat16
AXES = ("grp", "enc")
NT = (((1,), (1,)), ((), ()))


def silu(x):
    half = 0.5 * x
    return half + half * jnp.tanh(half)


def norm_rows(values):
    center = values - jnp.mean(values, axis=-1, keepdims=True)
    spread = jnp.mean(center * center, axis=-1, keepdims=True)
    return center * lax.rsqrt(spread + 1e-05)


def mm(a, b):
    return jnp.dot(a, b, preferred_element_type=F32)


def one_hot(hit):
    return jnp.where(hit, 1.0, 0.0).astype(BF16)


def iota(shape, dim):
    return lax.broadcasted_iota(jnp.int32, shape, dim)


def ranks(place, n_dev):
    count = place.shape[1]
    named = iota((n_dev, count), 0) == place
    before = mm(one_hot(named), one_hot(iota((count, count), 0) < iota((count, count), 1)))
    return named, jnp.sum(jnp.where(named, before, 0.0), axis=0, keepdims=True).astype(jnp.int32)


def place_of(owner, n_grp, n_enc):
    return lax.rem(owner, n_enc) * n_grp + lax.div(owner, n_enc)


def dispatch_kernel(
    n_grp, n_enc, cap, cand_hbm, gain_hbm, w_hbm, owner_hbm, user_hbm, out_hbm,
    cand_ref, gain_ref, wq_ref, owner_ref, user_ref, out_ref, q_ref, pick_ref, small_sem, cand_sem, w_sem, out_sem,
):
    n_dev = out_ref.shape[0]
    count, width = q_ref.shape
    heads = width // HDIM
    parts = cand_sem.shape[0]
    step = count // parts

    def block(ref, i):
        return ref.at[pl.ds(i * step, step), :]

    small = [
        pltpu.make_async_copy(owner_hbm, owner_ref, small_sem.at[0]),
        pltpu.make_async_copy(user_hbm, user_ref, small_sem.at[1]),
        pltpu.make_async_copy(gain_hbm, gain_ref, small_sem.at[2]),
    ]
    loads = [pltpu.make_async_copy(block(cand_hbm, i), block(cand_ref, i), cand_sem.at[i]) for i in range(parts)]
    weights = pltpu.make_async_copy(w_hbm.at[:, pl.ds(2 * width, width)], wq_ref, w_sem.at[0])
    for copy in small:
        copy.start()
    loads[0].start()
    weights.start()
    for copy in loads[1:]:
        copy.start()
    for copy in small:
        copy.wait()
    place = place_of(owner_ref[...], n_grp, n_enc)
    named, rank = ranks(place, n_dev)
    pick_ref[...] = one_hot(iota((n_dev * cap, count), 0) == place * cap + rank)
    users = jnp.where(named, user_ref[...].astype(F32), 0.0).astype(BF16)
    table = lax.dot_general(users, one_hot(iota((128, count), 0) == rank), NT, preferred_element_type=F32)
    out_ref[:, heads * cap :, :] = jnp.broadcast_to(table[:, None, :], (n_dev, 8, 128)).astype(BF16)
    gain = gain_ref[...]
    for i in range(parts):
        rows = slice(i * step, (i + 1) * step)
        loads[i].wait()
        normed = (norm_rows(cand_ref[rows, :].astype(F32)) * gain).astype(BF16)
        if i == 0:
            weights.wait()
        q_ref[rows, :] = silu(mm(normed, wq_ref[...])).astype(BF16)
    stores = []
    groups = out_sem.shape[0]
    span = n_dev // groups
    for g in range(groups):
        devs = slice(g * span, (g + 1) * span)
        sent = mm(pick_ref[g * span * cap : (g + 1) * span * cap, :], q_ref[...])
        for h in range(heads):
            part = sent[:, h * HDIM : (h + 1) * HDIM].reshape(span, cap, HDIM)
            out_ref[devs, h * cap : (h + 1) * cap, :] = part.astype(BF16)
        at = pl.ds(g * span, span)
        stores.append(pltpu.make_async_copy(out_ref.at[at], out_hbm.at[at], out_sem.at[g]))
        stores[-1].start()
    for copy in stores:
        copy.wait()


def encode_kernel(len_ref, hist_ref, gain_ref, wv_ref, wk_ref, out_ref, key_ref, value_ref):
    users, rows, dim = hist_ref.shape
    width = wk_ref.shape[1]
    first = pl.program_id(0) * users
    x = hist_ref[...].reshape(users * rows, dim).astype(F32)
    normed = (norm_rows(x) * gain_ref[...]).astype(BF16)
    keys = silu(mm(normed, wk_ref[...]))
    values = silu(mm(normed, wv_ref[...]))
    row_ids = iota((rows, width), 0)
    for u in range(users):
        live = row_ids < len_ref[first + u] * PIECE
        part = slice(u * rows, (u + 1) * rows)
        side = slice((u % 2) * rows, (u % 2 + 1) * rows)
        pair = slice((u // 2) * HDIM, (u // 2 + 1) * HDIM)
        key = jnp.where(live, keys[part], 0.0)
        value = jnp.where(live, values[part], 0.0).astype(BF16)
        out_ref[u, :, :width] = key.astype(BF16)
        out_ref[u, :, width:] = value
        for h in range(width // HDIM):
            cols = slice(h * HDIM, (h + 1) * HDIM)
            key_ref[h, pair, side] = key[:, cols].T.astype(BF16)
            value_ref[h, pair, side] = value[:, cols]


def own_kernel(n_grp, n_enc, cap, cand_ref, gain_ref, w_ref, owner_ref, u_ref, v_ref, aux_ref, slot_ref):
    step, width = u_ref.shape
    heads = width // HDIM
    i = pl.program_id(0)

    @pl.when(i == 0)
    def _():
        place = place_of(owner_ref[...], n_grp, n_enc)
        _, rank = ranks(place, n_grp * n_enc)
        slot = (place * cap + rank).astype(F32)
        slot_ref[...] = jnp.broadcast_to(slot, (128, slot.shape[1])).T

    normed = (norm_rows(cand_ref[...].astype(F32)) * gain_ref[...]).astype(BF16)

    def projected(part):
        return silu(mm(normed, w_ref[:, part * width : (part + 1) * width])).astype(BF16)

    u_ref[...] = projected(0)
    v_ref[...] = projected(1)
    prod = projected(2).astype(F32) * projected(3).astype(F32)
    lane = iota((step, 128), 1)
    aux = slot_ref[pl.ds(pl.multiple_of(i * step, step), step), :]
    for h in range(heads):
        score = jnp.sum(prod[:, h * HDIM : (h + 1) * HDIM], axis=-1, keepdims=True) * HDIM ** (-0.5)
        aux = jnp.where(lane == h, silu(score).astype(BF16).astype(F32), aux)
    aux_ref[...] = aux


def attend_kernel(
    cap, arrived_ref, k_hbm, v_hbm, out_hbm, k_ref, v_ref, out_ref, mask_ref, odd_ref, k_sem, v_sem, out_sem
):
    n_dev = arrived_ref.shape[0]
    heads = k_ref.shape[0]
    total = n_dev * cap
    pairs = k_ref.shape[1] // HDIM
    keys = [pltpu.make_async_copy(k_hbm.at[h], k_ref.at[h], k_sem.at[h]) for h in range(heads)]
    values = [pltpu.make_async_copy(v_hbm.at[h], v_ref.at[h], v_sem.at[h]) for h in range(heads)]
    for h in range(heads):
        keys[h].start()
        values[h].start()

    table = arrived_ref[:, heads * cap : heads * cap + 8, :].astype(F32)[:, 0:1, :]
    full = (n_dev, cap, 128)
    uid = jnp.where(iota(full, 1) == iota(full, 2), jnp.broadcast_to(table, full), 0.0)
    uid = jnp.broadcast_to(jnp.sum(uid, axis=2, keepdims=True), full).reshape(total, 128)
    pair = jnp.floor(uid * 0.5)
    odd_ref[...] = uid - 2.0 * pair
    for p in range(pairs):
        mask_ref[:, p * 128 : (p + 1) * 128] = one_hot(pair == 1.0 * p)

    def spread(x):
        return jnp.concatenate([x * mask_ref[:, p * 128 : (p + 1) * 128] for p in range(pairs)], axis=1)

    def chosen(x):
        return jnp.where(odd_ref[...] > 0.5, x[:, 128:], x[:, :128])

    def scores(h):
        query = arrived_ref[:, h * cap : (h + 1) * cap, :].astype(F32).reshape(total, HDIM).astype(BF16)
        keys[h].wait()
        return mm(spread(query), k_ref[h])

    stores = []
    score = scores(0)
    for h in range(heads):
        later = scores(h + 1) if h + 1 < heads else None
        weight = silu(chosen(score) * HDIM ** (-0.5)).astype(BF16)
        values[h].wait()
        attended = chosen(mm(spread(weight), v_ref[h]))
        out_ref[:, h * cap : (h + 1) * cap, :] = attended.reshape(n_dev, cap, HDIM).astype(BF16)
        at = (slice(None), pl.ds(h * cap, cap), slice(None))
        stores.append(pltpu.make_async_copy(out_ref.at[at], out_hbm.at[at], out_sem.at[h]))
        stores[-1].start()
        score = later
    for copy in stores:
        copy.wait()


def answer_kernel(back_ref, u_ref, v_ref, aux_ref, out_ref):
    count, width = u_ref.shape
    n_dev = back_ref.shape[0]
    heads = width // HDIM
    cap = back_ref.shape[1] // heads
    total = n_dev * cap
    back = [
        back_ref[:, h * cap : (h + 1) * cap, :].astype(F32).reshape(total, HDIM).astype(BF16) for h in range(heads)
    ]
    back = jnp.concatenate(back, axis=1)
    step = min(count, 128)
    for r in range(0, count, step):
        rows = slice(r, r + step)
        aux = aux_ref[rows, :]
        pick = one_hot(iota((step, total), 1) == aux[:, heads : heads + 1].astype(jnp.int32))
        own_v = v_ref[rows, :].astype(F32)
        own = [own_v[:, h * HDIM : (h + 1) * HDIM] * aux[:, h : h + 1] for h in range(heads)]
        normed = norm_rows(mm(pick, back) + jnp.concatenate(own, axis=1)).astype(BF16).astype(F32)
        out_ref[rows, :] = (normed * u_ref[rows, :].astype(F32)).astype(BF16)


def params():
    return pltpu.CompilerParams(vmem_limit_bytes=36 * 1024 * 1024)


def whole(shape):
    return pl.BlockSpec(shape, lambda *_: (0,) * len(shape))


def column(shape, index):
    return pl.BlockSpec(shape, lambda *_: (0, index))


def cost(flops, size):
    return pl.CostEstimate(flops=flops, bytes_accessed=size, transcendentals=0)


def in_hbm(x):
    return pltpu.with_memory_space_constraint(x, pltpu.HBM)


def in_vmem(x):
    return pltpu.with_memory_space_constraint(x, pltpu.VMEM)


def exchange(slots):
    return lax.all_to_all(slots, ("enc", "grp"), split_axis=0, concat_axis=0, tiled=True)


def body(history, hist_len, cand, cand_owner, cand_user, norm_gain, w_proj):
    users, rows, dim = history.shape
    width = w_proj.shape[1] // 4
    heads = width // HDIM
    count = cand.shape[0]
    n_grp, n_enc = lax.axis_size("grp"), lax.axis_size("enc")
    n_dev = n_grp * n_enc
    cap = -(-max(2, 3 * count // (2 * n_dev)) // 8) * 8
    total = n_dev * cap
    parts = 4
    shape = jax.ShapeDtypeStruct
    anywhere = pl.BlockSpec(memory_space=pl.ANY)
    dma = pltpu.SemaphoreType.DMA

    history, cand, w_proj = in_hbm(history), in_hbm(cand), in_hbm(w_proj)
    gain = in_hbm(norm_gain.reshape(1, dim))
    owner = in_hbm(cand_owner.reshape(1, count))
    user = in_hbm(cand_user.reshape(1, count))

    outgoing = pl.pallas_call(
        functools.partial(dispatch_kernel, n_grp, n_enc, cap),
        in_specs=[anywhere] * 5,
        out_specs=anywhere,
        out_shape=pltpu.HBM((n_dev, heads * cap + 8, HDIM), BF16),
        scratch_shapes=[
            pltpu.VMEM((count, dim), BF16),
            pltpu.VMEM((1, dim), F32),
            pltpu.VMEM((dim, width), BF16),
            pltpu.VMEM((1, count), jnp.int32),
            pltpu.VMEM((1, count), jnp.int32),
            pltpu.VMEM((n_dev, heads * cap + 8, HDIM), BF16),
            pltpu.VMEM((count, width), BF16),
            pltpu.VMEM((total, count), BF16),
            dma((3,)),
            dma((parts,)),
            dma((1,)),
            dma((parts,)),
        ],
        compiler_params=params(),
        cost_estimate=cost(2 * count * width * (dim + total), 4 << 20),
        name="dispatch",
    )(cand, gain, w_proj, owner, user)

    arrived = exchange(outgoing)

    span = 4
    kv_cache, keys, values = pl.pallas_call(
        encode_kernel,
        grid=(users // span,),
        in_specs=[
            pl.BlockSpec(memory_space=pltpu.SMEM),
            pl.BlockSpec((span, rows, dim), lambda i: (i, 0, 0)),
            whole((1, dim)),
            column((dim, width), 1),
            column((dim, width), 3),
        ],
        out_specs=[
            pl.BlockSpec((span, rows, 2 * width), lambda i: (i, 0, 0)),
            pl.BlockSpec((heads, span * HDIM // 2, 2 * rows), lambda i: (0, i, 0)),
            pl.BlockSpec((heads, span * rows // 2, 2 * HDIM), lambda i: (0, i, 0)),
        ],
        out_shape=[
            shape((users, rows, 2 * width), BF16),
            pltpu.HBM((heads, users * HDIM // 2, 2 * rows), BF16),
            pltpu.HBM((heads, users * rows // 2, 2 * HDIM), BF16),
        ],
        compiler_params=params(),
        cost_estimate=cost(2 * users * rows * dim * 2 * width, 12 << 20),
        name="encode",
    )(in_hbm(hist_len), history, gain, w_proj, w_proj)

    step = count // 2
    gate, own_v, aux = pl.pallas_call(
        functools.partial(own_kernel, n_grp, n_enc, cap),
        grid=(count // step,),
        in_specs=[
            pl.BlockSpec((step, dim), lambda i: (i, 0)),
            whole((1, dim)),
            whole((dim, 4 * width)),
            whole((1, count)),
        ],
        out_specs=[
            pl.BlockSpec((step, width), lambda i: (i, 0)),
            pl.BlockSpec((step, width), lambda i: (i, 0)),
            pl.BlockSpec((step, 128), lambda i: (i, 0)),
        ],
        out_shape=[shape((count, width), BF16), shape((count, width), BF16), shape((count, 128), F32)],
        scratch_shapes=[pltpu.VMEM((count, 128), F32)],
        compiler_params=params(),
        cost_estimate=cost(8 * count * dim * width, 6 << 20),
        name="own",
    )(cand, gain, w_proj, owner)

    kv_shape = (heads, users * HDIM // 2, 2 * rows)
    attended = pl.pallas_call(
        functools.partial(attend_kernel, cap),
        in_specs=[pl.BlockSpec(memory_space=pltpu.VMEM), anywhere, anywhere],
        out_specs=anywhere,
        out_shape=pltpu.HBM((n_dev, heads * cap, HDIM), BF16),
        scratch_shapes=[
            pltpu.VMEM(kv_shape, BF16),
            pltpu.VMEM(kv_shape, BF16),
            pltpu.VMEM((n_dev, heads * cap, HDIM), BF16),
            pltpu.VMEM((total, users * 64), BF16),
            pltpu.VMEM((total, 128), F32),
            dma((heads,)),
            dma((heads,)),
            dma((heads,)),
        ],
        compiler_params=params(),
        cost_estimate=cost(2 * total * rows * users * width * 2, 6 << 20),
        name="attend",
    )(in_vmem(arrived), in_hbm(keys), in_hbm(values))

    back = exchange(attended)

    cand_out = pl.pallas_call(
        answer_kernel,
        in_specs=[pl.BlockSpec(memory_space=pltpu.VMEM)] * 4,
        out_specs=pl.BlockSpec(memory_space=pltpu.VMEM),
        out_shape=shape((count, width), BF16),
        compiler_params=params(),
        cost_estimate=cost(2 * count * total * width, 4 << 20),
        name="answer",
    )(in_vmem(back), gate, own_v, aux)
    return (kv_cache, cand_out)


def solution(mesh):
    placed = (
        P(AXES, None, None),
        P(AXES),
        P(AXES, None),
        P(AXES, None),
        P(AXES),
        P(),
        P(),
    )
    return jax.shard_map(
        body,
        mesh=mesh,
        in_specs=placed,
        out_specs=(P(AXES, None, None), P(AXES, None)),
        check_vma=False,
    )
```

time: 71.6 us -> 69.6 us (0.972)
  waiting for transfers between devices: 24.6 us -> 27.2 us
  local copies, waits for them, and re-layouts: 1.83 us -> 0 us
  starting transfers between devices: 11.4 us -> 10.3 us
  Pallas kernels: 32.1 us -> 31.1 us
    all_to_all x2, waiting for transfers between devices: 24.6 us -> 27.2 us  [exchange(): lax.all_to_all(slots, ('enc', 'grp'), split_axis=0, concat_axis=0, tiled=...]
    unnamed x4 -> x0, local copies, waits for them, and re-layouts: 1.83 us -> none
    all_to_all x2, starting transfers between devices: 11.4 us -> 10.3 us  [exchange(): lax.all_to_all(slots, ('enc', 'grp'), split_axis=0, concat_axis=0, tiled=...]
    pallas_call x4, Pallas kernels: 22.8 us -> 21.8 us  [the longest x1 8.13 us: body(): pl.pallas_call(functools.partial(attend_kernel, cap), in_specs=[pl.BlockS...]
  transfers between devices with their start and end apart: 2 -> 2, of which waited for: 2 -> 2; matrix products, arithmetic and copies ran while one was open for 0% -> 0% of each run, Pallas kernels for 24% -> 23%
where the time goes in v3:
time: 69.6 us; the launch traced here: 69.3 us
  Pallas kernels  31.1 us (45%)
  waiting for transfers between devices  27.2 us (39%)
  starting transfers between devices  10.3 us (15%)
    all_to_all x2, waiting for transfers between devices, exchange(): lax.all_to_all(slots, ('enc', 'grp'), split_axis=0, concat_axis=0, tiled=...  27.2 us
    all_to_all x2, starting transfers between devices, exchange(): lax.all_to_all(slots, ('enc', 'grp'), split_axis=0, concat_axis=0, tiled=...  10.3 us
    pallas_call x1, Pallas kernels, body(): pl.pallas_call(encode_kernel, grid=(users // span,), in_specs=[pl.BlockSp...  9.28 us
    pallas_call x1, Pallas kernels, body(): pl.pallas_call(functools.partial(attend_kernel, cap), in_specs=[pl.BlockS...  8.13 us
    pallas_call x1, Pallas kernels, body(): pl.pallas_call(functools.partial(own_kernel, n_grp, n_enc, cap), grid=(co...  6.52 us
    pallas_call x1, Pallas kernels, body(): pl.pallas_call(functools.partial(dispatch_kernel, n_grp, n_enc, cap), in_...  4.83 us
    pallas_call x1, Pallas kernels, body(): pl.pallas_call(answer_kernel, in_specs=[pl.BlockSpec(memory_space=pltpu.V...  2.33 us
  transfers between devices with their start and end apart: 2, of which 2 were waited for; matrix products, arithmetic and copies ran while one was open for 0% of the time, Pallas kernels for 23%

profile of v3, /device:TPU:1, one launch (start us, length us, event | category | flops | bytes accessed | tf_op | source)
XLA Modules:
  0.0 69.3 jit_solution(13758517589716027239)
XLA Ops:
  0.6 4.8 %dispatch.1 = bf16[32,104,128]{2,1,0:T(8,128)(2,1)} custom-call(bf16[512,1024]{1,0:T(8,128)(2,1)} %cand_ref.1, f32[1,1024]{1,0:T(1,128)} %bitcast.3, bf16[1024,2048]{1,0:T(8,128)(2,1)} %w_ref.1, s32[1,512]{1,0:T(1,128)} %bitcast.7, s32[1,512]{1,0:T(1,128)} %bitcast.6), custom_call_target="tpu_custom_call" | custom-call | flops 939524096 | bytes 4194304 | tf_op jit(solution)/shard_map/dispatch/pallas_call | solution.py:279
  5.5 7.1 %all-to-all-start = ((bf16[32,104,128]{2,1,0:T(8,128)(2,1)}), bf16[32,104,128]{2,1,0:T(8,128)(2,1)S(1)}, u32[]{:S(2)}, u32[]{:S(2)}) async-start(bf16[32,104,128]{2,1,0:T(8,128)(2,1)} %dispatch.1), calls=%async_computation | async-start | bytes 1703936 | tf_op jit(solution)/shard_map/all_to_all | solution.py:257
  12.6 9.3 %encode.1 = (bf16[12,128,1024]{2,1,0:T(8,128)(2,1)}, bf16[4,768,256]{2,1,0:T(8,128)(2,1)}, bf16[4,768,256]{2,1,0:T(8,128)(2,1)}) custom-call(s32[12]{0:T(128)} %len_ref.1, bf16[12,128,1024]{2,1,0:T(8,128)(2,1)} %hist_ref.1, f32[1,1024]{1,0:T(1,128)} %bitcast.4, bf16[1024,2048]{1,0:T(8,128)(2,1)} %w_ref.1, bf16[1024,2048]{1,0:T(8,128)(2,1)} %w_ref.1), custom_call_target="tpu_custom_call" | custom-call | flops 3221225472 | bytes 12582912 | tf_op jit(solution)/shard_map/encode/pallas_call | solution.py:306
  21.9 12.9 %all-to-all-done.arrived_ref = bf16[32,104,128]{2,1,0:T(8,128)(2,1)S(1)} async-done(((bf16[32,104,128]{2,1,0:T(8,128)(2,1)}), bf16[32,104,128]{2,1,0:T(8,128)(2,1)S(1)}, u32[]{:S(2)}, u32[]{:S(2)}) %all-to-all-start) | async-done | bytes 852000 | tf_op jit(solution)/shard_map/all_to_all | solution.py:257
  34.8 8.1 %attend.1 = bf16[32,96,128]{2,1,0:T(8,128)(2,1)} custom-call(bf16[32,104,128]{2,1,0:T(8,128)(2,1)S(1)} %all-to-all-done.arrived_ref, bf16[4,768,256]{2,1,0:T(8,128)(2,1)} %get-tuple-element.9.k_hbm, bf16[4,768,256]{2,1,0:T(8,128)(2,1)} %get-tuple-element.10.v_hbm), custom_call_target="tpu_custom_call" | custom-call | flops 2415919104 | bytes 6291456 | tf_op jit(solution)/shard_map/attend/pallas_call | solution.py:354
  42.9 3.2 %all-to-all-start.1 = ((bf16[32,96,128]{2,1,0:T(8,128)(2,1)}), bf16[32,96,128]{2,1,0:T(8,128)(2,1)S(1)}, u32[]{:S(2)}, u32[]{:S(2)}) async-start(bf16[32,96,128]{2,1,0:T(8,128)(2,1)} %attend.1), calls=%async_computation.1 | async-start | bytes 1572864 | tf_op jit(solution)/shard_map/all_to_all | solution.py:257
  46.1 6.5 %own.1 = (bf16[512,512]{1,0:T(8,128)(2,1)S(1)}, bf16[512,512]{1,0:T(8,128)(2,1)S(1)}, f32[512,128]{1,0:T(8,128)S(1)}) custom-call(bf16[512,1024]{1,0:T(8,128)(2,1)} %cand_ref.1, f32[1,1024]{1,0:T(1,128)} %bitcast.5, bf16[1024,2048]{1,0:T(8,128)(2,1)} %w_ref.1, s32[1,512]{1,0:T(1,128)} %bitcast.8), custom_call_target="tpu_custom_call" | custom-call | flops 2147483648 | bytes 6291456 | tf_op jit(solution)/shard_map/own/pallas_call | solution.py:332
  52.6 14.3 %all-to-all-done.1.back_ref = bf16[32,96,128]{2,1,0:T(8,128)(2,1)S(1)} async-done(((bf16[32,96,128]{2,1,0:T(8,128)(2,1)}), bf16[32,96,128]{2,1,0:T(8,128)(2,1)S(1)}, u32[]{:S(2)}, u32[]{:S(2)}) %all-to-all-start.1) | async-done | bytes 786464 | tf_op jit(solution)/shard_map/all_to_all | solution.py:257
  66.9 2.3 %answer.1 = bf16[512,512]{1,0:T(8,128)(2,1)} custom-call(bf16[32,96,128]{2,1,0:T(8,128)(2,1)S(1)} %all-to-all-done.1.back_ref, bf16[512,512]{1,0:T(8,128)(2,1)S(1)} %get-tuple-element.11.u_ref, bf16[512,512]{1,0:T(8,128)(2,1)S(1)} %get-tuple-element.12.v_ref, f32[512,128]{1,0:T(8,128)S(1)} %get-tuple-element.13.aux_ref), custom_call_target="tpu_custom_call" | custom-call | flops 402653184 | bytes 4194304 | tf_op jit(solution)/shard_map/answer/pallas_call | solution.py:376
Async XLA Ops:
  5.5 29.3 %all-to-all-start = ((bf16[32,104,128]{2,1,0:T(8,128)(2,1)}), bf16[32,104,128]{2,1,0:T(8,128)(2,1)S(1)}, u32[]{:S(2)}, u32[]{:S(2)}) async-start(bf16[32,104,128]{2,1,0:T(8,128)(2,1)} %dispatch.1), calls=%async_computation | async-start | bytes 1703936 | tf_op jit(solution)/shard_map/all_to_all | solution.py:257
  42.9 24.0 %all-to-all-start.1 = ((bf16[32,96,128]{2,1,0:T(8,128)(2,1)}), bf16[32,96,128]{2,1,0:T(8,128)(2,1)S(1)}, u32[]{:S(2)}, u32[]{:S(2)}) async-start(bf16[32,96,128]{2,1,0:T(8,128)(2,1)} %attend.1), calls=%async_computation.1 | async-start | bytes 1572864 | tf_op jit(solution)/shard_map/all_to_all | solution.py:257

commit v4 on v3

--- a/solution.py
+++ b/solution.py
@@ -41,16 +41,19 @@
 def ranks(place, n_dev):
     count = place.shape[1]
     named = iota((n_dev, count), 0) == place
-    before = mm(one_hot(named), one_hot(iota((count, count), 0) < iota((count, count), 1)))
-    return named, jnp.sum(jnp.where(named, before, 0.0), axis=0, keepdims=True).astype(jnp.int32)
-
-
-def place_of(owner, n_grp, n_enc):
-    return lax.rem(owner, n_enc) * n_grp + lax.div(owner, n_enc)
+    hot = jnp.where(named, 1.0, 0.0)
+    upper = one_hot(iota((128, 128), 0) < iota((128, 128), 1))
+    carry, before = jnp.zeros((n_dev, 1), F32), []
+    for c in range(0, count, 128):
+        block = hot[:, c : c + 128]
+        before.append(mm(block.astype(BF16), upper) + carry)
+        carry = carry + jnp.sum(block, axis=1, keepdims=True)
+    rank = jnp.where(named, jnp.concatenate(before, axis=1), 0.0)
+    return named, jnp.sum(rank, axis=0, keepdims=True).astype(jnp.int32)
 
 
 def dispatch_kernel(
-    n_grp, n_enc, cap, cand_hbm, gain_hbm, w_hbm, owner_hbm, user_hbm, out_hbm,
+    cap, cand_hbm, gain_hbm, w_hbm, owner_hbm, user_hbm, out_hbm,
     cand_ref, gain_ref, wq_ref, owner_ref, user_ref, out_ref, q_ref, pick_ref, small_sem, cand_sem, w_sem, out_sem,
 ):
     n_dev = out_ref.shape[0]
@@ -77,20 +80,22 @@
         copy.start()
     for copy in small:
         copy.wait()
-    place = place_of(owner_ref[...], n_grp, n_enc)
+    place = owner_ref[...]
     named, rank = ranks(place, n_dev)
     pick_ref[...] = one_hot(iota((n_dev * cap, count), 0) == place * cap + rank)
     users = jnp.where(named, user_ref[...].astype(F32), 0.0).astype(BF16)
     table = lax.dot_general(users, one_hot(iota((128, count), 0) == rank), NT, preferred_element_type=F32)
     out_ref[:, heads * cap :, :] = jnp.broadcast_to(table[:, None, :], (n_dev, 8, 128)).astype(BF16)
+    for copy in loads:
+        copy.wait()
+    weights.wait()
     gain = gain_ref[...]
-    for i in range(parts):
-        rows = slice(i * step, (i + 1) * step)
-        loads[i].wait()
-        normed = (norm_rows(cand_ref[rows, :].astype(F32)) * gain).astype(BF16)
-        if i == 0:
-            weights.wait()
-        q_ref[rows, :] = silu(mm(normed, wq_ref[...])).astype(BF16)
+    for r in range(0, count, 256):
+        rows = slice(r, r + 256)
+        x = cand_ref[rows, :].astype(F32)
+        center = x - jnp.mean(x, axis=-1, keepdims=True)
+        scale = lax.rsqrt(jnp.mean(center * center, axis=-1, keepdims=True) + 1e-05)
+        q_ref[rows, :] = silu(mm((center * gain).astype(BF16), wq_ref[...]) * scale).astype(BF16)
     stores = []
     groups = out_sem.shape[0]
     span = n_dev // groups
@@ -131,15 +136,15 @@
             value_ref[h, pair, side] = value[:, cols]
 
 
-def own_kernel(n_grp, n_enc, cap, cand_ref, gain_ref, w_ref, owner_ref, u_ref, v_ref, aux_ref, slot_ref):
+def own_kernel(n_dev, cap, cand_ref, gain_ref, w_ref, owner_ref, u_ref, v_ref, aux_ref, slot_ref):
     step, width = u_ref.shape
     heads = width // HDIM
     i = pl.program_id(0)
 
     @pl.when(i == 0)
     def _():
-        place = place_of(owner_ref[...], n_grp, n_enc)
-        _, rank = ranks(place, n_grp * n_enc)
+        place = owner_ref[...]
+        _, rank = ranks(place, n_dev)
         slot = (place * cap + rank).astype(F32)
         slot_ref[...] = jnp.broadcast_to(slot, (128, slot.shape[1])).T
 
@@ -163,23 +168,30 @@
     cap, arrived_ref, k_hbm, v_hbm, out_hbm, k_ref, v_ref, out_ref, mask_ref, odd_ref, k_sem, v_sem, out_sem
 ):
     n_dev = arrived_ref.shape[0]
-    heads = k_ref.shape[0]
+    heads, depth = k_ref.shape[0], k_ref.shape[1]
     total = n_dev * cap
-    pairs = k_ref.shape[1] // HDIM
-    keys = [pltpu.make_async_copy(k_hbm.at[h], k_ref.at[h], k_sem.at[h]) for h in range(heads)]
-    values = [pltpu.make_async_copy(v_hbm.at[h], v_ref.at[h], v_sem.at[h]) for h in range(heads)]
-    for h in range(heads):
-        keys[h].start()
-        values[h].start()
-
+    pairs = depth // HDIM
+    groups = k_sem.shape[0]
+    each = heads // groups
+
+    def load(hbm, ref, sem, g):
+        at = pl.ds(g * each, each)
+        return pltpu.make_async_copy(hbm.at[at], ref.at[at], sem.at[g])
+
+    for g in range(groups):
+        load(k_hbm, k_ref, k_sem, g).start()
+        load(v_hbm, v_ref, v_sem, g).start()
+
+    full = (n_dev, cap, 128)
     table = arrived_ref[:, heads * cap : heads * cap + 8, :].astype(F32)[:, 0:1, :]
-    full = (n_dev, cap, 128)
-    uid = jnp.where(iota(full, 1) == iota(full, 2), jnp.broadcast_to(table, full), 0.0)
-    uid = jnp.broadcast_to(jnp.sum(uid, axis=2, keepdims=True), full).reshape(total, 128)
+    own = jnp.where(iota(full, 1) == iota(full, 2), jnp.broadcast_to(table, full), 0.0)
+    uid = mm(own.reshape(total, 128).astype(BF16), jnp.ones((128, 128), BF16))
     pair = jnp.floor(uid * 0.5)
     odd_ref[...] = uid - 2.0 * pair
+    pair = pair.astype(BF16)
     for p in range(pairs):
-        mask_ref[:, p * 128 : (p + 1) * 128] = one_hot(pair == 1.0 * p)
+        hit = pair == jnp.asarray(1.0 * p, BF16)
+        mask_ref[:, p * 128 : (p + 1) * 128] = jnp.where(hit, jnp.ones((), BF16), jnp.zeros((), BF16))
 
     def spread(x):
         return jnp.concatenate([x * mask_ref[:, p * 128 : (p + 1) * 128] for p in range(pairs)], axis=1)
@@ -187,46 +199,36 @@
     def chosen(x):
         return jnp.where(odd_ref[...] > 0.5, x[:, 128:], x[:, :128])
 
-    def scores(h):
-        query = arrived_ref[:, h * cap : (h + 1) * cap, :].astype(F32).reshape(total, HDIM).astype(BF16)
-        keys[h].wait()
-        return mm(spread(query), k_ref[h])
-
-    stores = []
-    score = scores(0)
-    for h in range(heads):
-        later = scores(h + 1) if h + 1 < heads else None
-        weight = silu(chosen(score) * HDIM ** (-0.5)).astype(BF16)
-        values[h].wait()
-        attended = chosen(mm(spread(weight), v_ref[h]))
-        out_ref[:, h * cap : (h + 1) * cap, :] = attended.reshape(n_dev, cap, HDIM).astype(BF16)
-        at = (slice(None), pl.ds(h * cap, cap), slice(None))
-        stores.append(pltpu.make_async_copy(out_ref.at[at], out_hbm.at[at], out_sem.at[h]))
-        stores[-1].start()
-        score = later
-    for copy in stores:
-        copy.wait()
+    @pl.loop(0, groups)
+    def _(g):
+        members = [g * each + t for t in range(each)]
+        load(k_hbm, k_ref, k_sem, g).wait()
+        load(v_hbm, v_ref, v_sem, g).wait()
+        scores = []
+        for h in members:
+            rows = pl.ds(pl.multiple_of(h * cap, cap), cap)
+            query = arrived_ref[:, rows, :].astype(F32).reshape(total, HDIM).astype(BF16)
+            scores.append(mm(spread(query), k_ref[h]))
+        weights = [silu(chosen(score) * HDIM ** (-0.5)).astype(BF16) for score in scores]
+        for h, weight in zip(members, weights):
+            cols = pl.ds(pl.multiple_of(h * HDIM, HDIM), HDIM)
+            out_ref[:, cols] = chosen(mm(spread(weight), v_ref[h])).astype(BF16)
+
+    copy = pltpu.make_async_copy(out_ref, out_hbm, out_sem.at[0])
+    copy.start()
+    copy.wait()
 
 
 def answer_kernel(back_ref, u_ref, v_ref, aux_ref, out_ref):
-    count, width = u_ref.shape
-    n_dev = back_ref.shape[0]
+    width = u_ref.shape[1]
+    total = back_ref.shape[0]
     heads = width // HDIM
-    cap = back_ref.shape[1] // heads
-    total = n_dev * cap
-    back = [
-        back_ref[:, h * cap : (h + 1) * cap, :].astype(F32).reshape(total, HDIM).astype(BF16) for h in range(heads)
-    ]
-    back = jnp.concatenate(back, axis=1)
-    step = min(count, 128)
-    for r in range(0, count, step):
-        rows = slice(r, r + step)
-        aux = aux_ref[rows, :]
-        pick = one_hot(iota((step, total), 1) == aux[:, heads : heads + 1].astype(jnp.int32))
-        own_v = v_ref[rows, :].astype(F32)
-        own = [own_v[:, h * HDIM : (h + 1) * HDIM] * aux[:, h : h + 1] for h in range(heads)]
-        normed = norm_rows(mm(pick, back) + jnp.concatenate(own, axis=1)).astype(BF16).astype(F32)
-        out_ref[rows, :] = (normed * u_ref[rows, :].astype(F32)).astype(BF16)
+    aux = aux_ref[...]
+    pick = one_hot(iota((aux.shape[0], total), 1) == aux[:, heads : heads + 1].astype(jnp.int32))
+    own_v = v_ref[...].astype(F32)
+    own = [own_v[:, h * HDIM : (h + 1) * HDIM] * aux[:, h : h + 1] for h in range(heads)]
+    normed = norm_rows(mm(pick, back_ref[...]) + jnp.concatenate(own, axis=1))
+    out_ref[...] = normed.astype(BF16) * u_ref[...]
 
 
 def params():
@@ -254,7 +256,7 @@
 
 
 def exchange(slots):
-    return lax.all_to_all(slots, ("enc", "grp"), split_axis=0, concat_axis=0, tiled=True)
+    return lax.all_to_all(slots, AXES, split_axis=0, concat_axis=0, tiled=True)
 
 
 def body(history, hist_len, cand, cand_owner, cand_user, norm_gain, w_proj):
@@ -262,8 +264,7 @@
     width = w_proj.shape[1] // 4
     heads = width // HDIM
     count = cand.shape[0]
-    n_grp, n_enc = lax.axis_size("grp"), lax.axis_size("enc")
-    n_dev = n_grp * n_enc
+    n_dev = lax.axis_size("grp") * lax.axis_size("enc")
     cap = -(-max(2, 3 * count // (2 * n_dev)) // 8) * 8
     total = n_dev * cap
     parts = 4
@@ -277,7 +278,7 @@
     user = in_hbm(cand_user.reshape(1, count))
 
     outgoing = pl.pallas_call(
-        functools.partial(dispatch_kernel, n_grp, n_enc, cap),
+        functools.partial(dispatch_kernel, cap),
         in_specs=[anywhere] * 5,
         out_specs=anywhere,
         out_shape=pltpu.HBM((n_dev, heads * cap + 8, HDIM), BF16),
@@ -293,7 +294,7 @@
             dma((3,)),
             dma((parts,)),
             dma((1,)),
-            dma((parts,)),
+            dma((1,)),
         ],
         compiler_params=params(),
         cost_estimate=cost(2 * count * width * (dim + total), 4 << 20),
@@ -330,7 +331,7 @@
 
     step = count // 2
     gate, own_v, aux = pl.pallas_call(
-        functools.partial(own_kernel, n_grp, n_enc, cap),
+        functools.partial(own_kernel, n_dev, cap),
         grid=(count // step,),
         in_specs=[
             pl.BlockSpec((step, dim), lambda i: (i, 0)),
@@ -355,23 +356,23 @@
         functools.partial(attend_kernel, cap),
         in_specs=[pl.BlockSpec(memory_space=pltpu.VMEM), anywhere, anywhere],
         out_specs=anywhere,
-        out_shape=pltpu.HBM((n_dev, heads * cap, HDIM), BF16),
+        out_shape=pltpu.HBM((total, width), BF16),
         scratch_shapes=[
             pltpu.VMEM(kv_shape, BF16),
             pltpu.VMEM(kv_shape, BF16),
-            pltpu.VMEM((n_dev, heads * cap, HDIM), BF16),
+            pltpu.VMEM((total, width), BF16),
             pltpu.VMEM((total, users * 64), BF16),
             pltpu.VMEM((total, 128), F32),
-            dma((heads,)),
-            dma((heads,)),
-            dma((heads,)),
+            dma((heads // 2,)),
+            dma((heads // 2,)),
+            dma((1,)),
         ],
         compiler_params=params(),
         cost_estimate=cost(2 * total * rows * users * width * 2, 6 << 20),
         name="attend",
     )(in_vmem(arrived), in_hbm(keys), in_hbm(values))
 
-    back = exchange(attended)
+    back = exchange(attended.reshape(n_dev, cap, width)).reshape(total, width)
 
     cand_out = pl.pallas_call(
         answer_kernel,

time: 69.6 us -> 65.4 us (0.940)
  Pallas kernels: 31.1 us -> 26.6 us
  waiting for transfers between devices: 27.2 us -> 25.7 us
  starting transfers between devices: 10.3 us -> 11.4 us
    pallas_call x1, Pallas kernels: 8.13 us -> 5.25 us  [body(): pl.pallas_call(functools.partial(attend_kernel, cap), in_specs=[pl.BlockS...]
    all_to_all x2, waiting for transfers between devices: 27.2 us -> 25.7 us  [exchange(): return lax.all_to_all(slots, AXES, split_axis=0, concat_axis=0, tiled=True)]
    all_to_all x2, starting transfers between devices: 10.3 us -> 11.4 us  [exchange(): return lax.all_to_all(slots, AXES, split_axis=0, concat_axis=0, tiled=True)]
    pallas_call x2, Pallas kernels: 11.3 us -> 10.5 us  [the longest x1 6.48 us: body(): pl.pallas_call(functools.partial(own_kernel, n_dev, cap), grid=(count //...]
  transfers between devices with their start and end apart: 2 -> 2, of which waited for: 2 -> 2; matrix products, arithmetic and copies ran while one was open for 0% -> 0% of each run, Pallas kernels for 23% -> 24%
where the time goes in v4:
time: 65.4 us; the launch traced here: 64.5 us
  Pallas kernels  26.6 us (41%)
  waiting for transfers between devices  25.7 us (39%)
  starting transfers between devices  11.4 us (17%)
  between operations  0.67 us (1%)
    all_to_all x2, waiting for transfers between devices, exchange(): return lax.all_to_all(slots, AXES, split_axis=0, concat_axis=0, tiled=True)  25.7 us
    all_to_all x2, starting transfers between devices, exchange(): return lax.all_to_all(slots, AXES, split_axis=0, concat_axis=0, tiled=True)  11.4 us
    pallas_call x1, Pallas kernels, body(): pl.pallas_call(encode_kernel, grid=(users // span,), in_specs=[pl.BlockSp...  9.28 us
    pallas_call x1, Pallas kernels, body(): pl.pallas_call(functools.partial(own_kernel, n_dev, cap), grid=(count //...  6.48 us
    pallas_call x1, Pallas kernels, body(): pl.pallas_call(functools.partial(attend_kernel, cap), in_specs=[pl.BlockS...  5.25 us
    pallas_call x1, Pallas kernels, body(): pl.pallas_call(functools.partial(dispatch_kernel, cap), in_specs=[anywher...  3.98 us
    pallas_call x1, Pallas kernels, body(): pl.pallas_call(answer_kernel, in_specs=[pl.BlockSpec(memory_space=pltpu.V...  1.66 us
  transfers between devices with their start and end apart: 2, of which 2 were waited for; matrix products, arithmetic and copies ran while one was open for 0% of the time, Pallas kernels for 24%

profile of v4, /device:TPU:1, one launch (start us, length us, event | category | flops | bytes accessed | tf_op | source)
XLA Modules:
  0.0 64.5 jit_solution(5416088211610589338)
XLA Ops:
  0.6 4.0 %dispatch.1 = bf16[32,104,128]{2,1,0:T(8,128)(2,1)} custom-call(bf16[512,1024]{1,0:T(8,128)(2,1)} %cand_ref.1, f32[1,1024]{1,0:T(1,128)} %bitcast.7, bf16[1024,2048]{1,0:T(8,128)(2,1)} %w_ref.1, s32[1,512]{1,0:T(1,128)} %bitcast.11, s32[1,512]{1,0:T(1,128)} %bitcast.10), custom_call_target="tpu_custom_call" | custom-call | flops 939524096 | bytes 4194304 | tf_op jit(solution)/shard_map/dispatch/pallas_call | solution.py:280
  4.6 7.1 %all-to-all-start = ((bf16[32,104,128]{2,1,0:T(8,128)(2,1)}), bf16[32,104,128]{2,1,0:T(8,128)(2,1)S(1)}, u32[]{:S(2)}, u32[]{:S(2)}) async-start(bf16[32,104,128]{2,1,0:T(8,128)(2,1)} %dispatch.1), calls=%async_computation | async-start | bytes 1703936 | tf_op jit(solution)/shard_map/all_to_all | solution.py:259
  11.7 9.3 %encode.1 = (bf16[12,128,1024]{2,1,0:T(8,128)(2,1)}, bf16[4,768,256]{2,1,0:T(8,128)(2,1)}, bf16[4,768,256]{2,1,0:T(8,128)(2,1)}) custom-call(s32[12]{0:T(128)} %len_ref.1, bf16[12,128,1024]{2,1,0:T(8,128)(2,1)} %hist_ref.1, f32[1,1024]{1,0:T(1,128)} %bitcast.8, bf16[1024,2048]{1,0:T(8,128)(2,1)} %w_ref.1, bf16[1024,2048]{1,0:T(8,128)(2,1)} %w_ref.1), custom_call_target="tpu_custom_call" | custom-call | flops 3221225472 | bytes 12582912 | tf_op jit(solution)/shard_map/encode/pallas_call | solution.py:307
  21.0 12.1 %all-to-all-done.arrived_ref = bf16[32,104,128]{2,1,0:T(8,128)(2,1)S(1)} async-done(((bf16[32,104,128]{2,1,0:T(8,128)(2,1)}), bf16[32,104,128]{2,1,0:T(8,128)(2,1)S(1)}, u32[]{:S(2)}, u32[]{:S(2)}) %all-to-all-start) | async-done | bytes 852000 | tf_op jit(solution)/shard_map/all_to_all | solution.py:259
  33.1 5.2 %attend.1 = bf16[768,512]{1,0:T(8,128)(2,1)} custom-call(bf16[32,104,128]{2,1,0:T(8,128)(2,1)S(1)} %all-to-all-done.arrived_ref, bf16[4,768,256]{2,1,0:T(8,128)(2,1)} %get-tuple-element.9.k_hbm, bf16[4,768,256]{2,1,0:T(8,128)(2,1)} %get-tuple-element.10.v_hbm), custom_call_target="tpu_custom_call" | custom-call | flops 2415919104 | bytes 6291456 | tf_op jit(solution)/shard_map/attend/pallas_call | solution.py:355
  38.3 4.3 %all-to-all-start.1 = ((bf16[32,24,512]{2,1,0:T(8,128)(2,1)}), bf16[32,24,512]{2,1,0:T(8,128)(2,1)S(1)}, u32[]{:S(2)}, u32[]{:S(2)}) async-start(bf16[32,24,512]{2,1,0:T(8,128)(2,1)} %bitcast.6), calls=%async_computation.1 | async-start | bytes 1572864 | tf_op jit(solution)/shard_map/all_to_all | solution.py:259
  42.6 6.5 %own.1 = (bf16[512,512]{1,0:T(8,128)(2,1)S(1)}, bf16[512,512]{1,0:T(8,128)(2,1)S(1)}, f32[512,128]{1,0:T(8,128)S(1)}) custom-call(bf16[512,1024]{1,0:T(8,128)(2,1)} %cand_ref.1, f32[1,1024]{1,0:T(1,128)} %bitcast.9, bf16[1024,2048]{1,0:T(8,128)(2,1)} %w_ref.1, s32[1,512]{1,0:T(1,128)} %bitcast.12), custom_call_target="tpu_custom_call" | custom-call | flops 2147483648 | bytes 6291456 | tf_op jit(solution)/shard_map/own/pallas_call | solution.py:333
  49.1 13.7 %all-to-all-done.1 = bf16[32,24,512]{2,1,0:T(8,128)(2,1)S(1)} async-done(((bf16[32,24,512]{2,1,0:T(8,128)(2,1)}), bf16[32,24,512]{2,1,0:T(8,128)(2,1)S(1)}, u32[]{:S(2)}, u32[]{:S(2)}) %all-to-all-start.1) | async-done | bytes 786464 | tf_op jit(solution)/shard_map/all_to_all | solution.py:259
  62.8 1.7 %answer.1 = bf16[512,512]{1,0:T(8,128)(2,1)} custom-call(bf16[768,512]{1,0:T(8,128)(2,1)S(1)} %bitcast.5, bf16[512,512]{1,0:T(8,128)(2,1)S(1)} %get-tuple-element.11.u_ref, bf16[512,512]{1,0:T(8,128)(2,1)S(1)} %get-tuple-element.12.v_ref, f32[512,128]{1,0:T(8,128)S(1)} %get-tuple-element.13.aux_ref), custom_call_target="tpu_custom_call" | custom-call | flops 402653184 | bytes 4194304 | tf_op jit(solution)/shard_map/answer/pallas_call | solution.py:377
Async XLA Ops:
  4.6 28.4 %all-to-all-start = ((bf16[32,104,128]{2,1,0:T(8,128)(2,1)}), bf16[32,104,128]{2,1,0:T(8,128)(2,1)S(1)}, u32[]{:S(2)}, u32[]{:S(2)}) async-start(bf16[32,104,128]{2,1,0:T(8,128)(2,1)} %dispatch.1), calls=%async_computation | async-start | bytes 1703936 | tf_op jit(solution)/shard_map/all_to_all | solution.py:259
  38.3 24.5 %all-to-all-start.1 = ((bf16[32,24,512]{2,1,0:T(8,128)(2,1)}), bf16[32,24,512]{2,1,0:T(8,128)(2,1)S(1)}, u32[]{:S(2)}, u32[]{:S(2)}) async-start(bf16[32,24,512]{2,1,0:T(8,128)(2,1)} %bitcast.6), calls=%async_computation.1 | async-start | bytes 1572864 | tf_op jit(solution)/shard_map/all_to_all | solution.py:259

commit v5 on v4

--- a/solution.py
+++ b/solution.py
@@ -136,7 +136,7 @@
             value_ref[h, pair, side] = value[:, cols]
 
 
-def own_kernel(n_dev, cap, cand_ref, gain_ref, w_ref, owner_ref, u_ref, v_ref, aux_ref, slot_ref):
+def own_kernel(n_dev, cap, me_ref, cand_ref, gain_ref, w_ref, owner_ref, u_ref, v_ref, aux_ref, slot_ref):
     step, width = u_ref.shape
     heads = width // HDIM
     i = pl.program_id(0)
@@ -145,7 +145,7 @@
     def _():
         place = owner_ref[...]
         _, rank = ranks(place, n_dev)
-        slot = (place * cap + rank).astype(F32)
+        slot = ((place ^ me_ref[0]) * cap + rank).astype(F32)
         slot_ref[...] = jnp.broadcast_to(slot, (128, slot.shape[1])).T
 
     normed = (norm_rows(cand_ref[...].astype(F32)) * gain_ref[...]).astype(BF16)
@@ -164,9 +164,8 @@
     aux_ref[...] = aux
 
 
-def attend_kernel(
-    cap, arrived_ref, k_hbm, v_hbm, out_hbm, k_ref, v_ref, out_ref, mask_ref, odd_ref, k_sem, v_sem, out_sem
-):
+def attend_kernel(cap, n_out, me_ref, arrived_ref, k_hbm, v_hbm, *refs):
+    out_hbm, (k_ref, v_ref, out_ref, mask_ref, odd_ref, k_sem, v_sem, out_sem) = refs[:n_out], refs[n_out:]
     n_dev = arrived_ref.shape[0]
     heads, depth = k_ref.shape[0], k_ref.shape[1]
     total = n_dev * cap
@@ -212,22 +211,32 @@
         weights = [silu(chosen(score) * HDIM ** (-0.5)).astype(BF16) for score in scores]
         for h, weight in zip(members, weights):
             cols = pl.ds(pl.multiple_of(h * HDIM, HDIM), HDIM)
-            out_ref[:, cols] = chosen(mm(spread(weight), v_ref[h])).astype(BF16)
-
-    copy = pltpu.make_async_copy(out_ref, out_hbm, out_sem.at[0])
-    copy.start()
-    copy.wait()
-
-
-def answer_kernel(back_ref, u_ref, v_ref, aux_ref, out_ref):
+            attended = chosen(mm(spread(weight), v_ref[h]))
+            out_ref[:, :, cols] = attended.reshape(n_dev, cap, HDIM).astype(BF16)
+
+    if n_out == 1:
+        stores = [pltpu.make_async_copy(out_ref, out_hbm[0], out_sem.at[0])]
+    else:
+        stores = [
+            pltpu.make_async_copy(out_ref.at[me_ref[0] ^ k], out_hbm[k], out_sem.at[k]) for k in range(n_out)
+        ]
+    for copy in stores:
+        copy.start()
+    for copy in stores:
+        copy.wait()
+
+
+def answer_kernel(n_back, *refs):
+    back_refs, (u_ref, v_ref, aux_ref, out_ref) = refs[:n_back], refs[n_back:]
     width = u_ref.shape[1]
-    total = back_ref.shape[0]
     heads = width // HDIM
+    back = jnp.concatenate([ref[...].astype(F32).reshape(-1, width) for ref in back_refs], axis=0).astype(BF16)
+    total = back.shape[0]
     aux = aux_ref[...]
     pick = one_hot(iota((aux.shape[0], total), 1) == aux[:, heads : heads + 1].astype(jnp.int32))
     own_v = v_ref[...].astype(F32)
     own = [own_v[:, h * HDIM : (h + 1) * HDIM] * aux[:, h : h + 1] for h in range(heads)]
-    normed = norm_rows(mm(pick, back_ref[...]) + jnp.concatenate(own, axis=1))
+    normed = norm_rows(mm(pick, back) + jnp.concatenate(own, axis=1))
     out_ref[...] = normed.astype(BF16) * u_ref[...]
 
 
@@ -257,6 +266,10 @@
 
 def exchange(slots):
     return lax.all_to_all(slots, AXES, split_axis=0, concat_axis=0, tiled=True)
+
+
+def swap(x, k, n_dev):
+    return lax.ppermute(x, AXES, [(i, i ^ k) for i in range(n_dev)])
 
 
 def body(history, hist_len, cand, cand_owner, cand_user, norm_gain, w_proj):
@@ -268,6 +281,11 @@
     cap = -(-max(2, 3 * count // (2 * n_dev)) // 8) * 8
     total = n_dev * cap
     parts = 4
+    direct = n_dev <= 32
+    n_out = n_dev if direct else 1
+    me = (lax.axis_index("grp") * lax.axis_size("enc") + lax.axis_index("enc")).astype(jnp.int32).reshape(1)
+    me = me if direct else jnp.zeros_like(me)
+    scalar = pl.BlockSpec(memory_space=pltpu.SMEM)
     shape = jax.ShapeDtypeStruct
     anywhere = pl.BlockSpec(memory_space=pl.ANY)
     dma = pltpu.SemaphoreType.DMA
@@ -334,6 +352,7 @@
         functools.partial(own_kernel, n_dev, cap),
         grid=(count // step,),
         in_specs=[
+            scalar,
             pl.BlockSpec((step, dim), lambda i: (i, 0)),
             whole((1, dim)),
             whole((dim, 4 * width)),
@@ -349,40 +368,44 @@
         compiler_params=params(),
         cost_estimate=cost(8 * count * dim * width, 6 << 20),
         name="own",
-    )(cand, gain, w_proj, owner)
+    )(me, cand, gain, w_proj, owner)
 
     kv_shape = (heads, users * HDIM // 2, 2 * rows)
     attended = pl.pallas_call(
-        functools.partial(attend_kernel, cap),
-        in_specs=[pl.BlockSpec(memory_space=pltpu.VMEM), anywhere, anywhere],
-        out_specs=anywhere,
-        out_shape=pltpu.HBM((total, width), BF16),
+        functools.partial(attend_kernel, cap, n_out),
+        in_specs=[scalar, pl.BlockSpec(memory_space=pltpu.VMEM), anywhere, anywhere],
+        out_specs=[anywhere] * n_out,
+        out_shape=[pltpu.HBM((cap, width) if direct else (n_dev, cap, width), BF16)] * n_out,
         scratch_shapes=[
             pltpu.VMEM(kv_shape, BF16),
             pltpu.VMEM(kv_shape, BF16),
-            pltpu.VMEM((total, width), BF16),
+            pltpu.VMEM((n_dev, cap, width), BF16),
             pltpu.VMEM((total, users * 64), BF16),
             pltpu.VMEM((total, 128), F32),
             dma((heads // 2,)),
             dma((heads // 2,)),
-            dma((1,)),
+            dma((n_out,)),
         ],
         compiler_params=params(),
         cost_estimate=cost(2 * total * rows * users * width * 2, 6 << 20),
         name="attend",
-    )(in_vmem(arrived), in_hbm(keys), in_hbm(values))
-
-    back = exchange(attended.reshape(n_dev, cap, width)).reshape(total, width)
+    )(me, in_vmem(arrived), in_hbm(keys), in_hbm(values))
+
+    if direct:
+        back = {k: swap(attended[k], k, n_dev) for k in range(n_dev - 1, 0, -1)}
+        back = [attended[0]] + [back[k] for k in range(1, n_dev)]
+    else:
+        back = [exchange(attended[0])]
 
     cand_out = pl.pallas_call(
-        answer_kernel,
-        in_specs=[pl.BlockSpec(memory_space=pltpu.VMEM)] * 4,
+        functools.partial(answer_kernel, n_out),
+        in_specs=[pl.BlockSpec(memory_space=pltpu.VMEM)] * (n_out + 3),
         out_specs=pl.BlockSpec(memory_space=pltpu.VMEM),
         out_shape=shape((count, width), BF16),
         compiler_params=params(),
         cost_estimate=cost(2 * count * total * width, 4 << 20),
         name="answer",
-    )(in_vmem(back), gate, own_v, aux)
+    )(*[in_vmem(x) for x in back], gate, own_v, aux)
     return (kv_cache, cand_out)
 
 

time: 65.4 us -> 97.3 us (1.49)
  starting transfers between devices: 11.4 us -> 56.3 us
  waiting for transfers between devices: 25.7 us -> 12.6 us
    ppermute x0 -> x31, starting transfers between devices: none -> 49.2 us  [swap(): return lax.ppermute(x, AXES, [(i, i ^ k) for i in range(n_dev)])]
    all_to_all x2 -> x1, waiting for transfers between devices: 25.7 us -> 12.1 us  [exchange(): return lax.all_to_all(slots, AXES, split_axis=0, concat_axis=0, tiled=True)]
    all_to_all x2 -> x1, starting transfers between devices: 11.4 us -> 7.1 us  [exchange(): return lax.all_to_all(slots, AXES, split_axis=0, concat_axis=0, tiled=True)]
  transfers between devices with their start and end apart: 2 -> 32, of which waited for: 2 -> 2; matrix products, arithmetic and copies ran while one was open for 0% -> 0% of each run, Pallas kernels for 24% -> 16%
where the time goes in v5:
time: 97.3 us; the launch traced here: 96.9 us
  starting transfers between devices  56.3 us (58%)
  Pallas kernels  27.2 us (28%)
  waiting for transfers between devices  12.6 us (13%)
    ppermute x31, starting transfers between devices, swap(): return lax.ppermute(x, AXES, [(i, i ^ k) for i in range(n_dev)])  49.2 us
    all_to_all x1, waiting for transfers between devices, exchange(): return lax.all_to_all(slots, AXES, split_axis=0, concat_axis=0, tiled=True)  12.1 us
    pallas_call x1, Pallas kernels, body(): pl.pallas_call(encode_kernel, grid=(users // span,), in_specs=[pl.BlockSp...  9.28 us
    all_to_all x1, starting transfers between devices, exchange(): return lax.all_to_all(slots, AXES, split_axis=0, concat_axis=0, tiled=True)  7.1 us
    pallas_call x1, Pallas kernels, body(): pl.pallas_call(functools.partial(own_kernel, n_dev, cap), grid=(count //...  6.46 us
    pallas_call x1, Pallas kernels, body(): pl.pallas_call(functools.partial(attend_kernel, cap, n_out), in_specs=[sc...  5.79 us
    pallas_call x1, Pallas kernels, body(): pl.pallas_call(functools.partial(dispatch_kernel, cap), in_specs=[anywher...  3.97 us
  transfers between devices with their start and end apart: 32, of which 2 were waited for; matrix products, arithmetic and copies ran while one was open for 0% of the time, Pallas kernels for 16%

profile of v5, /device:TPU:1, one launch (start us, length us, event | category | flops | bytes accessed | tf_op | source)
XLA Modules:
  0.0 96.9 jit_solution(4746900925166553345)
XLA Ops:
  0.6 4.0 %dispatch.1 = bf16[32,104,128]{2,1,0:T(8,128)(2,1)} custom-call(bf16[512,1024]{1,0:T(8,128)(2,1)} %cand_ref.1, f32[1,1024]{1,0:T(1,128)} %bitcast.4, bf16[1024,2048]{1,0:T(8,128)(2,1)} %w_ref.1, s32[1,512]{1,0:T(1,128)} %bitcast.8, s32[1,512]{1,0:T(1,128)} %bitcast.7), custom_call_target="tpu_custom_call" | custom-call | flops 939524096 | bytes 4194304 | tf_op jit(solution)/shard_map/dispatch/pallas_call | solution.py:298
  4.6 7.1 %all-to-all-start = ((bf16[32,104,128]{2,1,0:T(8,128)(2,1)}), bf16[32,104,128]{2,1,0:T(8,128)(2,1)S(1)}, u32[]{:S(2)}, u32[]{:S(2)}) async-start(bf16[32,104,128]{2,1,0:T(8,128)(2,1)} %dispatch.1), calls=%async_computation | async-start | bytes 1703936 | tf_op jit(solution)/shard_map/all_to_all | solution.py:268
  11.7 9.3 %encode.1 = (bf16[12,128,1024]{2,1,0:T(8,128)(2,1)}, bf16[4,768,256]{2,1,0:T(8,128)(2,1)}, bf16[4,768,256]{2,1,0:T(8,128)(2,1)}) custom-call(s32[12]{0:T(128)} %len_ref.1, bf16[12,128,1024]{2,1,0:T(8,128)(2,1)} %hist_ref.1, f32[1,1024]{1,0:T(1,128)} %bitcast.5, bf16[1024,2048]{1,0:T(8,128)(2,1)} %w_ref.1, bf16[1024,2048]{1,0:T(8,128)(2,1)} %w_ref.1), custom_call_target="tpu_custom_call" | custom-call | flops 3221225472 | bytes 12582912 | tf_op jit(solution)/shard_map/encode/pallas_call | solution.py:325
  21.0 12.1 %all-to-all-done.arrived_ref = bf16[32,104,128]{2,1,0:T(8,128)(2,1)S(1)} async-done(((bf16[32,104,128]{2,1,0:T(8,128)(2,1)}), bf16[32,104,128]{2,1,0:T(8,128)(2,1)S(1)}, u32[]{:S(2)}, u32[]{:S(2)}) %all-to-all-start) | async-done | bytes 852000 | tf_op jit(solution)/shard_map/all_to_all | solution.py:268
  33.1 5.8 %attend.1 = (bf16[24,512]{1,0:T(8,128)(2,1)}, bf16[24,512]{1,0:T(8,128)(2,1)}, bf16[24,512]{1,0:T(8,128)(2,1)}, bf16[24,512]{1,0:T(8,128)(2,1)}, bf16[24,512]{1,...) custom-call(s32[1]{0:T(128)} %bitcast.1.me_ref, ...), custom_call_target="tpu_custom_call" | custom-call | flops 2415919104 | bytes 6291456 | tf_op jit(solution)/shard_map/attend/pallas_call | solution.py:374
  39.9 1.2 %collective-permute-start.1 = (bf16[24,512]{1,0:T(8,128)(2,1)}, bf16[24,512]{1,0:T(8,128)(2,1)S(1)}, u32[]{:S(2)}, u32[]{:S(2)}) collective-permute-start(bf16[24,512]{1,0:T(8,128)(2,1)} %get-tuple-element.45), channel_id=1, source_target_pairs={{0,2},{1,3},{2,0},{3,1},{4,6},{5,7},{6,4},{7,5},{8,10},{9,11},{10,... | collective-permute-start | bytes 73736 | tf_op jit(solution)/shard_map/ppermute | solution.py:272
  41.1 1.2 %collective-permute-start.10 = (bf16[24,512]{1,0:T(8,128)(2,1)}, bf16[24,512]{1,0:T(8,128)(2,1)S(1)}, u32[]{:S(2)}, u32[]{:S(2)}) collective-permute-start(bf16[24,512]{1,0:T(8,128)(2,1)} %get-tuple-element.54), channel_id=1, source_target_pairs={{0,11},{1,10},{2,9},{3,8},{4,15},{5,14},{6,13},{7,12},{8,3},{9,2},... | collective-permute-start | bytes 73736 | tf_op jit(solution)/shard_map/ppermute | solution.py:272
  42.2 1.5 %collective-permute-start.11 = (bf16[24,512]{1,0:T(8,128)(2,1)}, bf16[24,512]{1,0:T(8,128)(2,1)S(1)}, u32[]{:S(2)}, u32[]{:S(2)}) collective-permute-start(bf16[24,512]{1,0:T(8,128)(2,1)} %get-tuple-element.55), channel_id=1, source_target_pairs={{0,12},{1,13},{2,14},{3,15},{4,8},{5,9},{6,10},{7,11},{8,4},{9,5},... | collective-permute-start | bytes 73736 | tf_op jit(solution)/shard_map/ppermute | solution.py:272
  43.7 1.2 %collective-permute-start.12 = (bf16[24,512]{1,0:T(8,128)(2,1)}, bf16[24,512]{1,0:T(8,128)(2,1)S(1)}, u32[]{:S(2)}, u32[]{:S(2)}) collective-permute-start(bf16[24,512]{1,0:T(8,128)(2,1)} %get-tuple-element.56), channel_id=1, source_target_pairs={{0,13},{1,12},{2,15},{3,14},{4,9},{5,8},{6,11},{7,10},{8,5},{9,4},... | collective-permute-start | bytes 73736 | tf_op jit(solution)/shard_map/ppermute | solution.py:272
  44.9 2.4 %collective-permute-start.13 = (bf16[24,512]{1,0:T(8,128)(2,1)}, bf16[24,512]{1,0:T(8,128)(2,1)S(1)}, u32[]{:S(2)}, u32[]{:S(2)}) collective-permute-start(bf16[24,512]{1,0:T(8,128)(2,1)} %get-tuple-element.57), channel_id=1, source_target_pairs={{0,14},{1,15},{2,12},{3,13},{4,10},{5,11},{6,8},{7,9},{8,6},{9,7},... | collective-permute-start | bytes 73736 | tf_op jit(solution)/shard_map/ppermute | solution.py:272
  47.3 1.1 %collective-permute-start.14 = (bf16[24,512]{1,0:T(8,128)(2,1)}, bf16[24,512]{1,0:T(8,128)(2,1)S(1)}, u32[]{:S(2)}, u32[]{:S(2)}) collective-permute-start(bf16[24,512]{1,0:T(8,128)(2,1)} %get-tuple-element.58), channel_id=1, source_target_pairs={{0,15},{1,14},{2,13},{3,12},{4,11},{5,10},{6,9},{7,8},{8,7},{9,6},... | collective-permute-start | bytes 73736 | tf_op jit(solution)/shard_map/ppermute | solution.py:272
  48.8 2.4 %collective-permute-start.16 = (bf16[24,512]{1,0:T(8,128)(2,1)}, bf16[24,512]{1,0:T(8,128)(2,1)S(1)}, u32[]{:S(2)}, u32[]{:S(2)}) collective-permute-start(bf16[24,512]{1,0:T(8,128)(2,1)} %get-tuple-element.60), channel_id=1, source_target_pairs={{0,17},{1,16},{2,19},{3,18},{4,21},{5,20},{6,23},{7,22},{8,25},{9,... | collective-permute-start | bytes 73736 | tf_op jit(solution)/shard_map/ppermute | solution.py:272
  51.1 1.4 %collective-permute-start.17 = (bf16[24,512]{1,0:T(8,128)(2,1)}, bf16[24,512]{1,0:T(8,128)(2,1)S(1)}, u32[]{:S(2)}, u32[]{:S(2)}) collective-permute-start(bf16[24,512]{1,0:T(8,128)(2,1)} %get-tuple-element.61), channel_id=1, source_target_pairs={{0,18},{1,19},{2,16},{3,17},{4,22},{5,23},{6,20},{7,21},{8,26},{9,... | collective-permute-start | bytes 73736 | tf_op jit(solution)/shard_map/ppermute | solution.py:272
  52.6 2.1 %collective-permute-start.18 = (bf16[24,512]{1,0:T(8,128)(2,1)}, bf16[24,512]{1,0:T(8,128)(2,1)S(1)}, u32[]{:S(2)}, u32[]{:S(2)}) collective-permute-start(bf16[24,512]{1,0:T(8,128)(2,1)} %get-tuple-element.62), channel_id=1, source_target_pairs={{0,19},{1,18},{2,17},{3,16},{4,23},{5,22},{6,21},{7,20},{8,27},{9,... | collective-permute-start | bytes 73736 | tf_op jit(solution)/shard_map/ppermute | solution.py:272
  54.6 1.5 %collective-permute-start.19 = (bf16[24,512]{1,0:T(8,128)(2,1)}, bf16[24,512]{1,0:T(8,128)(2,1)S(1)}, u32[]{:S(2)}, u32[]{:S(2)}) collective-permute-start(bf16[24,512]{1,0:T(8,128)(2,1)} %get-tuple-element.63), channel_id=1, source_target_pairs={{0,20},{1,21},{2,22},{3,23},{4,16},{5,17},{6,18},{7,19},{8,28},{9,... | collective-permute-start | bytes 73736 | tf_op jit(solution)/shard_map/ppermute | solution.py:272
  56.1 1.5 %collective-permute-start.2 = (bf16[24,512]{1,0:T(8,128)(2,1)}, bf16[24,512]{1,0:T(8,128)(2,1)S(1)}, u32[]{:S(2)}, u32[]{:S(2)}) collective-permute-start(bf16[24,512]{1,0:T(8,128)(2,1)} %get-tuple-element.46), channel_id=1, source_target_pairs={{0,3},{1,2},{2,1},{3,0},{4,7},{5,6},{6,5},{7,4},{8,11},{9,10},{10,... | collective-permute-start | bytes 73736 | tf_op jit(solution)/shard_map/ppermute | solution.py:272
  57.6 1.5 %collective-permute-start.20 = (bf16[24,512]{1,0:T(8,128)(2,1)}, bf16[24,512]{1,0:T(8,128)(2,1)S(1)}, u32[]{:S(2)}, u32[]{:S(2)}) collective-permute-start(bf16[24,512]{1,0:T(8,128)(2,1)} %get-tuple-element.64), channel_id=1, source_target_pairs={{0,21},{1,20},{2,23},{3,22},{4,17},{5,16},{6,19},{7,18},{8,29},{9,... | collective-permute-start | bytes 73736 | tf_op jit(solution)/shard_map/ppermute | solution.py:272
  59.1 1.7 %collective-permute-start.21 = (bf16[24,512]{1,0:T(8,128)(2,1)}, bf16[24,512]{1,0:T(8,128)(2,1)S(1)}, u32[]{:S(2)}, u32[]{:S(2)}) collective-permute-start(bf16[24,512]{1,0:T(8,128)(2,1)} %get-tuple-element.65), channel_id=1, source_target_pairs={{0,22},{1,23},{2,20},{3,21},{4,18},{5,19},{6,16},{7,17},{8,30},{9,... | collective-permute-start | bytes 73736 | tf_op jit(solution)/shard_map/ppermute | solution.py:272
  60.8 2.7 %collective-permute-start.22 = (bf16[24,512]{1,0:T(8,128)(2,1)}, bf16[24,512]{1,0:T(8,128)(2,1)S(1)}, u32[]{:S(2)}, u32[]{:S(2)}) collective-permute-start(bf16[24,512]{1,0:T(8,128)(2,1)} %get-tuple-element.66), channel_id=1, source_target_pairs={{0,23},{1,22},{2,21},{3,20},{4,19},{5,18},{6,17},{7,16},{8,31},{9,... | collective-permute-start | bytes 73736 | tf_op jit(solution)/shard_map/ppermute | solution.py:272
  63.5 1.4 %collective-permute-start.23 = (bf16[24,512]{1,0:T(8,128)(2,1)}, bf16[24,512]{1,0:T(8,128)(2,1)S(1)}, u32[]{:S(2)}, u32[]{:S(2)}) collective-permute-start(bf16[24,512]{1,0:T(8,128)(2,1)} %get-tuple-element.67), channel_id=1, source_target_pairs={{0,24},{1,25},{2,26},{3,27},{4,28},{5,29},{6,30},{7,31},{8,16},{9,... | collective-permute-start | bytes 73736 | tf_op jit(solution)/shard_map/ppermute | solution.py:272
  65.0 2.2 %collective-permute-start.24 = (bf16[24,512]{1,0:T(8,128)(2,1)}, bf16[24,512]{1,0:T(8,128)(2,1)S(1)}, u32[]{:S(2)}, u32[]{:S(2)}) collective-permute-start(bf16[24,512]{1,0:T(8,128)(2,1)} %get-tuple-element.68), channel_id=1, source_target_pairs={{0,25},{1,24},{2,27},{3,26},{4,29},{5,28},{6,31},{7,30},{8,17},{9,... | collective-permute-start | bytes 73736 | tf_op jit(solution)/shard_map/ppermute | solution.py:272
  67.1 1.8 %collective-permute-start.25 = (bf16[24,512]{1,0:T(8,128)(2,1)}, bf16[24,512]{1,0:T(8,128)(2,1)S(1)}, u32[]{:S(2)}, u32[]{:S(2)}) collective-permute-start(bf16[24,512]{1,0:T(8,128)(2,1)} %get-tuple-element.69), channel_id=1, source_target_pairs={{0,26},{1,27},{2,24},{3,25},{4,30},{5,31},{6,28},{7,29},{8,18},{9,... | collective-permute-start | bytes 73736 | tf_op jit(solution)/shard_map/ppermute | solution.py:272
  68.9 2.6 %collective-permute-start.26 = (bf16[24,512]{1,0:T(8,128)(2,1)}, bf16[24,512]{1,0:T(8,128)(2,1)S(1)}, u32[]{:S(2)}, u32[]{:S(2)}) collective-permute-start(bf16[24,512]{1,0:T(8,128)(2,1)} %get-tuple-element.70), channel_id=1, source_target_pairs={{0,27},{1,26},{2,25},{3,24},{4,31},{5,30},{6,29},{7,28},{8,19},{9,... | collective-permute-start | bytes 73736 | tf_op jit(solution)/shard_map/ppermute | solution.py:272
  71.5 1.6 %collective-permute-start.27 = (bf16[24,512]{1,0:T(8,128)(2,1)}, bf16[24,512]{1,0:T(8,128)(2,1)S(1)}, u32[]{:S(2)}, u32[]{:S(2)}) collective-permute-start(bf16[24,512]{1,0:T(8,128)(2,1)} %get-tuple-element.71), channel_id=1, source_target_pairs={{0,28},{1,29},{2,30},{3,31},{4,24},{5,25},{6,26},{7,27},{8,20},{9,... | collective-permute-start | bytes 73736 | tf_op jit(solution)/shard_map/ppermute | solution.py:272
  73.1 2.9 %collective-permute-start.28 = (bf16[24,512]{1,0:T(8,128)(2,1)}, bf16[24,512]{1,0:T(8,128)(2,1)S(1)}, u32[]{:S(2)}, u32[]{:S(2)}) collective-permute-start(bf16[24,512]{1,0:T(8,128)(2,1)} %get-tuple-element.72), channel_id=1, source_target_pairs={{0,29},{1,28},{2,31},{3,30},{4,25},{5,24},{6,27},{7,26},{8,21},{9,... | collective-permute-start | bytes 73736 | tf_op jit(solution)/shard_map/ppermute | solution.py:272
  76.0 1.6 %collective-permute-start.29 = (bf16[24,512]{1,0:T(8,128)(2,1)}, bf16[24,512]{1,0:T(8,128)(2,1)S(1)}, u32[]{:S(2)}, u32[]{:S(2)}) collective-permute-start(bf16[24,512]{1,0:T(8,128)(2,1)} %get-tuple-element.73), channel_id=1, source_target_pairs={{0,30},{1,31},{2,28},{3,29},{4,26},{5,27},{6,24},{7,25},{8,22},{9,... | collective-permute-start | bytes 73736 | tf_op jit(solution)/shard_map/ppermute | solution.py:272
  77.6 1.4 %collective-permute-start.3 = (bf16[24,512]{1,0:T(8,128)(2,1)}, bf16[24,512]{1,0:T(8,128)(2,1)S(1)}, u32[]{:S(2)}, u32[]{:S(2)}) collective-permute-start(bf16[24,512]{1,0:T(8,128)(2,1)} %get-tuple-element.47), channel_id=1, source_target_pairs={{0,4},{1,5},{2,6},{3,7},{4,0},{5,1},{6,2},{7,3},{8,12},{9,13},{10,... | collective-permute-start | bytes 73736 | tf_op jit(solution)/shard_map/ppermute | solution.py:272
  79.0 3.1 %collective-permute-start.30 = (bf16[24,512]{1,0:T(8,128)(2,1)}, bf16[24,512]{1,0:T(8,128)(2,1)S(1)}, u32[]{:S(2)}, u32[]{:S(2)}) collective-permute-start(bf16[24,512]{1,0:T(8,128)(2,1)} %get-tuple-element.74), channel_id=1, source_target_pairs={{0,31},{1,30},{2,29},{3,28},{4,27},{5,26},{6,25},{7,24},{8,23},{9,... | collective-permute-start | bytes 73736 | tf_op jit(solution)/shard_map/ppermute | solution.py:272
  83.9 2.1 %collective-permute-start.6 = (bf16[24,512]{1,0:T(8,128)(2,1)}, bf16[24,512]{1,0:T(8,128)(2,1)S(1)}, u32[]{:S(2)}, u32[]{:S(2)}) collective-permute-start(bf16[24,512]{1,0:T(8,128)(2,1)} %get-tuple-element.50), channel_id=1, source_target_pairs={{0,7},{1,6},{2,5},{3,4},{4,3},{5,2},{6,1},{7,0},{8,15},{9,14},{10,... | collective-permute-start | bytes 73736 | tf_op jit(solution)/shard_map/ppermute | solution.py:272
  87.3 1.4 %collective-permute-start.9 = (bf16[24,512]{1,0:T(8,128)(2,1)}, bf16[24,512]{1,0:T(8,128)(2,1)S(1)}, u32[]{:S(2)}, u32[]{:S(2)}) collective-permute-start(bf16[24,512]{1,0:T(8,128)(2,1)} %get-tuple-element.53), channel_id=1, source_target_pairs={{0,10},{1,11},{2,8},{3,9},{4,14},{5,15},{6,12},{7,13},{8,2},{9,3},... | collective-permute-start | bytes 73736 | tf_op jit(solution)/shard_map/ppermute | solution.py:272
  88.6 6.5 %own.1 = (bf16[512,512]{1,0:T(8,128)(2,1)S(1)}, bf16[512,512]{1,0:T(8,128)(2,1)S(1)}, f32[512,128]{1,0:T(8,128)S(1)}) custom-call(s32[1]{0:T(128)} %bitcast.1.me_ref, bf16[512,1024]{1,0:T(8,128)(2,1)} %cand_ref.1, f32[1,1024]{1,0:T(1,128)} %bitcast.6, bf16[1024,2048]{1,0:T(8,128)(2,1)} %w_ref.1, s32[1,512]{1,0:T(1,128)} %bitcast.9), custom_call_target="tpu_custom_call" | custom-call | flops 2147483648 | bytes 6291456 | tf_op jit(solution)/shard_map/own/pallas_call | solution.py:351
  95.1 1.7 %answer.1 = bf16[512,512]{1,0:T(8,128)(2,1)} custom-call(bf16[24,512]{1,0:T(8,128)(2,1)S(1)} %copy-done, bf16[24,512]{1,0:T(8,128)(2,1)S(1)} %collective-permute-done.refs_1_, bf16[24,512]{1,0:T(8,128)(2,1)S(1)} %collective-permute-done.1.refs_2_, bf16[24,512]{1,0:T(8,128)(2,1)S(1)} %collective-permute-done.2.refs_3_, ...), custom_call_target="tpu_custom_call" | custom-call | flops 402653184 | bytes 4194304 | tf_op jit(solution)/shard_map/answer/pallas_call | solution.py:400
  (39 shorter events, 4.4 us)
Async XLA Ops:
  4.6 28.4 %all-to-all-start = ((bf16[32,104,128]{2,1,0:T(8,128)(2,1)}), bf16[32,104,128]{2,1,0:T(8,128)(2,1)S(1)}, u32[]{:S(2)}, u32[]{:S(2)}) async-start(bf16[32,104,128]{2,1,0:T(8,128)(2,1)} %dispatch.1), calls=%async_computation | async-start | bytes 1703936 | tf_op jit(solution)/shard_map/all_to_all | solution.py:268
  38.9 6.1 %collective-permute-start = (bf16[24,512]{1,0:T(8,128)(2,1)}, bf16[24,512]{1,0:T(8,128)(2,1)S(1)}, u32[]{:S(2)}, u32[]{:S(2)}) collective-permute-start(bf16[24,512]{1,0:T(8,128)(2,1)} %get-tuple-element.44), channel_id=1, source_target_pairs={{0,1},{1,0},{2,3},{3,2},{4,5},{5,4},{6,7},{7,6},{8,9},{9,8},{10,11... | collective-permute-start | bytes 73736 | tf_op jit(solution)/shard_map/ppermute | solution.py:272
  39.9 7.4 %collective-permute-start.1 = (bf16[24,512]{1,0:T(8,128)(2,1)}, bf16[24,512]{1,0:T(8,128)(2,1)S(1)}, u32[]{:S(2)}, u32[]{:S(2)}) collective-permute-start(bf16[24,512]{1,0:T(8,128)(2,1)} %get-tuple-element.45), channel_id=1, source_target_pairs={{0,2},{1,3},{2,0},{3,1},{4,6},{5,7},{6,4},{7,5},{8,10},{9,11},{10,... | collective-permute-start | bytes 73736 | tf_op jit(solution)/shard_map/ppermute | solution.py:272
  41.1 7.4 %collective-permute-start.10 = (bf16[24,512]{1,0:T(8,128)(2,1)}, bf16[24,512]{1,0:T(8,128)(2,1)S(1)}, u32[]{:S(2)}, u32[]{:S(2)}) collective-permute-start(bf16[24,512]{1,0:T(8,128)(2,1)} %get-tuple-element.54), channel_id=1, source_target_pairs={{0,11},{1,10},{2,9},{3,8},{4,15},{5,14},{6,13},{7,12},{8,3},{9,2},... | collective-permute-start | bytes 73736 | tf_op jit(solution)/shard_map/ppermute | solution.py:272
  42.2 6.5 %collective-permute-start.11 = (bf16[24,512]{1,0:T(8,128)(2,1)}, bf16[24,512]{1,0:T(8,128)(2,1)S(1)}, u32[]{:S(2)}, u32[]{:S(2)}) collective-permute-start(bf16[24,512]{1,0:T(8,128)(2,1)} %get-tuple-element.55), channel_id=1, source_target_pairs={{0,12},{1,13},{2,14},{3,15},{4,8},{5,9},{6,10},{7,11},{8,4},{9,5},... | collective-permute-start | bytes 73736 | tf_op jit(solution)/shard_map/ppermute | solution.py:272
  43.7 7.4 %collective-permute-start.12 = (bf16[24,512]{1,0:T(8,128)(2,1)}, bf16[24,512]{1,0:T(8,128)(2,1)S(1)}, u32[]{:S(2)}, u32[]{:S(2)}) collective-permute-start(bf16[24,512]{1,0:T(8,128)(2,1)} %get-tuple-element.56), channel_id=1, source_target_pairs={{0,13},{1,12},{2,15},{3,14},{4,9},{5,8},{6,11},{7,10},{8,5},{9,4},... | collective-permute-start | bytes 73736 | tf_op jit(solution)/shard_map/ppermute | solution.py:272
  44.9 7.6 %collective-permute-start.13 = (bf16[24,512]{1,0:T(8,128)(2,1)}, bf16[24,512]{1,0:T(8,128)(2,1)S(1)}, u32[]{:S(2)}, u32[]{:S(2)}) collective-permute-start(bf16[24,512]{1,0:T(8,128)(2,1)} %get-tuple-element.57), channel_id=1, source_target_pairs={{0,14},{1,15},{2,12},{3,13},{4,10},{5,11},{6,8},{7,9},{8,6},{9,7},... | collective-permute-start | bytes 73736 | tf_op jit(solution)/shard_map/ppermute | solution.py:272
  47.3 7.3 %collective-permute-start.14 = (bf16[24,512]{1,0:T(8,128)(2,1)}, bf16[24,512]{1,0:T(8,128)(2,1)S(1)}, u32[]{:S(2)}, u32[]{:S(2)}) collective-permute-start(bf16[24,512]{1,0:T(8,128)(2,1)} %get-tuple-element.58), channel_id=1, source_target_pairs={{0,15},{1,14},{2,13},{3,12},{4,11},{5,10},{6,9},{7,8},{8,7},{9,6},... | collective-permute-start | bytes 73736 | tf_op jit(solution)/shard_map/ppermute | solution.py:272
  48.4 7.7 %collective-permute-start.15 = (bf16[24,512]{1,0:T(8,128)(2,1)}, bf16[24,512]{1,0:T(8,128)(2,1)S(1)}, u32[]{:S(2)}, u32[]{:S(2)}) collective-permute-start(bf16[24,512]{1,0:T(8,128)(2,1)} %get-tuple-element.59), channel_id=1, source_target_pairs={{0,16},{1,17},{2,18},{3,19},{4,20},{5,21},{6,22},{7,23},{8,24},{9,... | collective-permute-start | bytes 73736 | tf_op jit(solution)/shard_map/ppermute | solution.py:272
  48.8 8.8 %collective-permute-start.16 = (bf16[24,512]{1,0:T(8,128)(2,1)}, bf16[24,512]{1,0:T(8,128)(2,1)S(1)}, u32[]{:S(2)}, u32[]{:S(2)}) collective-permute-start(bf16[24,512]{1,0:T(8,128)(2,1)} %get-tuple-element.60), channel_id=1, source_target_pairs={{0,17},{1,16},{2,19},{3,18},{4,21},{5,20},{6,23},{7,22},{8,25},{9,... | collective-permute-start | bytes 73736 | tf_op jit(solution)/shard_map/ppermute | solution.py:272
  51.1 8.0 %collective-permute-start.17 = (bf16[24,512]{1,0:T(8,128)(2,1)}, bf16[24,512]{1,0:T(8,128)(2,1)S(1)}, u32[]{:S(2)}, u32[]{:S(2)}) collective-permute-start(bf16[24,512]{1,0:T(8,128)(2,1)} %get-tuple-element.61), channel_id=1, source_target_pairs={{0,18},{1,19},{2,16},{3,17},{4,22},{5,23},{6,20},{7,21},{8,26},{9,... | collective-permute-start | bytes 73736 | tf_op jit(solution)/shard_map/ppermute | solution.py:272
  52.6 8.3 %collective-permute-start.18 = (bf16[24,512]{1,0:T(8,128)(2,1)}, bf16[24,512]{1,0:T(8,128)(2,1)S(1)}, u32[]{:S(2)}, u32[]{:S(2)}) collective-permute-start(bf16[24,512]{1,0:T(8,128)(2,1)} %get-tuple-element.62), channel_id=1, source_target_pairs={{0,19},{1,18},{2,17},{3,16},{4,23},{5,22},{6,21},{7,20},{8,27},{9,... | collective-permute-start | bytes 73736 | tf_op jit(solution)/shard_map/ppermute | solution.py:272
  54.6 8.9 %collective-permute-start.19 = (bf16[24,512]{1,0:T(8,128)(2,1)}, bf16[24,512]{1,0:T(8,128)(2,1)S(1)}, u32[]{:S(2)}, u32[]{:S(2)}) collective-permute-start(bf16[24,512]{1,0:T(8,128)(2,1)} %get-tuple-element.63), channel_id=1, source_target_pairs={{0,20},{1,21},{2,22},{3,23},{4,16},{5,17},{6,18},{7,19},{8,28},{9,... | collective-permute-start | bytes 73736 | tf_op jit(solution)/shard_map/ppermute | solution.py:272
  56.1 8.9 %collective-permute-start.2 = (bf16[24,512]{1,0:T(8,128)(2,1)}, bf16[24,512]{1,0:T(8,128)(2,1)S(1)}, u32[]{:S(2)}, u32[]{:S(2)}) collective-permute-start(bf16[24,512]{1,0:T(8,128)(2,1)} %get-tuple-element.46), channel_id=1, source_target_pairs={{0,3},{1,2},{2,1},{3,0},{4,7},{5,6},{6,5},{7,4},{8,11},{9,10},{10,... | collective-permute-start | bytes 73736 | tf_op jit(solution)/shard_map/ppermute | solution.py:272
  57.6 9.5 %collective-permute-start.20 = (bf16[24,512]{1,0:T(8,128)(2,1)}, bf16[24,512]{1,0:T(8,128)(2,1)S(1)}, u32[]{:S(2)}, u32[]{:S(2)}) collective-permute-start(bf16[24,512]{1,0:T(8,128)(2,1)} %get-tuple-element.64), channel_id=1, source_target_pairs={{0,21},{1,20},{2,23},{3,22},{4,17},{5,16},{6,19},{7,18},{8,29},{9,... | collective-permute-start | bytes 73736 | tf_op jit(solution)/shard_map/ppermute | solution.py:272
  59.1 9.8 %collective-permute-start.21 = (bf16[24,512]{1,0:T(8,128)(2,1)}, bf16[24,512]{1,0:T(8,128)(2,1)S(1)}, u32[]{:S(2)}, u32[]{:S(2)}) collective-permute-start(bf16[24,512]{1,0:T(8,128)(2,1)} %get-tuple-element.65), channel_id=1, source_target_pairs={{0,22},{1,23},{2,20},{3,21},{4,18},{5,19},{6,16},{7,17},{8,30},{9,... | collective-permute-start | bytes 73736 | tf_op jit(solution)/shard_map/ppermute | solution.py:272
  60.8 10.7 %collective-permute-start.22 = (bf16[24,512]{1,0:T(8,128)(2,1)}, bf16[24,512]{1,0:T(8,128)(2,1)S(1)}, u32[]{:S(2)}, u32[]{:S(2)}) collective-permute-start(bf16[24,512]{1,0:T(8,128)(2,1)} %get-tuple-element.66), channel_id=1, source_target_pairs={{0,23},{1,22},{2,21},{3,20},{4,19},{5,18},{6,17},{7,16},{8,31},{9,... | collective-permute-start | bytes 73736 | tf_op jit(solution)/shard_map/ppermute | solution.py:272
  63.5 9.6 %collective-permute-start.23 = (bf16[24,512]{1,0:T(8,128)(2,1)}, bf16[24,512]{1,0:T(8,128)(2,1)S(1)}, u32[]{:S(2)}, u32[]{:S(2)}) collective-permute-start(bf16[24,512]{1,0:T(8,128)(2,1)} %get-tuple-element.67), channel_id=1, source_target_pairs={{0,24},{1,25},{2,26},{3,27},{4,28},{5,29},{6,30},{7,31},{8,16},{9,... | collective-permute-start | bytes 73736 | tf_op jit(solution)/shard_map/ppermute | solution.py:272
  65.0 11.1 %collective-permute-start.24 = (bf16[24,512]{1,0:T(8,128)(2,1)}, bf16[24,512]{1,0:T(8,128)(2,1)S(1)}, u32[]{:S(2)}, u32[]{:S(2)}) collective-permute-start(bf16[24,512]{1,0:T(8,128)(2,1)} %get-tuple-element.68), channel_id=1, source_target_pairs={{0,25},{1,24},{2,27},{3,26},{4,29},{5,28},{6,31},{7,30},{8,17},{9,... | collective-permute-start | bytes 73736 | tf_op jit(solution)/shard_map/ppermute | solution.py:272
  67.1 10.5 %collective-permute-start.25 = (bf16[24,512]{1,0:T(8,128)(2,1)}, bf16[24,512]{1,0:T(8,128)(2,1)S(1)}, u32[]{:S(2)}, u32[]{:S(2)}) collective-permute-start(bf16[24,512]{1,0:T(8,128)(2,1)} %get-tuple-element.69), channel_id=1, source_target_pairs={{0,26},{1,27},{2,24},{3,25},{4,30},{5,31},{6,28},{7,29},{8,18},{9,... | collective-permute-start | bytes 73736 | tf_op jit(solution)/shard_map/ppermute | solution.py:272
  68.9 10.1 %collective-permute-start.26 = (bf16[24,512]{1,0:T(8,128)(2,1)}, bf16[24,512]{1,0:T(8,128)(2,1)S(1)}, u32[]{:S(2)}, u32[]{:S(2)}) collective-permute-start(bf16[24,512]{1,0:T(8,128)(2,1)} %get-tuple-element.70), channel_id=1, source_target_pairs={{0,27},{1,26},{2,25},{3,24},{4,31},{5,30},{6,29},{7,28},{8,19},{9,... | collective-permute-start | bytes 73736 | tf_op jit(solution)/shard_map/ppermute | solution.py:272
  71.5 10.6 %collective-permute-start.27 = (bf16[24,512]{1,0:T(8,128)(2,1)}, bf16[24,512]{1,0:T(8,128)(2,1)S(1)}, u32[]{:S(2)}, u32[]{:S(2)}) collective-permute-start(bf16[24,512]{1,0:T(8,128)(2,1)} %get-tuple-element.71), channel_id=1, source_target_pairs={{0,28},{1,29},{2,30},{3,31},{4,24},{5,25},{6,26},{7,27},{8,20},{9,... | collective-permute-start | bytes 73736 | tf_op jit(solution)/shard_map/ppermute | solution.py:272
  73.1 9.7 %collective-permute-start.28 = (bf16[24,512]{1,0:T(8,128)(2,1)}, bf16[24,512]{1,0:T(8,128)(2,1)S(1)}, u32[]{:S(2)}, u32[]{:S(2)}) collective-permute-start(bf16[24,512]{1,0:T(8,128)(2,1)} %get-tuple-element.72), channel_id=1, source_target_pairs={{0,29},{1,28},{2,31},{3,30},{4,25},{5,24},{6,27},{7,26},{8,21},{9,... | collective-permute-start | bytes 73736 | tf_op jit(solution)/shard_map/ppermute | solution.py:272
  76.0 7.8 %collective-permute-start.29 = (bf16[24,512]{1,0:T(8,128)(2,1)}, bf16[24,512]{1,0:T(8,128)(2,1)S(1)}, u32[]{:S(2)}, u32[]{:S(2)}) collective-permute-start(bf16[24,512]{1,0:T(8,128)(2,1)} %get-tuple-element.73), channel_id=1, source_target_pairs={{0,30},{1,31},{2,28},{3,29},{4,26},{5,27},{6,24},{7,25},{8,22},{9,... | collective-permute-start | bytes 73736 | tf_op jit(solution)/shard_map/ppermute | solution.py:272
  77.6 8.4 %collective-permute-start.3 = (bf16[24,512]{1,0:T(8,128)(2,1)}, bf16[24,512]{1,0:T(8,128)(2,1)S(1)}, u32[]{:S(2)}, u32[]{:S(2)}) collective-permute-start(bf16[24,512]{1,0:T(8,128)(2,1)} %get-tuple-element.47), channel_id=1, source_target_pairs={{0,4},{1,5},{2,6},{3,7},{4,0},{5,1},{6,2},{7,3},{8,12},{9,13},{10,... | collective-permute-start | bytes 73736 | tf_op jit(solution)/shard_map/ppermute | solution.py:272
  79.0 7.5 %collective-permute-start.30 = (bf16[24,512]{1,0:T(8,128)(2,1)}, bf16[24,512]{1,0:T(8,128)(2,1)S(1)}, u32[]{:S(2)}, u32[]{:S(2)}) collective-permute-start(bf16[24,512]{1,0:T(8,128)(2,1)} %get-tuple-element.74), channel_id=1, source_target_pairs={{0,31},{1,30},{2,29},{3,28},{4,27},{5,26},{6,25},{7,24},{8,23},{9,... | collective-permute-start | bytes 73736 | tf_op jit(solution)/shard_map/ppermute | solution.py:272
  82.2 5.1 %collective-permute-start.4 = (bf16[24,512]{1,0:T(8,128)(2,1)}, bf16[24,512]{1,0:T(8,128)(2,1)S(1)}, u32[]{:S(2)}, u32[]{:S(2)}) collective-permute-start(bf16[24,512]{1,0:T(8,128)(2,1)} %get-tuple-element.48), channel_id=1, source_target_pairs={{0,5},{1,4},{2,7},{3,6},{4,1},{5,0},{6,3},{7,2},{8,13},{9,12},{10,... | collective-permute-start | bytes 73736 | tf_op jit(solution)/shard_map/ppermute | solution.py:272
  82.8 12.2 %collective-permute-start.5 = (bf16[24,512]{1,0:T(8,128)(2,1)}, bf16[24,512]{1,0:T(8,128)(2,1)S(1)}, u32[]{:S(2)}, u32[]{:S(2)}) collective-permute-start(bf16[24,512]{1,0:T(8,128)(2,1)} %get-tuple-element.49), channel_id=1, source_target_pairs={{0,6},{1,7},{2,4},{3,5},{4,2},{5,3},{6,0},{7,1},{8,14},{9,15},{10,... | collective-permute-start | bytes 73736 | tf_op jit(solution)/shard_map/ppermute | solution.py:272
  83.9 11.2 %collective-permute-start.6 = (bf16[24,512]{1,0:T(8,128)(2,1)}, bf16[24,512]{1,0:T(8,128)(2,1)S(1)}, u32[]{:S(2)}, u32[]{:S(2)}) collective-permute-start(bf16[24,512]{1,0:T(8,128)(2,1)} %get-tuple-element.50), channel_id=1, source_target_pairs={{0,7},{1,6},{2,5},{3,4},{4,3},{5,2},{6,1},{7,0},{8,15},{9,14},{10,... | collective-permute-start | bytes 73736 | tf_op jit(solution)/shard_map/ppermute | solution.py:272
  86.0 9.1 %collective-permute-start.7 = (bf16[24,512]{1,0:T(8,128)(2,1)}, bf16[24,512]{1,0:T(8,128)(2,1)S(1)}, u32[]{:S(2)}, u32[]{:S(2)}) collective-permute-start(bf16[24,512]{1,0:T(8,128)(2,1)} %get-tuple-element.51), channel_id=1, source_target_pairs={{0,8},{1,9},{2,10},{3,11},{4,12},{5,13},{6,14},{7,15},{8,0},{9,1},... | collective-permute-start | bytes 73736 | tf_op jit(solution)/shard_map/ppermute | solution.py:272
  86.5 8.6 %collective-permute-start.8 = (bf16[24,512]{1,0:T(8,128)(2,1)}, bf16[24,512]{1,0:T(8,128)(2,1)S(1)}, u32[]{:S(2)}, u32[]{:S(2)}) collective-permute-start(bf16[24,512]{1,0:T(8,128)(2,1)} %get-tuple-element.52), channel_id=1, source_target_pairs={{0,9},{1,8},{2,11},{3,10},{4,13},{5,12},{6,15},{7,14},{8,1},{9,0},... | collective-permute-start | bytes 73736 | tf_op jit(solution)/shard_map/ppermute | solution.py:272
  87.3 7.9 %collective-permute-start.9 = (bf16[24,512]{1,0:T(8,128)(2,1)}, bf16[24,512]{1,0:T(8,128)(2,1)S(1)}, u32[]{:S(2)}, u32[]{:S(2)}) collective-permute-start(bf16[24,512]{1,0:T(8,128)(2,1)} %get-tuple-element.53), channel_id=1, source_target_pairs={{0,10},{1,11},{2,8},{3,9},{4,14},{5,15},{6,12},{7,13},{8,2},{9,3},... | collective-permute-start | bytes 73736 | tf_op jit(solution)/shard_map/ppermute | solution.py:272
  (1 other events, 7.9 us)

commit v6 on v4

--- a/solution.py
+++ b/solution.py
@@ -136,15 +136,15 @@
             value_ref[h, pair, side] = value[:, cols]
 
 
-def own_kernel(n_dev, cap, cand_ref, gain_ref, w_ref, owner_ref, u_ref, v_ref, aux_ref, slot_ref):
+def own_kernel(cap, cand_ref, gain_ref, w_ref, owner_ref, u_ref, self_ref, pick_ref, slot_ref):
     step, width = u_ref.shape
-    heads = width // HDIM
+    total = pick_ref.shape[1]
     i = pl.program_id(0)
 
     @pl.when(i == 0)
     def _():
         place = owner_ref[...]
-        _, rank = ranks(place, n_dev)
+        _, rank = ranks(place, total // cap)
         slot = (place * cap + rank).astype(F32)
         slot_ref[...] = jnp.broadcast_to(slot, (128, slot.shape[1])).T
 
@@ -154,18 +154,18 @@
         return silu(mm(normed, w_ref[:, part * width : (part + 1) * width])).astype(BF16)
 
     u_ref[...] = projected(0)
-    v_ref[...] = projected(1)
+    own_v = projected(1).astype(F32)
     prod = projected(2).astype(F32) * projected(3).astype(F32)
-    lane = iota((step, 128), 1)
-    aux = slot_ref[pl.ds(pl.multiple_of(i * step, step), step), :]
-    for h in range(heads):
-        score = jnp.sum(prod[:, h * HDIM : (h + 1) * HDIM], axis=-1, keepdims=True) * HDIM ** (-0.5)
-        aux = jnp.where(lane == h, silu(score).astype(BF16).astype(F32), aux)
-    aux_ref[...] = aux
+    for h in range(width // HDIM):
+        cols = slice(h * HDIM, (h + 1) * HDIM)
+        score = jnp.sum(prod[:, cols], axis=-1, keepdims=True) * HDIM ** (-0.5)
+        self_ref[:, cols] = (silu(score).astype(BF16).astype(F32) * own_v[:, cols]).astype(BF16)
+    slot = slot_ref[pl.ds(pl.multiple_of(i * step, step), step), 0:1].astype(jnp.int32)
+    pick_ref[...] = one_hot(iota((step, total), 1) == slot)
 
 
 def attend_kernel(
-    cap, arrived_ref, k_hbm, v_hbm, out_hbm, k_ref, v_ref, out_ref, mask_ref, odd_ref, k_sem, v_sem, out_sem
+    cap, arrived_ref, k_hbm, v_hbm, _, out_hbm, k_ref, v_ref, out_ref, mask_ref, odd_ref, k_sem, v_sem, out_sem
 ):
     n_dev = arrived_ref.shape[0]
     heads, depth = k_ref.shape[0], k_ref.shape[1]
@@ -203,13 +203,13 @@
     def _(g):
         members = [g * each + t for t in range(each)]
         load(k_hbm, k_ref, k_sem, g).wait()
-        load(v_hbm, v_ref, v_sem, g).wait()
         scores = []
         for h in members:
             rows = pl.ds(pl.multiple_of(h * cap, cap), cap)
             query = arrived_ref[:, rows, :].astype(F32).reshape(total, HDIM).astype(BF16)
             scores.append(mm(spread(query), k_ref[h]))
         weights = [silu(chosen(score) * HDIM ** (-0.5)).astype(BF16) for score in scores]
+        load(v_hbm, v_ref, v_sem, g).wait()
         for h, weight in zip(members, weights):
             cols = pl.ds(pl.multiple_of(h * HDIM, HDIM), HDIM)
             out_ref[:, cols] = chosen(mm(spread(weight), v_ref[h])).astype(BF16)
@@ -219,15 +219,8 @@
     copy.wait()
 
 
-def answer_kernel(back_ref, u_ref, v_ref, aux_ref, out_ref):
-    width = u_ref.shape[1]
-    total = back_ref.shape[0]
-    heads = width // HDIM
-    aux = aux_ref[...]
-    pick = one_hot(iota((aux.shape[0], total), 1) == aux[:, heads : heads + 1].astype(jnp.int32))
-    own_v = v_ref[...].astype(F32)
-    own = [own_v[:, h * HDIM : (h + 1) * HDIM] * aux[:, h : h + 1] for h in range(heads)]
-    normed = norm_rows(mm(pick, back_ref[...]) + jnp.concatenate(own, axis=1))
+def answer_kernel(back_ref, u_ref, self_ref, pick_ref, out_ref):
+    normed = norm_rows(mm(pick_ref[...], back_ref[...]) + self_ref[...].astype(F32))
     out_ref[...] = normed.astype(BF16) * u_ref[...]
 
 
@@ -330,8 +323,8 @@
     )(in_hbm(hist_len), history, gain, w_proj, w_proj)
 
     step = count // 2
-    gate, own_v, aux = pl.pallas_call(
-        functools.partial(own_kernel, n_dev, cap),
+    gate, own, pick = pl.pallas_call(
+        functools.partial(own_kernel, cap),
         grid=(count // step,),
         in_specs=[
             pl.BlockSpec((step, dim), lambda i: (i, 0)),
@@ -342,9 +335,9 @@
         out_specs=[
             pl.BlockSpec((step, width), lambda i: (i, 0)),
             pl.BlockSpec((step, width), lambda i: (i, 0)),
-            pl.BlockSpec((step, 128), lambda i: (i, 0)),
-        ],
-        out_shape=[shape((count, width), BF16), shape((count, width), BF16), shape((count, 128), F32)],
+            pl.BlockSpec((step, total), lambda i: (i, 0)),
+        ],
+        out_shape=[shape((count, width), BF16), shape((count, width), BF16), shape((count, total), BF16)],
         scratch_shapes=[pltpu.VMEM((count, 128), F32)],
         compiler_params=params(),
         cost_estimate=cost(8 * count * dim * width, 6 << 20),
@@ -354,7 +347,7 @@
     kv_shape = (heads, users * HDIM // 2, 2 * rows)
     attended = pl.pallas_call(
         functools.partial(attend_kernel, cap),
-        in_specs=[pl.BlockSpec(memory_space=pltpu.VMEM), anywhere, anywhere],
+        in_specs=[pl.BlockSpec(memory_space=pltpu.VMEM), anywhere, anywhere, anywhere],
         out_specs=anywhere,
         out_shape=pltpu.HBM((total, width), BF16),
         scratch_shapes=[
@@ -370,7 +363,7 @@
         compiler_params=params(),
         cost_estimate=cost(2 * total * rows * users * width * 2, 6 << 20),
         name="attend",
-    )(in_vmem(arrived), in_hbm(keys), in_hbm(values))
+    )(in_vmem(arrived), in_hbm(keys), in_hbm(values), own)
 
     back = exchange(attended.reshape(n_dev, cap, width)).reshape(total, width)
 
@@ -382,7 +375,7 @@
         compiler_params=params(),
         cost_estimate=cost(2 * count * total * width, 4 << 20),
         name="answer",
-    )(in_vmem(back), gate, own_v, aux)
+    )(in_vmem(back), gate, own, pick)
     return (kv_cache, cand_out)
 
 

time: 65.4 us -> 65.4 us (level)
  blocking collectives: 0 us -> 24.5 us
  waiting for transfers between devices: 25.7 us -> 5.45 us
  starting transfers between devices: 11.4 us -> 7.1 us
    all_to_all x0 -> x1, blocking collectives: none -> 24.5 us  [exchange(): return lax.all_to_all(slots, AXES, split_axis=0, concat_axis=0, tiled=True)]
    all_to_all x2 -> x1, waiting for transfers between devices: 25.7 us -> 5.45 us  [exchange(): return lax.all_to_all(slots, AXES, split_axis=0, concat_axis=0, tiled=True)]
    all_to_all x2 -> x1, starting transfers between devices: 11.4 us -> 7.1 us  [exchange(): return lax.all_to_all(slots, AXES, split_axis=0, concat_axis=0, tiled=True)]
  transfers between devices with their start and end apart: 2 -> 1, of which waited for: 2 -> 1; matrix products, arithmetic and copies ran while one was open for 0% -> 0% of each run, Pallas kernels for 24% -> 25%
where the time goes in v6:
time: 65.4 us; the launch traced here: 64.4 us
  Pallas kernels  26.7 us (41%)
  blocking collectives  24.5 us (37%)
  starting transfers between devices  7.1 us (11%)
  waiting for transfers between devices  5.45 us (8%)
  between operations  0.66 us (1%)
    all_to_all x1, blocking collectives, exchange(): return lax.all_to_all(slots, AXES, split_axis=0, concat_axis=0, tiled=True)  24.5 us
    pallas_call x1, Pallas kernels, body(): pl.pallas_call(encode_kernel, grid=(users // span,), in_specs=[pl.BlockSp...  9.3 us
    all_to_all x1, starting transfers between devices, exchange(): return lax.all_to_all(slots, AXES, split_axis=0, concat_axis=0, tiled=True)  7.1 us
    pallas_call x1, Pallas kernels, body(): pl.pallas_call(functools.partial(own_kernel, cap), grid=(count // step,),...  6.57 us
    all_to_all x1, waiting for transfers between devices, exchange(): return lax.all_to_all(slots, AXES, split_axis=0, concat_axis=0, tiled=True)  5.45 us
    pallas_call x1, Pallas kernels, body(): pl.pallas_call(functools.partial(attend_kernel, cap), in_specs=[pl.BlockS...  5.28 us
    pallas_call x1, Pallas kernels, body(): pl.pallas_call(functools.partial(dispatch_kernel, cap), in_specs=[anywher...  3.97 us
    pallas_call x1, Pallas kernels, body(): pl.pallas_call(answer_kernel, in_specs=[pl.BlockSpec(memory_space=pltpu.V...  1.6 us
  transfers between devices with their start and end apart: 1, of which 1 were waited for; matrix products, arithmetic and copies ran while one was open for 0% of the time, Pallas kernels for 25%

profile of v6, /device:TPU:1, one launch (start us, length us, event | category | flops | bytes accessed | tf_op | source)
XLA Modules:
  0.0 64.4 jit_solution(13504055777865328644)
XLA Ops:
  0.6 4.0 %dispatch.1 = bf16[32,104,128]{2,1,0:T(8,128)(2,1)} custom-call(bf16[512,1024]{1,0:T(8,128)(2,1)} %cand_ref.1, f32[1,1024]{1,0:T(1,128)} %bitcast.7, bf16[1024,2048]{1,0:T(8,128)(2,1)} %w_ref.1, s32[1,512]{1,0:T(1,128)} %bitcast.11, s32[1,512]{1,0:T(1,128)} %bitcast.10), custom_call_target="tpu_custom_call" | custom-call | flops 939524096 | bytes 4194304 | tf_op jit(solution)/shard_map/dispatch/pallas_call | solution.py:273
  4.6 7.1 %all-to-all-start = ((bf16[32,104,128]{2,1,0:T(8,128)(2,1)}), bf16[32,104,128]{2,1,0:T(8,128)(2,1)S(1)}, u32[]{:S(2)}, u32[]{:S(2)}) async-start(bf16[32,104,128]{2,1,0:T(8,128)(2,1)} %dispatch.1), calls=%async_computation | async-start | bytes 1703936 | tf_op jit(solution)/shard_map/all_to_all | solution.py:252
  11.7 6.6 %own.1 = (bf16[512,512]{1,0:T(8,128)(2,1)S(1)}, bf16[512,512]{1,0:T(8,128)(2,1)S(1)}, bf16[512,768]{1,0:T(8,128)(2,1)S(1)}) custom-call(bf16[512,1024]{1,0:T(8,128)(2,1)} %cand_ref.1, f32[1,1024]{1,0:T(1,128)} %bitcast.8, bf16[1024,2048]{1,0:T(8,128)(2,1)} %w_ref.1, s32[1,512]{1,0:T(1,128)} %bitcast.12), custom_call_target="tpu_custom_call" | custom-call | flops 2147483648 | bytes 6291456 | tf_op jit(solution)/shard_map/own/pallas_call | solution.py:326
  18.3 9.3 %encode.1 = (bf16[12,128,1024]{2,1,0:T(8,128)(2,1)}, bf16[4,768,256]{2,1,0:T(8,128)(2,1)}, bf16[4,768,256]{2,1,0:T(8,128)(2,1)}) custom-call(s32[12]{0:T(128)} %len_ref.1, bf16[12,128,1024]{2,1,0:T(8,128)(2,1)} %hist_ref.1, f32[1,1024]{1,0:T(1,128)} %bitcast.9, bf16[1024,2048]{1,0:T(8,128)(2,1)} %w_ref.1, bf16[1024,2048]{1,0:T(8,128)(2,1)} %w_ref.1), custom_call_target="tpu_custom_call" | custom-call | flops 3221225472 | bytes 12582912 | tf_op jit(solution)/shard_map/encode/pallas_call | solution.py:300
  27.6 5.5 %all-to-all-done.arrived_ref = bf16[32,104,128]{2,1,0:T(8,128)(2,1)S(1)} async-done(((bf16[32,104,128]{2,1,0:T(8,128)(2,1)}), bf16[32,104,128]{2,1,0:T(8,128)(2,1)S(1)}, u32[]{:S(2)}, u32[]{:S(2)}) %all-to-all-start) | async-done | bytes 852000 | tf_op jit(solution)/shard_map/all_to_all | solution.py:252
  33.0 5.3 %attend.1 = bf16[768,512]{1,0:T(8,128)(2,1)} custom-call(bf16[32,104,128]{2,1,0:T(8,128)(2,1)S(1)} %all-to-all-done.arrived_ref, bf16[4,768,256]{2,1,0:T(8,128)(2,1)} %get-tuple-element.9.k_hbm, bf16[4,768,256]{2,1,0:T(8,128)(2,1)} %get-tuple-element.10.v_hbm, bf16[512,512]{1,0:T(8,128)(2,1)S(1)} %get-tuple-element.11._.self_ref), custom_call_target="tpu_custom_call" | custom-call | flops 2415919104 | bytes 6291456 | tf_op jit(solution)/shard_map/attend/pallas_call | solution.py:348
  38.3 24.5 %all_to_all.10 = bf16[32,24,512]{2,1,0:T(8,128)(2,1)S(1)} all-to-all(bf16[32,24,512]{2,1,0:T(8,128)(2,1)} %bitcast.6), channel_id=1, replica_groups=mesh['grp'=4,'enc'=8] {'grp','enc'}, dimensions={0} | all-to-all | bytes 1572864 | tf_op jit(solution)/shard_map/all_to_all | solution.py:252
  62.8 1.6 %answer.1 = bf16[512,512]{1,0:T(8,128)(2,1)} custom-call(bf16[768,512]{1,0:T(8,128)(2,1)S(1)} %bitcast.5, bf16[512,512]{1,0:T(8,128)(2,1)S(1)} %get-tuple-element.12.u_ref, bf16[512,512]{1,0:T(8,128)(2,1)S(1)} %get-tuple-element.11._.self_ref, bf16[512,768]{1,0:T(8,128)(2,1)S(1)} %get-tuple-element.13.pick_ref), custom_call_target="tpu_custom_call" | custom-call | flops 402653184 | bytes 4194304 | tf_op jit(solution)/shard_map/answer/pallas_call | solution.py:370
Async XLA Ops:
  4.6 28.4 %all-to-all-start = ((bf16[32,104,128]{2,1,0:T(8,128)(2,1)}), bf16[32,104,128]{2,1,0:T(8,128)(2,1)S(1)}, u32[]{:S(2)}, u32[]{:S(2)}) async-start(bf16[32,104,128]{2,1,0:T(8,128)(2,1)} %dispatch.1), calls=%async_computation | async-start | bytes 1703936 | tf_op jit(solution)/shard_map/all_to_all | solution.py:252

commit v7 on v6

--- a/solution.py
+++ b/solution.py
@@ -165,22 +165,21 @@
 
 
 def attend_kernel(
-    cap, arrived_ref, k_hbm, v_hbm, _, out_hbm, k_ref, v_ref, out_ref, mask_ref, odd_ref, k_sem, v_sem, out_sem
+    cap, arrived_ref, k_ref, v_hbm, out_hbm, v_ref, out_ref, mask_ref, odd_ref, v_sem, out_sem
 ):
     n_dev = arrived_ref.shape[0]
     heads, depth = k_ref.shape[0], k_ref.shape[1]
     total = n_dev * cap
     pairs = depth // HDIM
-    groups = k_sem.shape[0]
+    groups = v_sem.shape[0]
     each = heads // groups
 
-    def load(hbm, ref, sem, g):
+    def load(g):
         at = pl.ds(g * each, each)
-        return pltpu.make_async_copy(hbm.at[at], ref.at[at], sem.at[g])
+        return pltpu.make_async_copy(v_hbm.at[at], v_ref.at[at], v_sem.at[g])
 
     for g in range(groups):
-        load(k_hbm, k_ref, k_sem, g).start()
-        load(v_hbm, v_ref, v_sem, g).start()
+        load(g).start()
 
     full = (n_dev, cap, 128)
     table = arrived_ref[:, heads * cap : heads * cap + 8, :].astype(F32)[:, 0:1, :]
@@ -202,14 +201,13 @@
     @pl.loop(0, groups)
     def _(g):
         members = [g * each + t for t in range(each)]
-        load(k_hbm, k_ref, k_sem, g).wait()
         scores = []
         for h in members:
             rows = pl.ds(pl.multiple_of(h * cap, cap), cap)
             query = arrived_ref[:, rows, :].astype(F32).reshape(total, HDIM).astype(BF16)
             scores.append(mm(spread(query), k_ref[h]))
         weights = [silu(chosen(score) * HDIM ** (-0.5)).astype(BF16) for score in scores]
-        load(v_hbm, v_ref, v_sem, g).wait()
+        load(g).wait()
         for h, weight in zip(members, weights):
             cols = pl.ds(pl.multiple_of(h * HDIM, HDIM), HDIM)
             out_ref[:, cols] = chosen(mm(spread(weight), v_ref[h])).astype(BF16)
@@ -314,7 +312,7 @@
         ],
         out_shape=[
             shape((users, rows, 2 * width), BF16),
-            pltpu.HBM((heads, users * HDIM // 2, 2 * rows), BF16),
+            pltpu.VMEM((heads, users * HDIM // 2, 2 * rows), BF16),
             pltpu.HBM((heads, users * rows // 2, 2 * HDIM), BF16),
         ],
         compiler_params=params(),
@@ -344,26 +342,23 @@
         name="own",
     )(cand, gain, w_proj, owner)
 
-    kv_shape = (heads, users * HDIM // 2, 2 * rows)
     attended = pl.pallas_call(
         functools.partial(attend_kernel, cap),
-        in_specs=[pl.BlockSpec(memory_space=pltpu.VMEM), anywhere, anywhere, anywhere],
+        in_specs=[pl.BlockSpec(memory_space=pltpu.VMEM), pl.BlockSpec(memory_space=pltpu.VMEM), anywhere],
         out_specs=anywhere,
         out_shape=pltpu.HBM((total, width), BF16),
         scratch_shapes=[
-            pltpu.VMEM(kv_shape, BF16),
-            pltpu.VMEM(kv_shape, BF16),
+            pltpu.VMEM((heads, users * rows // 2, 2 * HDIM), BF16),
             pltpu.VMEM((total, width), BF16),
             pltpu.VMEM((total, users * 64), BF16),
             pltpu.VMEM((total, 128), F32),
             dma((heads // 2,)),
-            dma((heads // 2,)),
             dma((1,)),
         ],
         compiler_params=params(),
         cost_estimate=cost(2 * total * rows * users * width * 2, 6 << 20),
         name="attend",
-    )(in_vmem(arrived), in_hbm(keys), in_hbm(values), own)
+    )(in_vmem(arrived), in_vmem(keys), in_hbm(values))
 
     back = exchange(attended.reshape(n_dev, cap, width)).reshape(total, width)
 

time: 65.4 us -> 64.7 us (0.989)
  blocking collectives: 24.5 us -> 0 us
  waiting for transfers between devices: 5.45 us -> 25.7 us
  starting transfers between devices: 7.1 us -> 11.4 us
  Pallas kernels: 26.7 us -> 25.9 us
    all_to_all x1 -> x0, blocking collectives: 24.5 us -> none  [exchange(): return lax.all_to_all(slots, AXES, split_axis=0, concat_axis=0, tiled=True)]
    all_to_all x1 -> x2, waiting for transfers between devices: 5.45 us -> 25.7 us  [exchange(): return lax.all_to_all(slots, AXES, split_axis=0, concat_axis=0, tiled=True)]
    all_to_all x1 -> x2, starting transfers between devices: 7.1 us -> 11.4 us  [exchange(): return lax.all_to_all(slots, AXES, split_axis=0, concat_axis=0, tiled=True)]
    pallas_call x1, Pallas kernels: 5.28 us -> 4.56 us  [body(): pl.pallas_call(functools.partial(attend_kernel, cap), in_specs=[pl.BlockS...]
  transfers between devices with their start and end apart: 1 -> 2, of which waited for: 1 -> 2; matrix products, arithmetic and copies ran while one was open for 0% -> 0% of each run, Pallas kernels for 25% -> 25%
where the time goes in v7:
time: 64.7 us; the launch traced here: 63.7 us
  Pallas kernels  25.9 us (40%)
  waiting for transfers between devices  25.7 us (40%)
  starting transfers between devices  11.4 us (18%)
  between operations  0.67 us (1%)
    all_to_all x2, waiting for transfers between devices, exchange(): return lax.all_to_all(slots, AXES, split_axis=0, concat_axis=0, tiled=True)  25.7 us
    all_to_all x2, starting transfers between devices, exchange(): return lax.all_to_all(slots, AXES, split_axis=0, concat_axis=0, tiled=True)  11.4 us
    pallas_call x1, Pallas kernels, body(): pl.pallas_call(encode_kernel, grid=(users // span,), in_specs=[pl.BlockSp...  9.18 us
    pallas_call x1, Pallas kernels, body(): pl.pallas_call(functools.partial(own_kernel, cap), grid=(count // step,),...  6.57 us
    pallas_call x1, Pallas kernels, body(): pl.pallas_call(functools.partial(attend_kernel, cap), in_specs=[pl.BlockS...  4.56 us
    pallas_call x1, Pallas kernels, body(): pl.pallas_call(functools.partial(dispatch_kernel, cap), in_specs=[anywher...  3.97 us
    pallas_call x1, Pallas kernels, body(): pl.pallas_call(answer_kernel, in_specs=[pl.BlockSpec(memory_space=pltpu.V...  1.6 us
  transfers between devices with their start and end apart: 2, of which 2 were waited for; matrix products, arithmetic and copies ran while one was open for 0% of the time, Pallas kernels for 25%

profile of v7, /device:TPU:1, one launch (start us, length us, event | category | flops | bytes accessed | tf_op | source)
XLA Modules:
  0.0 63.7 jit_solution(7615754468683709284)
XLA Ops:
  0.6 4.0 %dispatch.1 = bf16[32,104,128]{2,1,0:T(8,128)(2,1)} custom-call(bf16[512,1024]{1,0:T(8,128)(2,1)} %cand_ref.1, f32[1,1024]{1,0:T(1,128)} %bitcast.7, bf16[1024,2048]{1,0:T(8,128)(2,1)} %w_ref.1, s32[1,512]{1,0:T(1,128)} %bitcast.11, s32[1,512]{1,0:T(1,128)} %bitcast.10), custom_call_target="tpu_custom_call" | custom-call | flops 939524096 | bytes 4194304 | tf_op jit(solution)/shard_map/dispatch/pallas_call | solution.py:271
  4.6 7.1 %all-to-all-start = ((bf16[32,104,128]{2,1,0:T(8,128)(2,1)}), bf16[32,104,128]{2,1,0:T(8,128)(2,1)S(1)}, u32[]{:S(2)}, u32[]{:S(2)}) async-start(bf16[32,104,128]{2,1,0:T(8,128)(2,1)} %dispatch.1), calls=%async_computation | async-start | bytes 1703936 | tf_op jit(solution)/shard_map/all_to_all | solution.py:250
  11.7 9.2 %encode.1 = (bf16[12,128,1024]{2,1,0:T(8,128)(2,1)}, bf16[4,768,256]{2,1,0:T(8,128)(2,1)S(1)}, bf16[4,768,256]{2,1,0:T(8,128)(2,1)}) custom-call(s32[12]{0:T(128)} %len_ref.1, bf16[12,128,1024]{2,1,0:T(8,128)(2,1)} %hist_ref.1, f32[1,1024]{1,0:T(1,128)} %bitcast.8, bf16[1024,2048]{1,0:T(8,128)(2,1)} %w_ref.1, bf16[1024,2048]{1,0:T(8,128)(2,1)} %w_ref.1), custom_call_target="tpu_custom_call" | custom-call | flops 3221225472 | bytes 12582912 | tf_op jit(solution)/shard_map/encode/pallas_call | solution.py:298
  20.9 12.2 %all-to-all-done.arrived_ref = bf16[32,104,128]{2,1,0:T(8,128)(2,1)S(1)} async-done(((bf16[32,104,128]{2,1,0:T(8,128)(2,1)}), bf16[32,104,128]{2,1,0:T(8,128)(2,1)S(1)}, u32[]{:S(2)}, u32[]{:S(2)}) %all-to-all-start) | async-done | bytes 852000 | tf_op jit(solution)/shard_map/all_to_all | solution.py:250
  33.0 4.6 %attend.1 = bf16[768,512]{1,0:T(8,128)(2,1)} custom-call(bf16[32,104,128]{2,1,0:T(8,128)(2,1)S(1)} %all-to-all-done.arrived_ref, bf16[4,768,256]{2,1,0:T(8,128)(2,1)S(1)} %get-tuple-element.9.k_ref, bf16[4,768,256]{2,1,0:T(8,128)(2,1)} %get-tuple-element.10.v_hbm), custom_call_target="tpu_custom_call" | custom-call | flops 2415919104 | bytes 6291456 | tf_op jit(solution)/shard_map/attend/pallas_call | solution.py:345
  37.6 4.3 %all-to-all-start.1 = ((bf16[32,24,512]{2,1,0:T(8,128)(2,1)}), bf16[32,24,512]{2,1,0:T(8,128)(2,1)S(1)}, u32[]{:S(2)}, u32[]{:S(2)}) async-start(bf16[32,24,512]{2,1,0:T(8,128)(2,1)} %bitcast.6), calls=%async_computation.1 | async-start | bytes 1572864 | tf_op jit(solution)/shard_map/all_to_all | solution.py:250
  41.9 6.6 %own.1 = (bf16[512,512]{1,0:T(8,128)(2,1)S(1)}, bf16[512,512]{1,0:T(8,128)(2,1)S(1)}, bf16[512,768]{1,0:T(8,128)(2,1)S(1)}) custom-call(bf16[512,1024]{1,0:T(8,128)(2,1)} %cand_ref.1, f32[1,1024]{1,0:T(1,128)} %bitcast.9, bf16[1024,2048]{1,0:T(8,128)(2,1)} %w_ref.1, s32[1,512]{1,0:T(1,128)} %bitcast.12), custom_call_target="tpu_custom_call" | custom-call | flops 2147483648 | bytes 6291456 | tf_op jit(solution)/shard_map/own/pallas_call | solution.py:324
  48.5 13.6 %all-to-all-done.1 = bf16[32,24,512]{2,1,0:T(8,128)(2,1)S(1)} async-done(((bf16[32,24,512]{2,1,0:T(8,128)(2,1)}), bf16[32,24,512]{2,1,0:T(8,128)(2,1)S(1)}, u32[]{:S(2)}, u32[]{:S(2)}) %all-to-all-start.1) | async-done | bytes 786464 | tf_op jit(solution)/shard_map/all_to_all | solution.py:250
  62.1 1.6 %answer.1 = bf16[512,512]{1,0:T(8,128)(2,1)} custom-call(bf16[768,512]{1,0:T(8,128)(2,1)S(1)} %bitcast.5, bf16[512,512]{1,0:T(8,128)(2,1)S(1)} %get-tuple-element.11.u_ref, bf16[512,512]{1,0:T(8,128)(2,1)S(1)} %get-tuple-element.12.self_ref, bf16[512,768]{1,0:T(8,128)(2,1)S(1)} %get-tuple-element.13.pick_ref), custom_call_target="tpu_custom_call" | custom-call | flops 402653184 | bytes 4194304 | tf_op jit(solution)/shard_map/answer/pallas_call | solution.py:365
Async XLA Ops:
  4.6 28.4 %all-to-all-start = ((bf16[32,104,128]{2,1,0:T(8,128)(2,1)}), bf16[32,104,128]{2,1,0:T(8,128)(2,1)S(1)}, u32[]{:S(2)}, u32[]{:S(2)}) async-start(bf16[32,104,128]{2,1,0:T(8,128)(2,1)} %dispatch.1), calls=%async_computation | async-start | bytes 1703936 | tf_op jit(solution)/shard_map/all_to_all | solution.py:250
  37.6 24.5 %all-to-all-start.1 = ((bf16[32,24,512]{2,1,0:T(8,128)(2,1)}), bf16[32,24,512]{2,1,0:T(8,128)(2,1)S(1)}, u32[]{:S(2)}, u32[]{:S(2)}) async-start(bf16[32,24,512]{2,1,0:T(8,128)(2,1)} %bitcast.6), calls=%async_computation.1 | async-start | bytes 1572864 | tf_op jit(solution)/shard_map/all_to_all | solution.py:250

commit v8 on v7

--- a/solution.py
+++ b/solution.py
@@ -53,8 +53,8 @@
 
 
 def dispatch_kernel(
-    cap, cand_hbm, gain_hbm, w_hbm, owner_hbm, user_hbm, out_hbm,
-    cand_ref, gain_ref, wq_ref, owner_ref, user_ref, out_ref, q_ref, pick_ref, small_sem, cand_sem, w_sem, out_sem,
+    cap, cand_hbm, gain_hbm, w_hbm, owner_hbm, user_hbm, out_ref,
+    cand_ref, gain_ref, wq_ref, owner_ref, user_ref, q_ref, pick_ref, small_sem, cand_sem, w_sem,
 ):
     n_dev = out_ref.shape[0]
     count, width = q_ref.shape
@@ -96,20 +96,10 @@
         center = x - jnp.mean(x, axis=-1, keepdims=True)
         scale = lax.rsqrt(jnp.mean(center * center, axis=-1, keepdims=True) + 1e-05)
         q_ref[rows, :] = silu(mm((center * gain).astype(BF16), wq_ref[...]) * scale).astype(BF16)
-    stores = []
-    groups = out_sem.shape[0]
-    span = n_dev // groups
-    for g in range(groups):
-        devs = slice(g * span, (g + 1) * span)
-        sent = mm(pick_ref[g * span * cap : (g + 1) * span * cap, :], q_ref[...])
-        for h in range(heads):
-            part = sent[:, h * HDIM : (h + 1) * HDIM].reshape(span, cap, HDIM)
-            out_ref[devs, h * cap : (h + 1) * cap, :] = part.astype(BF16)
-        at = pl.ds(g * span, span)
-        stores.append(pltpu.make_async_copy(out_ref.at[at], out_hbm.at[at], out_sem.at[g]))
-        stores[-1].start()
-    for copy in stores:
-        copy.wait()
+    sent = mm(pick_ref[...], q_ref[...])
+    for h in range(heads):
+        part = sent[:, h * HDIM : (h + 1) * HDIM].reshape(n_dev, cap, HDIM)
+        out_ref[:, h * cap : (h + 1) * cap, :] = part.astype(BF16)
 
 
 def encode_kernel(len_ref, hist_ref, gain_ref, wv_ref, wk_ref, out_ref, key_ref, value_ref):
@@ -165,7 +155,7 @@
 
 
 def attend_kernel(
-    cap, arrived_ref, k_ref, v_hbm, out_hbm, v_ref, out_ref, mask_ref, odd_ref, v_sem, out_sem
+    cap, arrived_ref, k_ref, v_hbm, out_ref, v_ref, mask_ref, odd_ref, v_sem
 ):
     n_dev = arrived_ref.shape[0]
     heads, depth = k_ref.shape[0], k_ref.shape[1]
@@ -212,10 +202,6 @@
             cols = pl.ds(pl.multiple_of(h * HDIM, HDIM), HDIM)
             out_ref[:, cols] = chosen(mm(spread(weight), v_ref[h])).astype(BF16)
 
-    copy = pltpu.make_async_copy(out_ref, out_hbm, out_sem.at[0])
-    copy.start()
-    copy.wait()
-
 
 def answer_kernel(back_ref, u_ref, self_ref, pick_ref, out_ref):
     normed = norm_rows(mm(pick_ref[...], back_ref[...]) + self_ref[...].astype(F32))
@@ -271,20 +257,18 @@
     outgoing = pl.pallas_call(
         functools.partial(dispatch_kernel, cap),
         in_specs=[anywhere] * 5,
-        out_specs=anywhere,
-        out_shape=pltpu.HBM((n_dev, heads * cap + 8, HDIM), BF16),
+        out_specs=pl.BlockSpec(memory_space=pltpu.VMEM),
+        out_shape=pltpu.VMEM((n_dev, heads * cap + 8, HDIM), BF16),
         scratch_shapes=[
             pltpu.VMEM((count, dim), BF16),
             pltpu.VMEM((1, dim), F32),
             pltpu.VMEM((dim, width), BF16),
             pltpu.VMEM((1, count), jnp.int32),
             pltpu.VMEM((1, count), jnp.int32),
-            pltpu.VMEM((n_dev, heads * cap + 8, HDIM), BF16),
             pltpu.VMEM((count, width), BF16),
             pltpu.VMEM((total, count), BF16),
             dma((3,)),
             dma((parts,)),
-            dma((1,)),
             dma((1,)),
         ],
         compiler_params=params(),
@@ -345,15 +329,13 @@
     attended = pl.pallas_call(
         functools.partial(attend_kernel, cap),
         in_specs=[pl.BlockSpec(memory_space=pltpu.VMEM), pl.BlockSpec(memory_space=pltpu.VMEM), anywhere],
-        out_specs=anywhere,
-        out_shape=pltpu.HBM((total, width), BF16),
+        out_specs=pl.BlockSpec(memory_space=pltpu.VMEM),
+        out_shape=pltpu.VMEM((total, width), BF16),
         scratch_shapes=[
             pltpu.VMEM((heads, users * rows // 2, 2 * HDIM), BF16),
-            pltpu.VMEM((total, width), BF16),
             pltpu.VMEM((total, users * 64), BF16),
             pltpu.VMEM((total, 128), F32),
             dma((heads // 2,)),
-            dma((1,)),
         ],
         compiler_params=params(),
         cost_estimate=cost(2 * total * rows * users * width * 2, 6 << 20),

time: 64.7 us -> 64.7 us (level)
  no operation moved by 1% of the time
where the time goes in v8:
time: 64.7 us; the launch traced here: 63.7 us
  Pallas kernels  25.9 us (40%)
  waiting for transfers between devices  25.7 us (40%)
  starting transfers between devices  11.4 us (18%)
  between operations  0.67 us (1%)
    all_to_all x2, waiting for transfers between devices, exchange(): return lax.all_to_all(slots, AXES, split_axis=0, concat_axis=0, tiled=True)  25.7 us
    all_to_all x2, starting transfers between devices, exchange(): return lax.all_to_all(slots, AXES, split_axis=0, concat_axis=0, tiled=True)  11.4 us
    pallas_call x1, Pallas kernels, body(): pl.pallas_call(encode_kernel, grid=(users // span,), in_specs=[pl.BlockSp...  9.18 us
    pallas_call x1, Pallas kernels, body(): pl.pallas_call(functools.partial(own_kernel, cap), grid=(count // step,),...  6.57 us
    pallas_call x1, Pallas kernels, body(): pl.pallas_call(functools.partial(attend_kernel, cap), in_specs=[pl.BlockS...  4.55 us
    pallas_call x1, Pallas kernels, body(): pl.pallas_call(functools.partial(dispatch_kernel, cap), in_specs=[anywher...  3.96 us
    pallas_call x1, Pallas kernels, body(): pl.pallas_call(answer_kernel, in_specs=[pl.BlockSpec(memory_space=pltpu.V...  1.6 us
  transfers between devices with their start and end apart: 2, of which 2 were waited for; matrix products, arithmetic and copies ran while one was open for 0% of the time, Pallas kernels for 25%

profile of v8, /device:TPU:1, one launch (start us, length us, event | category | flops | bytes accessed | tf_op | source)
XLA Modules:
  0.0 63.7 jit_solution(10859633166942745242)
XLA Ops:
  0.6 4.0 %dispatch.1 = bf16[32,104,128]{2,1,0:T(8,128)(2,1)} custom-call(bf16[512,1024]{1,0:T(8,128)(2,1)} %cand_ref.1, f32[1,1024]{1,0:T(1,128)} %bitcast.6, bf16[1024,2048]{1,0:T(8,128)(2,1)} %w_ref.1, s32[1,512]{1,0:T(1,128)} %bitcast.10, s32[1,512]{1,0:T(1,128)} %bitcast.9), custom_call_target="tpu_custom_call" | custom-call | flops 939524096 | bytes 4194304 | tf_op jit(solution)/shard_map/dispatch/pallas_call | solution.py:257
  4.6 7.1 %all-to-all-start = ((bf16[32,104,128]{2,1,0:T(8,128)(2,1)}), bf16[32,104,128]{2,1,0:T(8,128)(2,1)S(1)}, u32[]{:S(2)}, u32[]{:S(2)}) async-start(bf16[32,104,128]{2,1,0:T(8,128)(2,1)} %dispatch.1), calls=%async_computation | async-start | bytes 1703936 | tf_op jit(solution)/shard_map/all_to_all | solution.py:236
  11.7 9.2 %encode.1 = (bf16[12,128,1024]{2,1,0:T(8,128)(2,1)}, bf16[4,768,256]{2,1,0:T(8,128)(2,1)S(1)}, bf16[4,768,256]{2,1,0:T(8,128)(2,1)}) custom-call(s32[12]{0:T(128)} %len_ref.1, bf16[12,128,1024]{2,1,0:T(8,128)(2,1)} %hist_ref.1, f32[1,1024]{1,0:T(1,128)} %bitcast.7, bf16[1024,2048]{1,0:T(8,128)(2,1)} %w_ref.1, bf16[1024,2048]{1,0:T(8,128)(2,1)} %w_ref.1), custom_call_target="tpu_custom_call" | custom-call | flops 3221225472 | bytes 12582912 | tf_op jit(solution)/shard_map/encode/pallas_call | solution.py:282
  20.9 12.2 %all-to-all-done.arrived_ref = bf16[32,104,128]{2,1,0:T(8,128)(2,1)S(1)} async-done(((bf16[32,104,128]{2,1,0:T(8,128)(2,1)}), bf16[32,104,128]{2,1,0:T(8,128)(2,1)S(1)}, u32[]{:S(2)}, u32[]{:S(2)}) %all-to-all-start) | async-done | bytes 852000 | tf_op jit(solution)/shard_map/all_to_all | solution.py:236
  33.0 4.5 %attend.1 = bf16[768,512]{1,0:T(8,128)(2,1)} custom-call(bf16[32,104,128]{2,1,0:T(8,128)(2,1)S(1)} %all-to-all-done.arrived_ref, bf16[4,768,256]{2,1,0:T(8,128)(2,1)S(1)} %get-tuple-element.9.k_ref, bf16[4,768,256]{2,1,0:T(8,128)(2,1)} %get-tuple-element.10.v_hbm), custom_call_target="tpu_custom_call" | custom-call | flops 2415919104 | bytes 6291456 | tf_op jit(solution)/shard_map/attend/pallas_call | solution.py:329
  37.6 4.3 %all-to-all-start.1 = ((bf16[32,24,512]{2,1,0:T(8,128)(2,1)}), bf16[32,24,512]{2,1,0:T(8,128)(2,1)S(1)}, u32[]{:S(2)}, u32[]{:S(2)}) async-start(bf16[32,24,512]{2,1,0:T(8,128)(2,1)} %bitcast.3), calls=%async_computation.1 | async-start | bytes 1572864 | tf_op jit(solution)/shard_map/all_to_all | solution.py:236
  41.9 6.6 %own.1 = (bf16[512,512]{1,0:T(8,128)(2,1)S(1)}, bf16[512,512]{1,0:T(8,128)(2,1)S(1)}, bf16[512,768]{1,0:T(8,128)(2,1)S(1)}) custom-call(bf16[512,1024]{1,0:T(8,128)(2,1)} %cand_ref.1, f32[1,1024]{1,0:T(1,128)} %bitcast.8, bf16[1024,2048]{1,0:T(8,128)(2,1)} %w_ref.1, s32[1,512]{1,0:T(1,128)} %bitcast.11), custom_call_target="tpu_custom_call" | custom-call | flops 2147483648 | bytes 6291456 | tf_op jit(solution)/shard_map/own/pallas_call | solution.py:308
  48.5 13.6 %all-to-all-done.1 = bf16[32,24,512]{2,1,0:T(8,128)(2,1)S(1)} async-done(((bf16[32,24,512]{2,1,0:T(8,128)(2,1)}), bf16[32,24,512]{2,1,0:T(8,128)(2,1)S(1)}, u32[]{:S(2)}, u32[]{:S(2)}) %all-to-all-start.1) | async-done | bytes 786464 | tf_op jit(solution)/shard_map/all_to_all | solution.py:236
  62.1 1.6 %answer.1 = bf16[512,512]{1,0:T(8,128)(2,1)} custom-call(bf16[768,512]{1,0:T(8,128)(2,1)S(1)} %bitcast.5, bf16[512,512]{1,0:T(8,128)(2,1)S(1)} %get-tuple-element.11.u_ref, bf16[512,512]{1,0:T(8,128)(2,1)S(1)} %get-tuple-element.12.self_ref, bf16[512,768]{1,0:T(8,128)(2,1)S(1)} %get-tuple-element.13.pick_ref), custom_call_target="tpu_custom_call" | custom-call | flops 402653184 | bytes 4194304 | tf_op jit(solution)/shard_map/answer/pallas_call | solution.py:347
Async XLA Ops:
  4.6 28.4 %all-to-all-start = ((bf16[32,104,128]{2,1,0:T(8,128)(2,1)}), bf16[32,104,128]{2,1,0:T(8,128)(2,1)S(1)}, u32[]{:S(2)}, u32[]{:S(2)}) async-start(bf16[32,104,128]{2,1,0:T(8,128)(2,1)} %dispatch.1), calls=%async_computation | async-start | bytes 1703936 | tf_op jit(solution)/shard_map/all_to_all | solution.py:236
  37.6 24.5 %all-to-all-start.1 = ((bf16[32,24,512]{2,1,0:T(8,128)(2,1)}), bf16[32,24,512]{2,1,0:T(8,128)(2,1)S(1)}, u32[]{:S(2)}, u32[]{:S(2)}) async-start(bf16[32,24,512]{2,1,0:T(8,128)(2,1)} %bitcast.3), calls=%async_computation.1 | async-start | bytes 1572864 | tf_op jit(solution)/shard_map/all_to_all | solution.py:236

commit v9 on v7

--- a/solution.py
+++ b/solution.py
@@ -112,7 +112,7 @@
         copy.wait()
 
 
-def encode_kernel(len_ref, hist_ref, gain_ref, wv_ref, wk_ref, out_ref, key_ref, value_ref):
+def encode_kernel(len_ref, hist_ref, gain_ref, wv_ref, wk_ref, out_ref, near_ref, far_ref, value_ref):
     users, rows, dim = hist_ref.shape
     width = wk_ref.shape[1]
     first = pl.program_id(0) * users
@@ -132,7 +132,8 @@
         out_ref[u, :, width:] = value
         for h in range(width // HDIM):
             cols = slice(h * HDIM, (h + 1) * HDIM)
-            key_ref[h, pair, side] = key[:, cols].T.astype(BF16)
+            key_ref, at = (near_ref, h) if h < near_ref.shape[0] else (far_ref, h - near_ref.shape[0])
+            key_ref[at, pair, side] = key[:, cols].T.astype(BF16)
             value_ref[h, pair, side] = value[:, cols]
 
 
@@ -165,10 +166,10 @@
 
 
 def attend_kernel(
-    cap, arrived_ref, k_ref, v_hbm, out_hbm, v_ref, out_ref, mask_ref, odd_ref, v_sem, out_sem
+    cap, arrived_ref, near_ref, far_hbm, v_hbm, _, out_ref, far_ref, v_ref, mask_ref, odd_ref, far_sem, v_sem
 ):
     n_dev = arrived_ref.shape[0]
-    heads, depth = k_ref.shape[0], k_ref.shape[1]
+    heads, depth = v_ref.shape[0], v_ref.shape[1]
     total = n_dev * cap
     pairs = depth // HDIM
     groups = v_sem.shape[0]
@@ -178,7 +179,10 @@
         at = pl.ds(g * each, each)
         return pltpu.make_async_copy(v_hbm.at[at], v_ref.at[at], v_sem.at[g])
 
-    for g in range(groups):
+    far = pltpu.make_async_copy(far_hbm, far_ref, far_sem.at[0])
+    load(0).start()
+    far.start()
+    for g in range(1, groups):
         load(g).start()
 
     full = (n_dev, cap, 128)
@@ -198,23 +202,19 @@
     def chosen(x):
         return jnp.where(odd_ref[...] > 0.5, x[:, 128:], x[:, :128])
 
-    @pl.loop(0, groups)
-    def _(g):
+    for g in range(groups):
         members = [g * each + t for t in range(each)]
+        if g == groups // 2:
+            far.wait()
         scores = []
         for h in members:
-            rows = pl.ds(pl.multiple_of(h * cap, cap), cap)
-            query = arrived_ref[:, rows, :].astype(F32).reshape(total, HDIM).astype(BF16)
-            scores.append(mm(spread(query), k_ref[h]))
+            query = arrived_ref[:, h * cap : (h + 1) * cap, :].astype(F32).reshape(total, HDIM).astype(BF16)
+            key = near_ref[h] if h < near_ref.shape[0] else far_ref[h - near_ref.shape[0]]
+            scores.append(mm(spread(query), key))
         weights = [silu(chosen(score) * HDIM ** (-0.5)).astype(BF16) for score in scores]
         load(g).wait()
         for h, weight in zip(members, weights):
-            cols = pl.ds(pl.multiple_of(h * HDIM, HDIM), HDIM)
-            out_ref[:, cols] = chosen(mm(spread(weight), v_ref[h])).astype(BF16)
-
-    copy = pltpu.make_async_copy(out_ref, out_hbm, out_sem.at[0])
-    copy.start()
-    copy.wait()
+            out_ref[:, h * HDIM : (h + 1) * HDIM] = chosen(mm(spread(weight), v_ref[h])).astype(BF16)
 
 
 def answer_kernel(back_ref, u_ref, self_ref, pick_ref, out_ref):
@@ -285,7 +285,7 @@
             dma((3,)),
             dma((parts,)),
             dma((1,)),
-            dma((1,)),
+            dma((2,)),
         ],
         compiler_params=params(),
         cost_estimate=cost(2 * count * width * (dim + total), 4 << 20),
@@ -295,7 +295,8 @@
     arrived = exchange(outgoing)
 
     span = 4
-    kv_cache, keys, values = pl.pallas_call(
+    half = heads // 2
+    kv_cache, near_keys, far_keys, values = pl.pallas_call(
         encode_kernel,
         grid=(users // span,),
         in_specs=[
@@ -307,12 +308,14 @@
         ],
         out_specs=[
             pl.BlockSpec((span, rows, 2 * width), lambda i: (i, 0, 0)),
-            pl.BlockSpec((heads, span * HDIM // 2, 2 * rows), lambda i: (0, i, 0)),
+            pl.BlockSpec((half, span * HDIM // 2, 2 * rows), lambda i: (0, i, 0)),
+            pl.BlockSpec((half, span * HDIM // 2, 2 * rows), lambda i: (0, i, 0)),
             pl.BlockSpec((heads, span * rows // 2, 2 * HDIM), lambda i: (0, i, 0)),
         ],
         out_shape=[
             shape((users, rows, 2 * width), BF16),
-            pltpu.VMEM((heads, users * HDIM // 2, 2 * rows), BF16),
+            pltpu.VMEM((half, users * HDIM // 2, 2 * rows), BF16),
+            pltpu.HBM((half, users * HDIM // 2, 2 * rows), BF16),
             pltpu.HBM((heads, users * rows // 2, 2 * HDIM), BF16),
         ],
         compiler_params=params(),
@@ -344,21 +347,21 @@
 
     attended = pl.pallas_call(
         functools.partial(attend_kernel, cap),
-        in_specs=[pl.BlockSpec(memory_space=pltpu.VMEM), pl.BlockSpec(memory_space=pltpu.VMEM), anywhere],
-        out_specs=anywhere,
-        out_shape=pltpu.HBM((total, width), BF16),
+        in_specs=[pl.BlockSpec(memory_space=pltpu.VMEM)] * 2 + [anywhere] * 3,
+        out_specs=pl.BlockSpec(memory_space=pltpu.VMEM),
+        out_shape=pltpu.VMEM((total, width), BF16),
         scratch_shapes=[
+            pltpu.VMEM((half, users * HDIM // 2, 2 * rows), BF16),
             pltpu.VMEM((heads, users * rows // 2, 2 * HDIM), BF16),
-            pltpu.VMEM((total, width), BF16),
             pltpu.VMEM((total, users * 64), BF16),
             pltpu.VMEM((total, 128), F32),
+            dma((1,)),
             dma((heads // 2,)),
-            dma((1,)),
         ],
         compiler_params=params(),
         cost_estimate=cost(2 * total * rows * users * width * 2, 6 << 20),
         name="attend",
-    )(in_vmem(arrived), in_vmem(keys), in_hbm(values))
+    )(in_vmem(arrived), in_vmem(near_keys), in_hbm(far_keys), in_hbm(values), own)
 
     back = exchange(attended.reshape(n_dev, cap, width)).reshape(total, width)
 

time: 64.7 us -> 63.3 us (0.978)
  blocking collectives: 0 us -> 24.3 us
  waiting for transfers between devices: 25.7 us -> 5.49 us
  starting transfers between devices: 11.4 us -> 7.1 us
  Pallas kernels: 25.9 us -> 24.9 us
    all_to_all x0 -> x1, blocking collectives: none -> 24.3 us  [exchange(): return lax.all_to_all(slots, AXES, split_axis=0, concat_axis=0, tiled=True)]
    all_to_all x2 -> x1, waiting for transfers between devices: 25.7 us -> 5.49 us  [exchange(): return lax.all_to_all(slots, AXES, split_axis=0, concat_axis=0, tiled=True)]
    all_to_all x2 -> x1, starting transfers between devices: 11.4 us -> 7.1 us  [exchange(): return lax.all_to_all(slots, AXES, split_axis=0, concat_axis=0, tiled=True)]
    pallas_call x1, Pallas kernels: 4.56 us -> 3.51 us  [body(): pl.pallas_call(functools.partial(attend_kernel, cap), in_specs=[pl.BlockS...]
  transfers between devices with their start and end apart: 2 -> 1, of which waited for: 2 -> 1; matrix products, arithmetic and copies ran while one was open for 0% -> 0% of each run, Pallas kernels for 25% -> 25%
where the time goes in v9:
time: 63.3 us; the launch traced here: 62.4 us
  Pallas kernels  24.9 us (39%)
  blocking collectives  24.3 us (38%)
  starting transfers between devices  7.1 us (11%)
  waiting for transfers between devices  5.49 us (9%)
  between operations  0.66 us (1%)
    all_to_all x1, blocking collectives, exchange(): return lax.all_to_all(slots, AXES, split_axis=0, concat_axis=0, tiled=True)  24.3 us
    pallas_call x1, Pallas kernels, body(): pl.pallas_call(encode_kernel, grid=(users // span,), in_specs=[pl.BlockSp...  9.26 us
    all_to_all x1, starting transfers between devices, exchange(): return lax.all_to_all(slots, AXES, split_axis=0, concat_axis=0, tiled=True)  7.1 us
    pallas_call x1, Pallas kernels, body(): pl.pallas_call(functools.partial(own_kernel, cap), grid=(count // step,),...  6.57 us
    all_to_all x1, waiting for transfers between devices, exchange(): return lax.all_to_all(slots, AXES, split_axis=0, concat_axis=0, tiled=True)  5.49 us
    pallas_call x1, Pallas kernels, body(): pl.pallas_call(functools.partial(dispatch_kernel, cap), in_specs=[anywher...  3.92 us
    pallas_call x1, Pallas kernels, body(): pl.pallas_call(functools.partial(attend_kernel, cap), in_specs=[pl.BlockS...  3.51 us
    pallas_call x1, Pallas kernels, body(): pl.pallas_call(answer_kernel, in_specs=[pl.BlockSpec(memory_space=pltpu.V...  1.6 us
  transfers between devices with their start and end apart: 1, of which 1 were waited for; matrix products, arithmetic and copies ran while one was open for 0% of the time, Pallas kernels for 25%

profile of v9, /device:TPU:1, one launch (start us, length us, event | category | flops | bytes accessed | tf_op | source)
XLA Modules:
  0.0 62.4 jit_solution(12230579490036178049)
XLA Ops:
  0.6 3.9 %dispatch.1 = bf16[32,104,128]{2,1,0:T(8,128)(2,1)} custom-call(bf16[512,1024]{1,0:T(8,128)(2,1)} %cand_ref.1, f32[1,1024]{1,0:T(1,128)} %bitcast.7, bf16[1024,2048]{1,0:T(8,128)(2,1)} %w_ref.1, s32[1,512]{1,0:T(1,128)} %bitcast.11, s32[1,512]{1,0:T(1,128)} %bitcast.10), custom_call_target="tpu_custom_call" | custom-call | flops 939524096 | bytes 4194304 | tf_op jit(solution)/shard_map/dispatch/pallas_call | solution.py:271
  4.6 7.1 %all-to-all-start = ((bf16[32,104,128]{2,1,0:T(8,128)(2,1)}), bf16[32,104,128]{2,1,0:T(8,128)(2,1)S(1)}, u32[]{:S(2)}, u32[]{:S(2)}) async-start(bf16[32,104,128]{2,1,0:T(8,128)(2,1)} %dispatch.1), calls=%async_computation | async-start | bytes 1703936 | tf_op jit(solution)/shard_map/all_to_all | solution.py:250
  11.7 6.6 %own.1 = (bf16[512,512]{1,0:T(8,128)(2,1)S(1)}, bf16[512,512]{1,0:T(8,128)(2,1)S(1)}, bf16[512,768]{1,0:T(8,128)(2,1)S(1)}) custom-call(bf16[512,1024]{1,0:T(8,128)(2,1)} %cand_ref.1, f32[1,1024]{1,0:T(1,128)} %bitcast.8, bf16[1024,2048]{1,0:T(8,128)(2,1)} %w_ref.1, s32[1,512]{1,0:T(1,128)} %bitcast.12), custom_call_target="tpu_custom_call" | custom-call | flops 2147483648 | bytes 6291456 | tf_op jit(solution)/shard_map/own/pallas_call | solution.py:327
  18.2 9.3 %encode.1 = (bf16[12,128,1024]{2,1,0:T(8,128)(2,1)}, bf16[2,768,256]{2,1,0:T(8,128)(2,1)S(1)}, bf16[2,768,256]{2,1,0:T(8,128)(2,1)}, bf16[4,768,256]{2,1,0:T(8,128)(2,1)}) custom-call(s32[12]{0:T(128)} %len_ref.1, bf16[12,128,1024]{2,1,0:T(8,128)(2,1)} %hist_ref.1, f32[1,1024]{1,0:T(1,128)} %bitcast.9, bf16[1024,2048]{1,0:T(8,128)(2,1)} %w_ref.1, ...), custom_call_target="tpu_custom_call" | custom-call | flops 3221225472 | bytes 12582912 | tf_op jit(solution)/shard_map/encode/pallas_call | solution.py:299
  27.5 5.5 %all-to-all-done.arrived_ref = bf16[32,104,128]{2,1,0:T(8,128)(2,1)S(1)} async-done(((bf16[32,104,128]{2,1,0:T(8,128)(2,1)}), bf16[32,104,128]{2,1,0:T(8,128)(2,1)S(1)}, u32[]{:S(2)}, u32[]{:S(2)}) %all-to-all-start) | async-done | bytes 852000 | tf_op jit(solution)/shard_map/all_to_all | solution.py:250
  33.0 3.5 %attend.1 = bf16[768,512]{1,0:T(8,128)(2,1)S(1)} custom-call(bf16[32,104,128]{2,1,0:T(8,128)(2,1)S(1)} %all-to-all-done.arrived_ref, bf16[2,768,256]{2,1,0:T(8,128)(2,1)S(1)} %get-tuple-element.10.near_ref, bf16[2,768,256]{2,1,0:T(8,128)(2,1)} %get-tuple-element.11.far_hbm, bf16[4,768,256]{2,1,0:T(8,128)(2,1)} %get-tuple-element.12.v_hbm, ...), custom_call_target="tpu_custom_call" | custom-call | flops 2415919104 | bytes 6291456 | tf_op jit(solution)/shard_map/attend/pallas_call | solution.py:348
  36.5 24.3 %all_to_all.10 = bf16[32,24,512]{2,1,0:T(8,128)(2,1)S(1)} all-to-all(bf16[32,24,512]{2,1,0:T(8,128)(2,1)S(1)} %bitcast.6), channel_id=1, replica_groups=mesh['grp'=4,'enc'=8] {'grp','enc'}, dimensions={0} | all-to-all | bytes 1572864 | tf_op jit(solution)/shard_map/all_to_all | solution.py:250
  60.8 1.6 %answer.1 = bf16[512,512]{1,0:T(8,128)(2,1)} custom-call(bf16[768,512]{1,0:T(8,128)(2,1)S(1)} %bitcast.5, bf16[512,512]{1,0:T(8,128)(2,1)S(1)} %get-tuple-element.14.u_ref, bf16[512,512]{1,0:T(8,128)(2,1)S(1)} %get-tuple-element.13._.self_ref, bf16[512,768]{1,0:T(8,128)(2,1)S(1)} %get-tuple-element.15.pick_ref), custom_call_target="tpu_custom_call" | custom-call | flops 402653184 | bytes 4194304 | tf_op jit(solution)/shard_map/answer/pallas_call | solution.py:368
Async XLA Ops:
  4.6 28.4 %all-to-all-start = ((bf16[32,104,128]{2,1,0:T(8,128)(2,1)}), bf16[32,104,128]{2,1,0:T(8,128)(2,1)S(1)}, u32[]{:S(2)}, u32[]{:S(2)}) async-start(bf16[32,104,128]{2,1,0:T(8,128)(2,1)} %dispatch.1), calls=%async_computation | async-start | bytes 1703936 | tf_op jit(solution)/shard_map/all_to_all | solution.py:250

commit v10 on v9

--- a/solution.py
+++ b/solution.py
@@ -52,8 +52,14 @@
     return named, jnp.sum(rank, axis=0, keepdims=True).astype(jnp.int32)
 
 
+def place_of(owner, n_grp, n_enc):
+    if n_enc & (n_enc - 1):
+        return lax.rem(owner, n_enc) * n_grp + lax.div(owner, n_enc)
+    return (owner & (n_enc - 1)) * n_grp + (owner >> (n_enc.bit_length() - 1))
+
+
 def dispatch_kernel(
-    cap, cand_hbm, gain_hbm, w_hbm, owner_hbm, user_hbm, out_hbm,
+    n_grp, n_enc, cap, cand_hbm, gain_hbm, w_hbm, owner_hbm, user_hbm, out_hbm,
     cand_ref, gain_ref, wq_ref, owner_ref, user_ref, out_ref, q_ref, pick_ref, small_sem, cand_sem, w_sem, out_sem,
 ):
     n_dev = out_ref.shape[0]
@@ -80,7 +86,7 @@
         copy.start()
     for copy in small:
         copy.wait()
-    place = owner_ref[...]
+    place = place_of(owner_ref[...], n_grp, n_enc)
     named, rank = ranks(place, n_dev)
     pick_ref[...] = one_hot(iota((n_dev * cap, count), 0) == place * cap + rank)
     users = jnp.where(named, user_ref[...].astype(F32), 0.0).astype(BF16)
@@ -137,14 +143,14 @@
             value_ref[h, pair, side] = value[:, cols]
 
 
-def own_kernel(cap, cand_ref, gain_ref, w_ref, owner_ref, u_ref, self_ref, pick_ref, slot_ref):
+def own_kernel(n_grp, n_enc, cap, cand_ref, gain_ref, w_ref, owner_ref, u_ref, self_ref, pick_ref, slot_ref):
     step, width = u_ref.shape
     total = pick_ref.shape[1]
     i = pl.program_id(0)
 
     @pl.when(i == 0)
     def _():
-        place = owner_ref[...]
+        place = place_of(owner_ref[...], n_grp, n_enc)
         _, rank = ranks(place, total // cap)
         slot = (place * cap + rank).astype(F32)
         slot_ref[...] = jnp.broadcast_to(slot, (128, slot.shape[1])).T
@@ -204,15 +210,16 @@
 
     for g in range(groups):
         members = [g * each + t for t in range(each)]
-        if g == groups // 2:
-            far.wait()
         scores = []
         for h in members:
             query = arrived_ref[:, h * cap : (h + 1) * cap, :].astype(F32).reshape(total, HDIM).astype(BF16)
             key = near_ref[h] if h < near_ref.shape[0] else far_ref[h - near_ref.shape[0]]
             scores.append(mm(spread(query), key))
         weights = [silu(chosen(score) * HDIM ** (-0.5)).astype(BF16) for score in scores]
-        load(g).wait()
+        if g == 0:
+            load(0).wait()
+            far.wait()
+            load(1).wait()
         for h, weight in zip(members, weights):
             out_ref[:, h * HDIM : (h + 1) * HDIM] = chosen(mm(spread(weight), v_ref[h])).astype(BF16)
 
@@ -247,7 +254,7 @@
 
 
 def exchange(slots):
-    return lax.all_to_all(slots, AXES, split_axis=0, concat_axis=0, tiled=True)
+    return lax.all_to_all(slots, ("enc", "grp"), split_axis=0, concat_axis=0, tiled=True)
 
 
 def body(history, hist_len, cand, cand_owner, cand_user, norm_gain, w_proj):
@@ -255,7 +262,8 @@
     width = w_proj.shape[1] // 4
     heads = width // HDIM
     count = cand.shape[0]
-    n_dev = lax.axis_size("grp") * lax.axis_size("enc")
+    n_grp, n_enc = lax.axis_size("grp"), lax.axis_size("enc")
+    n_dev = n_grp * n_enc
     cap = -(-max(2, 3 * count // (2 * n_dev)) // 8) * 8
     total = n_dev * cap
     parts = 4
@@ -269,7 +277,7 @@
     user = in_hbm(cand_user.reshape(1, count))
 
     outgoing = pl.pallas_call(
-        functools.partial(dispatch_kernel, cap),
+        functools.partial(dispatch_kernel, n_grp, n_enc, cap),
         in_specs=[anywhere] * 5,
         out_specs=anywhere,
         out_shape=pltpu.HBM((n_dev, heads * cap + 8, HDIM), BF16),
@@ -325,7 +333,7 @@
 
     step = count // 2
     gate, own, pick = pl.pallas_call(
-        functools.partial(own_kernel, cap),
+        functools.partial(own_kernel, n_grp, n_enc, cap),
         grid=(count // step,),
         in_specs=[
             pl.BlockSpec((step, dim), lambda i: (i, 0)),

time: 63.3 us -> 63.2 us (level)
  waiting for transfers between devices: 5.49 us -> 6.37 us
    all_to_all x1, waiting for transfers between devices: 5.49 us -> 6.37 us  [exchange(): lax.all_to_all(slots, ('enc', 'grp'), split_axis=0, concat_axis=0, tiled=...]
where the time goes in v10:
time: 63.2 us; the launch traced here: 62.9 us
  Pallas kernels  25 us (40%)
  blocking collectives  23.8 us (38%)
  starting transfers between devices  7.1 us (11%)
  waiting for transfers between devices  6.37 us (10%)
  between operations  0.66 us (1%)
    all_to_all x1, blocking collectives, exchange(): lax.all_to_all(slots, ('enc', 'grp'), split_axis=0, concat_axis=0, tiled=...  23.8 us
    pallas_call x1, Pallas kernels, body(): pl.pallas_call(encode_kernel, grid=(users // span,), in_specs=[pl.BlockSp...  9.26 us
    all_to_all x1, starting transfers between devices, exchange(): lax.all_to_all(slots, ('enc', 'grp'), split_axis=0, concat_axis=0, tiled=...  7.1 us
    pallas_call x1, Pallas kernels, body(): pl.pallas_call(functools.partial(own_kernel, n_grp, n_enc, cap), grid=(co...  6.57 us
    all_to_all x1, waiting for transfers between devices, exchange(): lax.all_to_all(slots, ('enc', 'grp'), split_axis=0, concat_axis=0, tiled=...  6.37 us
    pallas_call x1, Pallas kernels, body(): pl.pallas_call(functools.partial(dispatch_kernel, n_grp, n_enc, cap), in_...  3.91 us
    pallas_call x1, Pallas kernels, body(): pl.pallas_call(functools.partial(attend_kernel, cap), in_specs=[pl.BlockS...  3.64 us
    pallas_call x1, Pallas kernels, body(): pl.pallas_call(answer_kernel, in_specs=[pl.BlockSpec(memory_space=pltpu.V...  1.6 us
  transfers between devices with their start and end apart: 1, of which 1 were waited for; matrix products, arithmetic and copies ran while one was open for 0% of the time, Pallas kernels for 25%

profile of v10, /device:TPU:1, one launch (start us, length us, event | category | flops | bytes accessed | tf_op | source)
XLA Modules:
  0.0 62.9 jit_solution(1619950753987174997)
XLA Ops:
  0.6 3.9 %dispatch.1 = bf16[32,104,128]{2,1,0:T(8,128)(2,1)} custom-call(bf16[512,1024]{1,0:T(8,128)(2,1)} %cand_ref.1, f32[1,1024]{1,0:T(1,128)} %bitcast.7, bf16[1024,2048]{1,0:T(8,128)(2,1)} %w_ref.1, s32[1,512]{1,0:T(1,128)} %bitcast.11, s32[1,512]{1,0:T(1,128)} %bitcast.10), custom_call_target="tpu_custom_call" | custom-call | flops 939524096 | bytes 4194304 | tf_op jit(solution)/shard_map/dispatch/pallas_call | solution.py:279
  4.5 7.1 %all-to-all-start = ((bf16[32,104,128]{2,1,0:T(8,128)(2,1)}), bf16[32,104,128]{2,1,0:T(8,128)(2,1)S(1)}, u32[]{:S(2)}, u32[]{:S(2)}) async-start(bf16[32,104,128]{2,1,0:T(8,128)(2,1)} %dispatch.1), calls=%async_computation | async-start | bytes 1703936 | tf_op jit(solution)/shard_map/all_to_all | solution.py:257
  11.7 6.6 %own.1 = (bf16[512,512]{1,0:T(8,128)(2,1)S(1)}, bf16[512,512]{1,0:T(8,128)(2,1)S(1)}, bf16[512,768]{1,0:T(8,128)(2,1)S(1)}) custom-call(bf16[512,1024]{1,0:T(8,128)(2,1)} %cand_ref.1, f32[1,1024]{1,0:T(1,128)} %bitcast.8, bf16[1024,2048]{1,0:T(8,128)(2,1)} %w_ref.1, s32[1,512]{1,0:T(1,128)} %bitcast.12), custom_call_target="tpu_custom_call" | custom-call | flops 2147483648 | bytes 6291456 | tf_op jit(solution)/shard_map/own/pallas_call | solution.py:335
  18.2 9.3 %encode.1 = (bf16[12,128,1024]{2,1,0:T(8,128)(2,1)}, bf16[2,768,256]{2,1,0:T(8,128)(2,1)S(1)}, bf16[2,768,256]{2,1,0:T(8,128)(2,1)}, bf16[4,768,256]{2,1,0:T(8,128)(2,1)}) custom-call(s32[12]{0:T(128)} %len_ref.1, bf16[12,128,1024]{2,1,0:T(8,128)(2,1)} %hist_ref.1, f32[1,1024]{1,0:T(1,128)} %bitcast.9, bf16[1024,2048]{1,0:T(8,128)(2,1)} %w_ref.1, ...), custom_call_target="tpu_custom_call" | custom-call | flops 3221225472 | bytes 12582912 | tf_op jit(solution)/shard_map/encode/pallas_call | solution.py:307
  27.5 6.4 %all-to-all-done.arrived_ref = bf16[32,104,128]{2,1,0:T(8,128)(2,1)S(1)} async-done(((bf16[32,104,128]{2,1,0:T(8,128)(2,1)}), bf16[32,104,128]{2,1,0:T(8,128)(2,1)S(1)}, u32[]{:S(2)}, u32[]{:S(2)}) %all-to-all-start) | async-done | bytes 852000 | tf_op jit(solution)/shard_map/all_to_all | solution.py:257
  33.9 3.6 %attend.1 = bf16[768,512]{1,0:T(8,128)(2,1)S(1)} custom-call(bf16[32,104,128]{2,1,0:T(8,128)(2,1)S(1)} %all-to-all-done.arrived_ref, bf16[2,768,256]{2,1,0:T(8,128)(2,1)S(1)} %get-tuple-element.10.near_ref, bf16[2,768,256]{2,1,0:T(8,128)(2,1)} %get-tuple-element.11.far_hbm, bf16[4,768,256]{2,1,0:T(8,128)(2,1)} %get-tuple-element.12.v_hbm, ...), custom_call_target="tpu_custom_call" | custom-call | flops 2415919104 | bytes 6291456 | tf_op jit(solution)/shard_map/attend/pallas_call | solution.py:356
  37.5 23.8 %all_to_all.10 = bf16[32,24,512]{2,1,0:T(8,128)(2,1)S(1)} all-to-all(bf16[32,24,512]{2,1,0:T(8,128)(2,1)S(1)} %bitcast.6), channel_id=1, replica_groups=mesh['grp'=4,'enc'=8] {'enc','grp'}, dimensions={0} | all-to-all | bytes 1572864 | tf_op jit(solution)/shard_map/all_to_all | solution.py:257
  61.3 1.6 %answer.1 = bf16[512,512]{1,0:T(8,128)(2,1)} custom-call(bf16[768,512]{1,0:T(8,128)(2,1)S(1)} %bitcast.5, bf16[512,512]{1,0:T(8,128)(2,1)S(1)} %get-tuple-element.14.u_ref, bf16[512,512]{1,0:T(8,128)(2,1)S(1)} %get-tuple-element.13._.self_ref, bf16[512,768]{1,0:T(8,128)(2,1)S(1)} %get-tuple-element.15.pick_ref), custom_call_target="tpu_custom_call" | custom-call | flops 402653184 | bytes 4194304 | tf_op jit(solution)/shard_map/answer/pallas_call | solution.py:376
Async XLA Ops:
  4.5 29.3 %all-to-all-start = ((bf16[32,104,128]{2,1,0:T(8,128)(2,1)}), bf16[32,104,128]{2,1,0:T(8,128)(2,1)S(1)}, u32[]{:S(2)}, u32[]{:S(2)}) async-start(bf16[32,104,128]{2,1,0:T(8,128)(2,1)} %dispatch.1), calls=%async_computation | async-start | bytes 1703936 | tf_op jit(solution)/shard_map/all_to_all | solution.py:257

commit v11 on v10

--- a/solution.py
+++ b/solution.py
@@ -91,7 +91,7 @@
     pick_ref[...] = one_hot(iota((n_dev * cap, count), 0) == place * cap + rank)
     users = jnp.where(named, user_ref[...].astype(F32), 0.0).astype(BF16)
     table = lax.dot_general(users, one_hot(iota((128, count), 0) == rank), NT, preferred_element_type=F32)
-    out_ref[:, heads * cap :, :] = jnp.broadcast_to(table[:, None, :], (n_dev, 8, 128)).astype(BF16)
+    out_ref[:, heads * cap // 8, :, :] = jnp.broadcast_to(table[:, None, :], (n_dev, 8, 128)).astype(BF16)
     for copy in loads:
         copy.wait()
     weights.wait()
@@ -109,8 +109,8 @@
         devs = slice(g * span, (g + 1) * span)
         sent = mm(pick_ref[g * span * cap : (g + 1) * span * cap, :], q_ref[...])
         for h in range(heads):
-            part = sent[:, h * HDIM : (h + 1) * HDIM].reshape(span, cap, HDIM)
-            out_ref[devs, h * cap : (h + 1) * cap, :] = part.astype(BF16)
+            part = sent[:, h * HDIM : (h + 1) * HDIM].reshape(span, cap // 8, 8, HDIM)
+            out_ref[devs, h * cap // 8 : (h + 1) * cap // 8, :, :] = part.astype(BF16)
         at = pl.ds(g * span, span)
         stores.append(pltpu.make_async_copy(out_ref.at[at], out_hbm.at[at], out_sem.at[g]))
         stores[-1].start()
@@ -192,7 +192,7 @@
         load(g).start()
 
     full = (n_dev, cap, 128)
-    table = arrived_ref[:, heads * cap : heads * cap + 8, :].astype(F32)[:, 0:1, :]
+    table = arrived_ref[:, heads * cap // 8, :, :].astype(F32)[:, 0:1, :]
     own = jnp.where(iota(full, 1) == iota(full, 2), jnp.broadcast_to(table, full), 0.0)
     uid = mm(own.reshape(total, 128).astype(BF16), jnp.ones((128, 128), BF16))
     pair = jnp.floor(uid * 0.5)
@@ -210,16 +210,16 @@
 
     for g in range(groups):
         members = [g * each + t for t in range(each)]
+        if g == groups // 2:
+            far.wait()
         scores = []
         for h in members:
-            query = arrived_ref[:, h * cap : (h + 1) * cap, :].astype(F32).reshape(total, HDIM).astype(BF16)
+            query = arrived_ref[:, h * cap // 8 : (h + 1) * cap // 8, :, :].astype(F32)
+            query = query.reshape(total, HDIM).astype(BF16)
             key = near_ref[h] if h < near_ref.shape[0] else far_ref[h - near_ref.shape[0]]
             scores.append(mm(spread(query), key))
         weights = [silu(chosen(score) * HDIM ** (-0.5)).astype(BF16) for score in scores]
-        if g == 0:
-            load(0).wait()
-            far.wait()
-            load(1).wait()
+        load(g).wait()
         for h, weight in zip(members, weights):
             out_ref[:, h * HDIM : (h + 1) * HDIM] = chosen(mm(spread(weight), v_ref[h])).astype(BF16)
 
@@ -280,14 +280,14 @@
         functools.partial(dispatch_kernel, n_grp, n_enc, cap),
         in_specs=[anywhere] * 5,
         out_specs=anywhere,
-        out_shape=pltpu.HBM((n_dev, heads * cap + 8, HDIM), BF16),
+        out_shape=pltpu.HBM((n_dev, heads * cap // 8 + 1, 8, HDIM), BF16),
         scratch_shapes=[
             pltpu.VMEM((count, dim), BF16),
             pltpu.VMEM((1, dim), F32),
             pltpu.VMEM((dim, width), BF16),
             pltpu.VMEM((1, count), jnp.int32),
             pltpu.VMEM((1, count), jnp.int32),
-            pltpu.VMEM((n_dev, heads * cap + 8, HDIM), BF16),
+            pltpu.VMEM((n_dev, heads * cap // 8 + 1, 8, HDIM), BF16),
             pltpu.VMEM((count, width), BF16),
             pltpu.VMEM((total, count), BF16),
             dma((3,)),

time: 63.2 us -> 63.1 us (level)
  no operation moved by 1% of the time
where the time goes in v11:
time: 63.1 us; the launch traced here: 62.8 us
  Pallas kernels  24.9 us (39%)
  blocking collectives  23.8 us (38%)
  starting transfers between devices  7.1 us (11%)
  waiting for transfers between devices  6.37 us (10%)
  between operations  0.66 us (1%)
    all_to_all x1, blocking collectives, exchange(): lax.all_to_all(slots, ('enc', 'grp'), split_axis=0, concat_axis=0, tiled=...  23.8 us
    pallas_call x1, Pallas kernels, body(): pl.pallas_call(encode_kernel, grid=(users // span,), in_specs=[pl.BlockSp...  9.26 us
    all_to_all x1, starting transfers between devices, exchange(): lax.all_to_all(slots, ('enc', 'grp'), split_axis=0, concat_axis=0, tiled=...  7.1 us
    pallas_call x1, Pallas kernels, body(): pl.pallas_call(functools.partial(own_kernel, n_grp, n_enc, cap), grid=(co...  6.57 us
    all_to_all x1, waiting for transfers between devices, exchange(): lax.all_to_all(slots, ('enc', 'grp'), split_axis=0, concat_axis=0, tiled=...  6.37 us
    pallas_call x1, Pallas kernels, body(): pl.pallas_call(functools.partial(dispatch_kernel, n_grp, n_enc, cap), in_...  3.91 us
    pallas_call x1, Pallas kernels, body(): pl.pallas_call(functools.partial(attend_kernel, cap), in_specs=[pl.BlockS...  3.51 us
    pallas_call x1, Pallas kernels, body(): pl.pallas_call(answer_kernel, in_specs=[pl.BlockSpec(memory_space=pltpu.V...  1.6 us
  transfers between devices with their start and end apart: 1, of which 1 were waited for; matrix products, arithmetic and copies ran while one was open for 0% of the time, Pallas kernels for 25%

profile of v11, /device:TPU:1, one launch (start us, length us, event | category | flops | bytes accessed | tf_op | source)
XLA Modules:
  0.0 62.8 jit_solution(10701024464490628876)
XLA Ops:
  0.6 3.9 %dispatch.1 = bf16[32,13,8,128]{3,2,1,0:T(8,128)(2,1)} custom-call(bf16[512,1024]{1,0:T(8,128)(2,1)} %cand_ref.1, f32[1,1024]{1,0:T(1,128)} %bitcast.7, bf16[1024,2048]{1,0:T(8,128)(2,1)} %w_ref.1, s32[1,512]{1,0:T(1,128)} %bitcast.11, s32[1,512]{1,0:T(1,128)} %bitcast.10), custom_call_target="tpu_custom_call" | custom-call | flops 939524096 | bytes 4194304 | tf_op jit(solution)/shard_map/dispatch/pallas_call | solution.py:279
  4.5 7.1 %all-to-all-start = ((bf16[32,13,8,128]{3,2,1,0:T(8,128)(2,1)}), bf16[32,13,8,128]{3,2,1,0:T(8,128)(2,1)S(1)}, u32[]{:S(2)}, u32[]{:S(2)}) async-start(bf16[32,13,8,128]{3,2,1,0:T(8,128)(2,1)} %dispatch.1), calls=%async_computation | async-start | bytes 1703936 | tf_op jit(solution)/shard_map/all_to_all | solution.py:257
  11.7 6.6 %own.1 = (bf16[512,512]{1,0:T(8,128)(2,1)S(1)}, bf16[512,512]{1,0:T(8,128)(2,1)S(1)}, bf16[512,768]{1,0:T(8,128)(2,1)S(1)}) custom-call(bf16[512,1024]{1,0:T(8,128)(2,1)} %cand_ref.1, f32[1,1024]{1,0:T(1,128)} %bitcast.8, bf16[1024,2048]{1,0:T(8,128)(2,1)} %w_ref.1, s32[1,512]{1,0:T(1,128)} %bitcast.12), custom_call_target="tpu_custom_call" | custom-call | flops 2147483648 | bytes 6291456 | tf_op jit(solution)/shard_map/own/pallas_call | solution.py:335
  18.2 9.3 %encode.1 = (bf16[12,128,1024]{2,1,0:T(8,128)(2,1)}, bf16[2,768,256]{2,1,0:T(8,128)(2,1)S(1)}, bf16[2,768,256]{2,1,0:T(8,128)(2,1)}, bf16[4,768,256]{2,1,0:T(8,128)(2,1)}) custom-call(s32[12]{0:T(128)} %len_ref.1, bf16[12,128,1024]{2,1,0:T(8,128)(2,1)} %hist_ref.1, f32[1,1024]{1,0:T(1,128)} %bitcast.9, bf16[1024,2048]{1,0:T(8,128)(2,1)} %w_ref.1, ...), custom_call_target="tpu_custom_call" | custom-call | flops 3221225472 | bytes 12582912 | tf_op jit(solution)/shard_map/encode/pallas_call | solution.py:307
  27.5 6.4 %all-to-all-done.arrived_ref = bf16[32,13,8,128]{3,2,1,0:T(8,128)(2,1)S(1)} async-done(((bf16[32,13,8,128]{3,2,1,0:T(8,128)(2,1)}), bf16[32,13,8,128]{3,2,1,0:T(8,128)(2,1)S(1)}, u32[]{:S(2)}, u32[]{:S(2)}) %all-to-all-start) | async-done | bytes 852000 | tf_op jit(solution)/shard_map/all_to_all | solution.py:257
  33.9 3.5 %attend.1 = bf16[768,512]{1,0:T(8,128)(2,1)S(1)} custom-call(bf16[32,13,8,128]{3,2,1,0:T(8,128)(2,1)S(1)} %all-to-all-done.arrived_ref, bf16[2,768,256]{2,1,0:T(8,128)(2,1)S(1)} %get-tuple-element.10.near_ref, bf16[2,768,256]{2,1,0:T(8,128)(2,1)} %get-tuple-element.11.far_hbm, bf16[4,768,256]{2,1,0:T(8,128)(2,1)} %get-tuple-element.12.v_hbm, ...), custom_call_target="tpu_custom_call" | custom-call | flops 2415919104 | bytes 6291456 | tf_op jit(solution)/shard_map/attend/pallas_call | solution.py:356
  37.4 23.8 %all_to_all.10 = bf16[32,24,512]{2,1,0:T(8,128)(2,1)S(1)} all-to-all(bf16[32,24,512]{2,1,0:T(8,128)(2,1)S(1)} %bitcast.6), channel_id=1, replica_groups=mesh['grp'=4,'enc'=8] {'enc','grp'}, dimensions={0} | all-to-all | bytes 1572864 | tf_op jit(solution)/shard_map/all_to_all | solution.py:257
  61.2 1.6 %answer.1 = bf16[512,512]{1,0:T(8,128)(2,1)} custom-call(bf16[768,512]{1,0:T(8,128)(2,1)S(1)} %bitcast.5, bf16[512,512]{1,0:T(8,128)(2,1)S(1)} %get-tuple-element.14.u_ref, bf16[512,512]{1,0:T(8,128)(2,1)S(1)} %get-tuple-element.13._.self_ref, bf16[512,768]{1,0:T(8,128)(2,1)S(1)} %get-tuple-element.15.pick_ref), custom_call_target="tpu_custom_call" | custom-call | flops 402653184 | bytes 4194304 | tf_op jit(solution)/shard_map/answer/pallas_call | solution.py:376
Async XLA Ops:
  4.5 29.3 %all-to-all-start = ((bf16[32,13,8,128]{3,2,1,0:T(8,128)(2,1)}), bf16[32,13,8,128]{3,2,1,0:T(8,128)(2,1)S(1)}, u32[]{:S(2)}, u32[]{:S(2)}) async-start(bf16[32,13,8,128]{3,2,1,0:T(8,128)(2,1)} %dispatch.1), calls=%async_computation | async-start | bytes 1703936 | tf_op jit(solution)/shard_map/all_to_all | solution.py:257

commit v12 on v11

--- a/solution.py
+++ b/solution.py
@@ -186,9 +186,8 @@
         return pltpu.make_async_copy(v_hbm.at[at], v_ref.at[at], v_sem.at[g])
 
     far = pltpu.make_async_copy(far_hbm, far_ref, far_sem.at[0])
-    load(0).start()
     far.start()
-    for g in range(1, groups):
+    for g in range(groups):
         load(g).start()
 
     full = (n_dev, cap, 128)
@@ -208,20 +207,18 @@
     def chosen(x):
         return jnp.where(odd_ref[...] > 0.5, x[:, 128:], x[:, :128])
 
+    weights = []
+    for h in range(heads):
+        if h == near_ref.shape[0]:
+            far.wait()
+        query = arrived_ref[:, h * cap // 8 : (h + 1) * cap // 8, :, :].astype(F32)
+        query = query.reshape(total, HDIM).astype(BF16)
+        key = near_ref[h] if h < near_ref.shape[0] else far_ref[h - near_ref.shape[0]]
+        weights.append(silu(chosen(mm(spread(query), key)) * HDIM ** (-0.5)).astype(BF16))
     for g in range(groups):
-        members = [g * each + t for t in range(each)]
-        if g == groups // 2:
-            far.wait()
-        scores = []
-        for h in members:
-            query = arrived_ref[:, h * cap // 8 : (h + 1) * cap // 8, :, :].astype(F32)
-            query = query.reshape(total, HDIM).astype(BF16)
-            key = near_ref[h] if h < near_ref.shape[0] else far_ref[h - near_ref.shape[0]]
-            scores.append(mm(spread(query), key))
-        weights = [silu(chosen(score) * HDIM ** (-0.5)).astype(BF16) for score in scores]
         load(g).wait()
-        for h, weight in zip(members, weights):
-            out_ref[:, h * HDIM : (h + 1) * HDIM] = chosen(mm(spread(weight), v_ref[h])).astype(BF16)
+    for h, weight in enumerate(weights):
+        out_ref[:, h * HDIM : (h + 1) * HDIM] = chosen(mm(spread(weight), v_ref[h])).astype(BF16)
 
 
 def answer_kernel(back_ref, u_ref, self_ref, pick_ref, out_ref):

time: 63.1 us -> 63.1 us (level)
  no operation moved by 1% of the time
where the time goes in v12:
time: 63.1 us; the launch traced here: 62.8 us
  Pallas kernels  24.9 us (39%)
  blocking collectives  23.8 us (38%)
  starting transfers between devices  7.1 us (11%)
  waiting for transfers between devices  6.37 us (10%)
  between operations  0.66 us (1%)
    all_to_all x1, blocking collectives, exchange(): lax.all_to_all(slots, ('enc', 'grp'), split_axis=0, concat_axis=0, tiled=...  23.8 us
    pallas_call x1, Pallas kernels, body(): pl.pallas_call(encode_kernel, grid=(users // span,), in_specs=[pl.BlockSp...  9.26 us
    all_to_all x1, starting transfers between devices, exchange(): lax.all_to_all(slots, ('enc', 'grp'), split_axis=0, concat_axis=0, tiled=...  7.1 us
    pallas_call x1, Pallas kernels, body(): pl.pallas_call(functools.partial(own_kernel, n_grp, n_enc, cap), grid=(co...  6.57 us
    all_to_all x1, waiting for transfers between devices, exchange(): lax.all_to_all(slots, ('enc', 'grp'), split_axis=0, concat_axis=0, tiled=...  6.37 us
    pallas_call x1, Pallas kernels, body(): pl.pallas_call(functools.partial(dispatch_kernel, n_grp, n_enc, cap), in_...  3.91 us
    pallas_call x1, Pallas kernels, body(): pl.pallas_call(functools.partial(attend_kernel, cap), in_specs=[pl.BlockS...  3.58 us
    pallas_call x1, Pallas kernels, body(): pl.pallas_call(answer_kernel, in_specs=[pl.BlockSpec(memory_space=pltpu.V...  1.6 us
  transfers between devices with their start and end apart: 1, of which 1 were waited for; matrix products, arithmetic and copies ran while one was open for 0% of the time, Pallas kernels for 25%

profile of v12, /device:TPU:1, one launch (start us, length us, event | category | flops | bytes accessed | tf_op | source)
XLA Modules:
  0.0 62.8 jit_solution(3083206021355017514)
XLA Ops:
  0.6 3.9 %dispatch.1 = bf16[32,13,8,128]{3,2,1,0:T(8,128)(2,1)} custom-call(bf16[512,1024]{1,0:T(8,128)(2,1)} %cand_ref.1, f32[1,1024]{1,0:T(1,128)} %bitcast.7, bf16[1024,2048]{1,0:T(8,128)(2,1)} %w_ref.1, s32[1,512]{1,0:T(1,128)} %bitcast.11, s32[1,512]{1,0:T(1,128)} %bitcast.10), custom_call_target="tpu_custom_call" | custom-call | flops 939524096 | bytes 4194304 | tf_op jit(solution)/shard_map/dispatch/pallas_call | solution.py:276
  4.5 7.1 %all-to-all-start = ((bf16[32,13,8,128]{3,2,1,0:T(8,128)(2,1)}), bf16[32,13,8,128]{3,2,1,0:T(8,128)(2,1)S(1)}, u32[]{:S(2)}, u32[]{:S(2)}) async-start(bf16[32,13,8,128]{3,2,1,0:T(8,128)(2,1)} %dispatch.1), calls=%async_computation | async-start | bytes 1703936 | tf_op jit(solution)/shard_map/all_to_all | solution.py:254
  11.7 6.6 %own.1 = (bf16[512,512]{1,0:T(8,128)(2,1)S(1)}, bf16[512,512]{1,0:T(8,128)(2,1)S(1)}, bf16[512,768]{1,0:T(8,128)(2,1)S(1)}) custom-call(bf16[512,1024]{1,0:T(8,128)(2,1)} %cand_ref.1, f32[1,1024]{1,0:T(1,128)} %bitcast.8, bf16[1024,2048]{1,0:T(8,128)(2,1)} %w_ref.1, s32[1,512]{1,0:T(1,128)} %bitcast.12), custom_call_target="tpu_custom_call" | custom-call | flops 2147483648 | bytes 6291456 | tf_op jit(solution)/shard_map/own/pallas_call | solution.py:332
  18.2 9.3 %encode.1 = (bf16[12,128,1024]{2,1,0:T(8,128)(2,1)}, bf16[2,768,256]{2,1,0:T(8,128)(2,1)S(1)}, bf16[2,768,256]{2,1,0:T(8,128)(2,1)}, bf16[4,768,256]{2,1,0:T(8,128)(2,1)}) custom-call(s32[12]{0:T(128)} %len_ref.1, bf16[12,128,1024]{2,1,0:T(8,128)(2,1)} %hist_ref.1, f32[1,1024]{1,0:T(1,128)} %bitcast.9, bf16[1024,2048]{1,0:T(8,128)(2,1)} %w_ref.1, ...), custom_call_target="tpu_custom_call" | custom-call | flops 3221225472 | bytes 12582912 | tf_op jit(solution)/shard_map/encode/pallas_call | solution.py:304
  27.5 6.4 %all-to-all-done.arrived_ref = bf16[32,13,8,128]{3,2,1,0:T(8,128)(2,1)S(1)} async-done(((bf16[32,13,8,128]{3,2,1,0:T(8,128)(2,1)}), bf16[32,13,8,128]{3,2,1,0:T(8,128)(2,1)S(1)}, u32[]{:S(2)}, u32[]{:S(2)}) %all-to-all-start) | async-done | bytes 852000 | tf_op jit(solution)/shard_map/all_to_all | solution.py:254
  33.9 3.6 %attend.1 = bf16[768,512]{1,0:T(8,128)(2,1)S(1)} custom-call(bf16[32,13,8,128]{3,2,1,0:T(8,128)(2,1)S(1)} %all-to-all-done.arrived_ref, bf16[2,768,256]{2,1,0:T(8,128)(2,1)S(1)} %get-tuple-element.10.near_ref, bf16[2,768,256]{2,1,0:T(8,128)(2,1)} %get-tuple-element.11.far_hbm, bf16[4,768,256]{2,1,0:T(8,128)(2,1)} %get-tuple-element.12.v_hbm, ...), custom_call_target="tpu_custom_call" | custom-call | flops 2415919104 | bytes 6291456 | tf_op jit(solution)/shard_map/attend/pallas_call | solution.py:353
  37.5 23.8 %all_to_all.10 = bf16[32,24,512]{2,1,0:T(8,128)(2,1)S(1)} all-to-all(bf16[32,24,512]{2,1,0:T(8,128)(2,1)S(1)} %bitcast.6), channel_id=1, replica_groups=mesh['grp'=4,'enc'=8] {'enc','grp'}, dimensions={0} | all-to-all | bytes 1572864 | tf_op jit(solution)/shard_map/all_to_all | solution.py:254
  61.2 1.6 %answer.1 = bf16[512,512]{1,0:T(8,128)(2,1)} custom-call(bf16[768,512]{1,0:T(8,128)(2,1)S(1)} %bitcast.5, bf16[512,512]{1,0:T(8,128)(2,1)S(1)} %get-tuple-element.14.u_ref, bf16[512,512]{1,0:T(8,128)(2,1)S(1)} %get-tuple-element.13._.self_ref, bf16[512,768]{1,0:T(8,128)(2,1)S(1)} %get-tuple-element.15.pick_ref), custom_call_target="tpu_custom_call" | custom-call | flops 402653184 | bytes 4194304 | tf_op jit(solution)/shard_map/answer/pallas_call | solution.py:373
Async XLA Ops:
  4.5 29.3 %all-to-all-start = ((bf16[32,13,8,128]{3,2,1,0:T(8,128)(2,1)}), bf16[32,13,8,128]{3,2,1,0:T(8,128)(2,1)S(1)}, u32[]{:S(2)}, u32[]{:S(2)}) async-start(bf16[32,13,8,128]{3,2,1,0:T(8,128)(2,1)} %dispatch.1), calls=%async_computation | async-start | bytes 1703936 | tf_op jit(solution)/shard_map/all_to_all | solution.py:254
